TPU v7x, 256 devices: a whole 4x4x8 slice. The times are simulated.
256 devices in a mesh: docs: 32 (over x, y, core), heads: 8 (over z).
Axes of the slice: x: 4, y: 4, z: 8, core: 2. Of those that a mesh axis runs over, the one named last changes fastest.
Arguments:
- queries: bfloat16 [96, 128, 8192], P('docs', 'heads'), may hold values from -12 to 12
- keys: bfloat16 [96, 128, 1024], P('docs', 'heads'), may hold values from -6 to 6
- values: bfloat16 [96, 128, 1024], P('docs', 'heads'), may hold values from -6 to 6
- out_grad: bfloat16 [96, 128, 8192], P('docs', 'heads'), may hold values from -6 to 6
- doc_keys: bfloat16 [256, 256, 1024], P('docs', None, 'heads'), may hold values from -6 to 6
- doc_values: bfloat16 [256, 256, 1024], P('docs', None, 'heads'), may hold values from -6 to 6
- owner_pick: int32 [96, 8], P('docs'), may hold values from 0 to 31, all different within a row; in each aligned block of 3 rows (0 to 2, 3 to 5, ...) at most 2 rows name the same one
- doc_pick: int32 [96, 8], P('docs'), may hold values from 0 to 7
Outputs:
- attended: bfloat16 [96, 128, 8192], P('docs', 'heads')
- query_grad: bfloat16 [96, 128, 8192], P('docs', 'heads')
- key_grad: bfloat16 [96, 128, 1024], P('docs', 'heads')
- value_grad: bfloat16 [96, 128, 1024], P('docs', 'heads')
- doc_key_grad: bfloat16 [256, 256, 1024], P('docs', None, 'heads')
- doc_value_grad: bfloat16 [256, 256, 1024], P('docs', None, 'heads')
Inputs may be any that keep to these rules, and one draw needn't show every extreme that they name: `owner_pick`: each row names 8 different owners. Among the 3 rows of one index of docs no owner is named more than 2 times, a bound that some block reaches.
All inputs are finite; a program needn't handle non-finite values.
Results may differ from a plain program's by a relative error of at most 0.039.
Values may be sent and summed in bfloat16 or wider, within the bound.
No kernel may reach another device: no remote copies, remote signals or barrier semaphores. Data moves between devices by JAX's collectives and lax.ppermute only.
A program may use at most 128 MiB of HBM per device.

v0:
```python
import math

import jax
import jax.numpy as jnp
from jax import lax
from jax.sharding import PartitionSpec as P


def slot_table(owner_ids, pick_ids, capacity, peer_count):
    total = owner_ids.shape[0]
    ordinal = jnp.arange(total)
    earlier = (owner_ids[None, :] == owner_ids[:, None]) & (ordinal[None, :] < ordinal[:, None])
    ranking = jnp.sum(earlier.astype(jnp.int32), axis=1)
    slots = owner_ids * capacity + ranking
    matches = slots[:, None] == jnp.arange(peer_count * capacity)[None, :]
    request_table = jnp.sum(jnp.where(matches, pick_ids[:, None] + 1, 0), axis=0) - 1
    return (slots, request_table)


def attend_block(query, grad_out, key_all, value_all):
    length, features = query.shape
    key_count, head_dim = key_all.shape
    group_size = features // head_dim
    scaling = 1.0 / math.sqrt(head_dim)
    query_heads = query.reshape(length, group_size, head_dim)
    grad_heads = grad_out.reshape(length, group_size, head_dim)
    scores = (
        jnp.einsum("lgd,kd->glk", query_heads, key_all, preferred_element_type=jnp.float32)
        * scaling
    )
    offset = key_count - length
    row_index = jnp.arange(length)[:, None]
    col_index = jnp.arange(key_count)[None, :]
    visible = (col_index < offset) | (col_index - offset <= row_index)
    scores = jnp.where(visible, scores, -jnp.inf)
    row_max = jnp.max(scores, axis=-1, keepdims=True)
    log_total = row_max + jnp.log(jnp.sum(jnp.exp(scores - row_max), axis=-1, keepdims=True))
    weights = jnp.exp(scores - log_total)
    weights_low = weights.astype(jnp.bfloat16)
    attended = jnp.einsum(
        "glk,kd->lgd", weights_low, value_all, preferred_element_type=jnp.float32
    ).astype(jnp.bfloat16)
    row_dot = jnp.sum(grad_heads.astype(jnp.float32) * attended.astype(jnp.float32), axis=-1)
    row_dot = jnp.transpose(row_dot)[..., None]
    value_grad = jnp.einsum(
        "glk,lgd->kd", weights_low, grad_heads, preferred_element_type=jnp.float32
    )
    weight_grad = jnp.einsum(
        "lgd,kd->glk", grad_heads, value_all, preferred_element_type=jnp.float32
    )
    score_grad = (scaling * weights * (weight_grad - row_dot)).astype(jnp.bfloat16)
    query_grad = jnp.einsum(
        "glk,kd->lgd", score_grad, key_all, preferred_element_type=jnp.float32
    ).astype(jnp.bfloat16)
    key_grad = jnp.einsum(
        "glk,lgd->kd", score_grad, query_heads, preferred_element_type=jnp.float32
    )
    return (
        attended.reshape(length, features),
        query_grad.reshape(length, features),
        key_grad,
        value_grad,
    )


def shards(queries, keys, values, out_grad, doc_keys, doc_values, owner_pick, doc_pick):
    query_rows, key_rows, value_rows, grad_rows = (
        lax.all_to_all(queries, "heads", split_axis=2, concat_axis=1, tiled=True),
        lax.all_to_all(keys, "heads", split_axis=2, concat_axis=1, tiled=True),
        lax.all_to_all(values, "heads", split_axis=2, concat_axis=1, tiled=True),
        lax.all_to_all(out_grad, "heads", split_axis=2, concat_axis=1, tiled=True),
    )
    peer_count = lax.axis_size("docs")
    block_count, fan_count = owner_pick.shape
    capacity = min(
        block_count, max(2, (3 * block_count * fan_count + 2 * peer_count - 1) // (2 * peer_count))
    )
    slots, request_table = slot_table(
        owner_pick.reshape(-1), doc_pick.reshape(-1), capacity, peer_count
    )
    requested = lax.all_to_all(
        request_table.reshape(peer_count, capacity), "docs", split_axis=0, concat_axis=0, tiled=True
    )
    flat_requested = requested.reshape(-1)
    doc_length = doc_keys.shape[1]
    head_dim = doc_keys.shape[2]
    stored = jnp.concatenate([doc_keys, doc_values], axis=-1)
    outgoing = jnp.take(stored, jnp.maximum(flat_requested, 0), axis=0)
    outgoing = jnp.where(
        (flat_requested >= 0)[:, None, None], outgoing, jnp.zeros((), jnp.bfloat16)
    )
    arrived = lax.all_to_all(
        outgoing.reshape(peer_count, capacity, doc_length, 2 * head_dim),
        "docs",
        split_axis=0,
        concat_axis=0,
        tiled=True,
    )
    arrived = arrived.reshape(peer_count * capacity, doc_length, 2 * head_dim)
    per_pair = jnp.take(arrived, slots, axis=0).reshape(
        block_count, fan_count * doc_length, 2 * head_dim
    )

    def one_block(inputs):
        query, key_own, value_own, grad_out, fetched = inputs
        key_all = jnp.concatenate([fetched[:, :head_dim], key_own], axis=0)
        value_all = jnp.concatenate([fetched[:, head_dim:], value_own], axis=0)
        attended, query_grad, key_grad, value_grad = attend_block(
            query, grad_out, key_all, value_all
        )
        doc_rows = fetched.shape[0]
        return (
            attended,
            query_grad,
            key_grad[doc_rows:].astype(jnp.bfloat16),
            value_grad[doc_rows:].astype(jnp.bfloat16),
            jnp.concatenate([key_grad[:doc_rows], value_grad[:doc_rows]], axis=-1).astype(
                jnp.bfloat16
            ),
        )

    attended, query_grad, key_grad, value_grad, doc_part = lax.map(
        one_block, (query_rows, key_rows, value_rows, grad_rows, per_pair)
    )
    doc_part = doc_part.reshape(block_count * fan_count, doc_length, 2 * head_dim)
    returning = (
        jnp.zeros((peer_count * capacity, doc_length, 2 * head_dim), jnp.bfloat16)
        .at[slots]
        .set(doc_part)
    )
    received = lax.all_to_all(
        returning.reshape(peer_count, capacity, doc_length, 2 * head_dim),
        "docs",
        split_axis=0,
        concat_axis=0,
        tiled=True,
    )
    local_docs = doc_keys.shape[0]
    selector = (flat_requested[None, :] == jnp.arange(local_docs)[:, None]).astype(jnp.float32)
    summed = jnp.dot(
        selector,
        received.reshape(peer_count * capacity, -1).astype(jnp.float32),
        precision=lax.Precision.HIGHEST,
        preferred_element_type=jnp.float32,
    )
    summed = summed.reshape(local_docs, doc_length, 2 * head_dim)
    doc_key_grad = summed[..., :head_dim].astype(jnp.bfloat16)
    doc_value_grad = summed[..., head_dim:].astype(jnp.bfloat16)
    attended, query_grad, key_grad, value_grad = (
        lax.all_to_all(attended, "heads", split_axis=1, concat_axis=2, tiled=True),
        lax.all_to_all(query_grad, "heads", split_axis=1, concat_axis=2, tiled=True),
        lax.all_to_all(key_grad, "heads", split_axis=1, concat_axis=2, tiled=True),
        lax.all_to_all(value_grad, "heads", split_axis=1, concat_axis=2, tiled=True),
    )
    return (attended, query_grad, key_grad, value_grad, doc_key_grad, doc_value_grad)


def solution(mesh):
    return jax.shard_map(
        shards,
        mesh=mesh,
        in_specs=(
            P("docs", "heads", None),
            P("docs", "heads", None),
            P("docs", "heads", None),
            P("docs", "heads", None),
            P("docs", None, "heads"),
            P("docs", None, "heads"),
            P("docs", None),
            P("docs", None),
        ),
        out_specs=(
            P("docs", "heads", None),
            P("docs", "heads", None),
            P("docs", "heads", None),
            P("docs", "heads", None),
            P("docs", None, "heads"),
            P("docs", None, "heads"),
        ),
        check_vma=False,
    )
```

profile of v0, /device:TPU:8, one launch (start us, length us, event | category | flops | bytes accessed | tf_op | source)
XLA Modules:
  0.0 530.8 jit_solution(6358203416143624944)
XLA Ops:
  3.2 7.5 %all-to-all-start = ((s32[32,1,2]{2,1,0:T(1,128)}), s32[32,1,2]{2,1,0:T(1,128)S(1)}, u32[]{:S(2)}, u32[]{:S(2)}) async-start(s32[32,1,2]{2,1,0:T(1,128)} %bitcast.22), calls=%async_computation | async-start | bytes 32768 | tf_op jit(solution)/shard_map/all_to_all | solution.py:81
  13.8 3.0 all-to-all-done
  16.8 8.5 %all-to-all-start.3 = ((bf16[8,2,3072]{2,1,0:T(2,128)(2,1)}), bf16[8,2,3072]{2,1,0:T(2,128)(2,1)S(1)}, u32[]{:S(2)}, u32[]{:S(2)}) async-start(bf16[8,2,3072]{2,1,0:T(2,128)(2,1)} %reshape.271), calls=%async_computation.3 | async-start | bytes 196608 | tf_op jit(solution)/shard_map/all_to_all | solution.py:69
  28.3 5.7 %all-to-all-done.3 = bf16[8,2,3072]{2,1,0:T(2,128)(2,1)S(1)} async-done(((bf16[8,2,3072]{2,1,0:T(2,128)(2,1)}), bf16[8,2,3072]{2,1,0:T(2,128)(2,1)S(1)}, u32[]{:S(2)}, u32[]{:S(2)}) %all-to-all-start.3) | async-done | bytes 98336 | tf_op jit(solution)/shard_map/all_to_all | solution.py:69
  34.0 3.4 all-to-all-start.2
  37.4 10.0 %copy.219 = bf16[3,16,8192]{1,0,2:T(4,128)(2,1)} copy(bf16[3,16,8192]{2,1,0:T(8,128)(2,1)} %param.10) | data formatting | bytes 1572864 | tf_op args[0]
  47.4 10.3 %reshape.273 = bf16[8,2,24576]{2,1,0:T(2,128)(2,1)} reshape(bf16[8192,3,16]{2,1,0:T(4,128)(2,1)} %bitcast.210) | data formatting | bytes 1572864
  57.6 7.1 %all-to-all-start.4 = ((bf16[8,2,24576]{2,1,0:T(2,128)(2,1)}), bf16[8,2,24576]{2,1,0:T(2,128)(2,1)S(1)}, u32[]{:S(2)}, u32[]{:S(2)}) async-start(bf16[8,2,24576]{2,1,0:T(2,128)(2,1)} %reshape.273), calls=%async_computation.4 | async-start | bytes 1572864 | tf_op jit(solution)/shard_map/all_to_all | solution.py:68
  64.8 8.3 %copy.222 = bf16[3,16,8192]{1,0,2:T(4,128)(2,1)} copy(bf16[3,16,8192]{2,1,0:T(8,128)(2,1)S(1)} %copy-done) | data formatting | bytes 1572864 | tf_op args[3]
  73.0 10.3 %reshape.275 = bf16[8,2,24576]{2,1,0:T(2,128)(2,1)} reshape(bf16[8192,3,16]{2,1,0:T(4,128)(2,1)} %bitcast.211) | data formatting | bytes 1572864
  83.5 2.7 all-to-all-done.4
  86.2 4.5 all-to-all-start.5
  91.1 5.3 %gather_fusion = bf16[64,256,256]{2,1,0:T(8,128)(2,1)} fusion(bf16[8,256,256]{2,1,0:T(8,128)(2,1)S(1)} %pad_maximum_fusion.1, s32[1024]{0:T(1024)S(1)} %pad_clamp_fusion.1), kind=kCustom, calls=%fused_computation | custom fusion | bytes 16777472 | tf_op jit(solution)/shard_map/jit(_take)/gather | solution.py:88
  96.5 7.6 %select_select_fusion = bf16[32,2,256,256]{3,2,1,0:T(8,128)(2,1)} fusion(bf16[32,2,256,256]{3,2,1,0:T(8,128)(2,1)} %bitcast.207, pred[32,2]{1,0:T(8,128)(4,1)S(1)} %copy.213, pred[32,2]{1,0:T(8,128)(4,1)S(1)} %copy.211), kind=kLoop, calls=%fused_computation.46 | loop fusion | flops 8388608 | bytes 16777344 | tf_op jit(solution)/shard_map/jit(_where)/select_n | solution.py:89
  104.1 7.5 %all-to-all-done.5 = bf16[8,2,24576]{2,1,0:T(2,128)(2,1)S(1)} async-done(((bf16[8,2,24576]{2,1,0:T(2,128)(2,1)}), bf16[8,2,24576]{2,1,0:T(2,128)(2,1)S(1)}, u32[]{:S(2)}, u32[]{:S(2)}) %all-to-all-start.5) | async-done | bytes 786464 | tf_op jit(solution)/shard_map/all_to_all | solution.py:71
  111.6 6.0 %all-to-all-start.1 = ((bf16[32,2,256,256]{3,2,1,0:T(8,128)(2,1)}), bf16[32,2,256,256]{3,2,1,0:T(8,128)(2,1)}, u32[]{:S(2)}, u32[]{:S(2)}) async-start(bf16[32,2,256,256]{3,2,1,0:T(8,128)(2,1)} %select_select_fusion), calls=%async_computation.1 | async-start | bytes 16777216 | tf_op jit(solution)/shard_map/all_to_all | solution.py:92
  121.1 8.8 %reshape.274 = bf16[8192,3,16]{2,1,0:T(4,128)(2,1)} reshape(bf16[8,2,24576]{2,1,0:T(2,128)(2,1)S(1)} %all-to-all-done.4) | data formatting | bytes 1572864
  129.9 11.6 %copy.254 = bf16[3,16,8,1024]{3,1,2,0:T(8,128)(2,1)} copy(bf16[3,16,8,1024]{1,0,3,2:T(4,128)(2,1)} %bitcast.208) | data formatting | bytes 1572864 | tf_op jit(solution)/shard_map/all_to_all | solution.py:68
  141.5 8.8 %reshape.276 = bf16[8192,3,16]{2,1,0:T(4,128)(2,1)} reshape(bf16[8,2,24576]{2,1,0:T(2,128)(2,1)S(1)} %all-to-all-done.5) | data formatting | bytes 1572864
  150.3 11.6 %copy.256 = bf16[3,16,8,1024]{3,1,2,0:T(8,128)(2,1)} copy(bf16[3,16,8,1024]{1,0,3,2:T(4,128)(2,1)} %bitcast.209) | data formatting | bytes 1572864 | tf_op jit(solution)/shard_map/all_to_all | solution.py:71
  162.0 79.7 %all-to-all-done.1 = bf16[32,2,256,256]{3,2,1,0:T(8,128)(2,1)} async-done(((bf16[32,2,256,256]{3,2,1,0:T(8,128)(2,1)}), bf16[32,2,256,256]{3,2,1,0:T(8,128)(2,1)}, u32[]{:S(2)}, u32[]{:S(2)}) %all-to-all-start.1) | async-done | bytes 8388640 | tf_op jit(solution)/shard_map/all_to_all | solution.py:92
  241.6 4.1 gather_fusion.1
  245.7 2.6 bitcast_select_fusion.1
  248.4 57.6 %while.20 = (s32[]{:T(128)}, bf16[3,128,1024]{1,2,0:T(8,128)(2,1)}, bf16[3,128,1024]{1,2,0:T(8,128)(2,1)}, bf16[3,128,128]{1,2,0:T(8,128)(2,1)S(1)}, bf16[3,128,...) while((s32[]{:T(128)}, bf16[3,128,1024]{1,2,0:T(8,128)(2,1)}, ...), condition=%wide.region_6.7_spmd, body=%wide.region_2.6_spmd.sunk | while | flops 3462203648 | bytes 79725976 | solution.py:122
  256.2 1.7 multiply_reduce_fusion.2
  257.8 1.7 fusion.59
  259.5 3.0 fusion.58
  275.4 1.7 multiply_reduce_fusion.2
  277.1 1.7 fusion.59
  278.8 3.0 fusion.58
  294.6 1.7 multiply_reduce_fusion.2
  296.3 1.7 fusion.59
  297.9 3.0 fusion.58
  306.7 3.4 all-to-all-start.8
  310.9 8.3 %all-to-all-done.8 = bf16[3,128,128]{2,0,1:T(4,128)(2,1)S(1)} async-done(((bf16[3,128,128]{2,0,1:T(4,128)(2,1)}), bf16[3,128,128]{2,0,1:T(4,128)(2,1)S(1)}, u32[]{:S(2)}, u32[]{:S(2)}) %all-to-all-start.8) | async-done | bytes 98336 | tf_op jit(solution)/shard_map/all_to_all | solution.py:152
  319.2 3.4 all-to-all-start.9
  322.6 2.6 copy.227
  325.2 6.4 %all-to-all-done.9 = bf16[3,128,128]{2,0,1:T(4,128)(2,1)S(1)} async-done(((bf16[3,128,128]{2,0,1:T(4,128)(2,1)}), bf16[3,128,128]{2,0,1:T(4,128)(2,1)S(1)}, u32[]{:S(2)}, u32[]{:S(2)}) %all-to-all-start.9) | async-done | bytes 98336 | tf_op jit(solution)/shard_map/all_to_all | solution.py:153
  331.5 3.6 all-to-all-start.6
  335.1 2.6 copy.230
  337.8 23.7 %all-to-all-done.6 = bf16[3,128,1024]{2,0,1:T(4,128)(2,1)S(1)} async-done(((bf16[3,128,1024]{2,0,1:T(4,128)(2,1)}), bf16[3,128,1024]{2,0,1:T(4,128)(2,1)S(1)}, u32[]{:S(2)}, u32[]{:S(2)}) %all-to-all-start.6) | async-done | bytes 786464 | tf_op jit(solution)/shard_map/all_to_all | solution.py:150
  361.4 3.8 all-to-all-start.7
  365.2 4.3 broadcast_in_dim.119
  369.5 8.7 %scatter_fusion = bf16[64,256,256]{2,1,0:T(8,128)(2,1)} fusion(bf16[64,256,256]{2,1,0:T(8,128)(2,1)} %broadcast_in_dim.119, s32[24]{0:T(128)S(1)} %copy-done.7, bf16[24,256,256]{2,1,0:T(8,128)(2,1)} %bitcast.225), kind=kCustom, calls=%fused_computation.2 | custom fusion | bytes 9437280 | tf_op jit(solution)/shard_map/scatter | solution.py:129
  378.1 12.1 %all-to-all-done.7 = bf16[3,128,1024]{2,0,1:T(4,128)(2,1)S(1)} async-done(((bf16[3,128,1024]{2,0,1:T(4,128)(2,1)}), bf16[3,128,1024]{2,0,1:T(4,128)(2,1)S(1)}, u32[]{:S(2)}, u32[]{:S(2)}) %all-to-all-start.7) | async-done | bytes 786464 | tf_op jit(solution)/shard_map/all_to_all | solution.py:151
  390.3 6.5 %all-to-all-start.10 = ((bf16[32,2,256,256]{3,2,1,0:T(8,128)(2,1)}), bf16[32,2,256,256]{3,2,1,0:T(8,128)(2,1)}, u32[]{:S(2)}, u32[]{:S(2)}) async-start(bf16[32,2,256,256]{3,2,1,0:T(8,128)(2,1)} %bitcast.206), calls=%async_computation.10 | async-start | bytes 16777216 | tf_op jit(solution)/shard_map/all_to_all | solution.py:131
  402.0 119.1 %all-to-all-done.10 = bf16[32,2,256,256]{3,2,1,0:T(8,128)(2,1)} async-done(((bf16[32,2,256,256]{3,2,1,0:T(8,128)(2,1)}), bf16[32,2,256,256]{3,2,1,0:T(8,128)(2,1)}, u32[]{:S(2)}, u32[]{:S(2)}) %all-to-all-start.10) | async-done | bytes 8388640 | tf_op jit(solution)/shard_map/all_to_all | solution.py:131
  521.0 7.9 %fusion.17 = bf16[8,256,256]{2,0,1:T(8,128)(2,1)S(1)} fusion(s32[64]{0:T(128)S(1)} %reshape.224, bf16[8,8,256,256]{3,2,1,0:T(8,128)(2,1)} %bitcast.80), kind=kOutput, calls=%fused_computation.48 | convolution fusion | flops 67633664 | bytes 9437440 | tf_op jit(solution)/shard_map/dot_general | solution.py:140
  (137 shorter events, 59.4 us)
Async XLA Ops:
  3.2 13.6 %all-to-all-start = ((s32[32,1,2]{2,1,0:T(1,128)}), s32[32,1,2]{2,1,0:T(1,128)S(1)}, u32[]{:S(2)}, u32[]{:S(2)}) async-start(s32[32,1,2]{2,1,0:T(1,128)} %bitcast.22), calls=%async_computation | async-start | bytes 32768 | tf_op jit(solution)/shard_map/all_to_all | solution.py:81
  16.8 66.6 %copy-start.3 = (s32[32,1,2]{2,1,0:T(1,128)}, s32[32,1,2]{2,1,0:T(1,128)S(1)}, u32[]{:S(2)}) copy-start(s32[32,1,2]{2,1,0:T(1,128)S(1)} %all-to-all-done) | copy-start | bytes 772
  16.8 17.2 %all-to-all-start.3 = ((bf16[8,2,3072]{2,1,0:T(2,128)(2,1)}), bf16[8,2,3072]{2,1,0:T(2,128)(2,1)S(1)}, u32[]{:S(2)}, u32[]{:S(2)}) async-start(bf16[8,2,3072]{2,1,0:T(2,128)(2,1)} %reshape.271), calls=%async_computation.3 | async-start | bytes 196608 | tf_op jit(solution)/shard_map/all_to_all | solution.py:69
  34.0 23.6 %all-to-all-start.2 = ((bf16[8,2,3072]{2,1,0:T(2,128)(2,1)}), bf16[8,2,3072]{2,1,0:T(2,128)(2,1)S(1)}, u32[]{:S(2)}, u32[]{:S(2)}) async-start(bf16[8,2,3072]{2,1,0:T(2,128)(2,1)} %reshape.269), calls=%async_computation.2 | async-start | bytes 196608 | tf_op jit(solution)/shard_map/all_to_all | solution.py:70
  37.4 27.4 %copy-start = (bf16[3,16,8192]{2,1,0:T(8,128)(2,1)S(1)}, bf16[3,16,8192]{2,1,0:T(8,128)(2,1)}, u32[]{:S(2)}) copy-start(bf16[3,16,8192]{2,1,0:T(8,128)(2,1)} %param.13) | copy-start | bytes 2359300
  57.6 28.6 %all-to-all-start.4 = ((bf16[8,2,24576]{2,1,0:T(2,128)(2,1)}), bf16[8,2,24576]{2,1,0:T(2,128)(2,1)S(1)}, u32[]{:S(2)}, u32[]{:S(2)}) async-start(bf16[8,2,24576]{2,1,0:T(2,128)(2,1)} %reshape.273), calls=%async_computation.4 | async-start | bytes 1572864 | tf_op jit(solution)/shard_map/all_to_all | solution.py:68
  64.7 18.5 %copy-start.1 = (bf16[8,256,128]{2,1,0:T(8,128)(2,1)S(1)}, bf16[8,256,128]{2,1,0:T(8,128)(2,1)}, u32[]{:S(2)}) copy-start(bf16[8,256,128]{2,1,0:T(8,128)(2,1)} %param.15) | copy-start | bytes 1572868
  64.7 18.5 %copy-start.2 = (bf16[8,256,128]{2,1,0:T(8,128)(2,1)S(1)}, bf16[8,256,128]{2,1,0:T(8,128)(2,1)}, u32[]{:S(2)}) copy-start(bf16[8,256,128]{2,1,0:T(8,128)(2,1)} %param.14) | copy-start | bytes 1572868
  86.2 25.4 %all-to-all-start.5 = ((bf16[8,2,24576]{2,1,0:T(2,128)(2,1)}), bf16[8,2,24576]{2,1,0:T(2,128)(2,1)S(1)}, u32[]{:S(2)}, u32[]{:S(2)}) async-start(bf16[8,2,24576]{2,1,0:T(2,128)(2,1)} %reshape.275), calls=%async_computation.5 | async-start | bytes 1572864 | tf_op jit(solution)/shard_map/all_to_all | solution.py:71
  104.1 13.6 %copy-start.5 = (s32[3,8]{1,0:T(4,128)S(1)}, s32[3,8]{1,0:T(4,128)}, u32[]{:S(2)}) copy-start(s32[3,8]{1,0:T(4,128)} %param.16) | copy-start | bytes 292
  111.6 130.0 %all-to-all-start.1 = ((bf16[32,2,256,256]{3,2,1,0:T(8,128)(2,1)}), bf16[32,2,256,256]{3,2,1,0:T(8,128)(2,1)}, u32[]{:S(2)}, u32[]{:S(2)}) async-start(bf16[32,2,256,256]{3,2,1,0:T(8,128)(2,1)} %select_select_fusion), calls=%async_computation.1 | async-start | bytes 16777216 | tf_op jit(solution)/shard_map/all_to_all | solution.py:92
  117.9 23.6 %copy-start.6 = (s32[24]{0:T(128)}, s32[24]{0:T(128)S(1)}, u32[]{:S(2)}) copy-start(s32[24]{0:T(128)S(1)} %fusion.24) | copy-start | bytes 292
  306.7 12.4 %all-to-all-start.8 = ((bf16[3,128,128]{2,0,1:T(4,128)(2,1)}), bf16[3,128,128]{2,0,1:T(4,128)(2,1)S(1)}, u32[]{:S(2)}, u32[]{:S(2)}) async-start(bf16[3,128,128]{2,0,1:T(4,128)(2,1)} %copy.233), calls=%async_computation.8 | async-start | bytes 262144 | tf_op jit(solution)/shard_map/all_to_all | solution.py:152
  310.1 59.4 %copy-start.7 = (s32[24]{0:T(128)S(1)}, s32[24]{0:T(128)}, u32[]{:S(2)}) copy-start(s32[24]{0:T(128)} %copy-done.6) | copy-start | bytes 292
  319.2 12.4 %all-to-all-start.9 = ((bf16[3,128,128]{2,0,1:T(4,128)(2,1)}), bf16[3,128,128]{2,0,1:T(4,128)(2,1)S(1)}, u32[]{:S(2)}, u32[]{:S(2)}) async-start(bf16[3,128,128]{2,0,1:T(4,128)(2,1)} %copy.236), calls=%async_computation.9 | async-start | bytes 262144 | tf_op jit(solution)/shard_map/all_to_all | solution.py:153
  331.5 29.9 %all-to-all-start.6 = ((bf16[3,128,1024]{2,0,1:T(4,128)(2,1)}), bf16[3,128,1024]{2,0,1:T(4,128)(2,1)S(1)}, u32[]{:S(2)}, u32[]{:S(2)}) async-start(bf16[3,128,1024]{2,0,1:T(4,128)(2,1)} %copy.227), calls=%async_computation.6 | async-start | bytes 2097152 | tf_op jit(solution)/shard_map/all_to_all | solution.py:150
  361.4 28.8 %all-to-all-start.7 = ((bf16[3,128,1024]{2,0,1:T(4,128)(2,1)}), bf16[3,128,1024]{2,0,1:T(4,128)(2,1)S(1)}, u32[]{:S(2)}, u32[]{:S(2)}) async-start(bf16[3,128,1024]{2,0,1:T(4,128)(2,1)} %copy.230), calls=%async_computation.7 | async-start | bytes 2097152 | tf_op jit(solution)/shard_map/all_to_all | solution.py:151
  390.3 7.0 %copy-start.4 = (s32[32,1,2]{2,1,0:T(1,128)S(1)}, s32[32,1,2]{2,1,0:T(1,128)}, u32[]{:S(2)}) copy-start(s32[32,1,2]{2,1,0:T(1,128)} %copy-done.3) | copy-start | bytes 772
  390.3 130.8 %all-to-all-start.10 = ((bf16[32,2,256,256]{3,2,1,0:T(8,128)(2,1)}), bf16[32,2,256,256]{3,2,1,0:T(8,128)(2,1)}, u32[]{:S(2)}, u32[]{:S(2)}) async-start(bf16[32,2,256,256]{3,2,1,0:T(8,128)(2,1)} %bitcast.206), calls=%async_computation.10 | async-start | bytes 16777216 | tf_op jit(solution)/shard_map/all_to_all | solution.py:131
where the time goes:
time: 534 us; the launch traced here: 531 us
  waiting for transfers between devices  268 us (50%)
  local copies, waits for them, and re-layouts  145 us (27%)
  starting transfers between devices  57.5 us (11%)
  matrix products  37.9 us (7%)
  other arithmetic  20.5 us (4%)
    all_to_all x1, waiting for transfers between devices, shards(): lax.all_to_all(returning.reshape(peer_count, capacity, doc_length, 2 * he...  119 us
    all_to_all x1, waiting for transfers between devices, shards(): lax.all_to_all(outgoing.reshape(peer_count, capacity, doc_length, 2 * hea...  79.7 us
    unnamed x32, local copies, waits for them, and re-layouts  66.4 us
    all_to_all x1, waiting for transfers between devices, shards(): lax.all_to_all(attended, 'heads', split_axis=1, concat_axis=2, tiled=True)  23.7 us
    all_to_all x1, waiting for transfers between devices, shards(): lax.all_to_all(query_grad, 'heads', split_axis=1, concat_axis=2, tiled=True)  12.1 us
    all_to_all x1, local copies, waits for them, and re-layouts, shards(): lax.all_to_all(out_grad, 'heads', split_axis=2, concat_axis=1, tiled=True)  11.6 us
    all_to_all x1, local copies, waits for them, and re-layouts, shards(): lax.all_to_all(queries, 'heads', split_axis=2, concat_axis=1, tiled=True)  11.6 us
  transfers between devices with their start and end apart: 11, of which 10 were waited for; matrix products, arithmetic and copies ran while one was open for 24% of the time, Pallas kernels for 0%

commit v1 on v0

v1 whole, which is shorter than its diff:
```python
import functools
import math

import jax
import jax.numpy as jnp
from jax import lax
from jax.experimental import pallas as pl
from jax.experimental.pallas import tpu as pltpu
from jax.sharding import PartitionSpec as P

VMEM_LIMIT = 60 * 1024 * 1024
SLICE = 16
LOG2E = 1.4426950408889634


def vmem():
    return pl.BlockSpec(memory_space=pltpu.VMEM)


def smem():
    return pl.BlockSpec(memory_space=pltpu.SMEM)


def params(**kw):
    return pltpu.CompilerParams(vmem_limit_bytes=VMEM_LIMIT, **kw)


def split_docs(doc_keys, doc_values, owner_pick, doc_pick, peers):
    docs, length, head_dim = doc_keys.shape
    blocks, fan = owner_pick.shape
    half = peers // 2

    def kernel(key_ref, value_ref, owner_ref, pick_ref, out_ref):
        chosen = (owner_ref[...] * docs + pick_ref[...]).astype(jnp.float32)
        chosen = jnp.pad(chosen, ((0, SLICE - blocks), (0, head_dim - fan)))
        chosen = chosen.astype(jnp.bfloat16)
        for i in range(half):
            rows = slice(i * SLICE, (i + 1) * SLICE)
            out_ref[i, :docs] = key_ref[:, rows, :]
            out_ref[half + i, :docs] = value_ref[:, rows, :]
            out_ref[i, docs] = chosen
            out_ref[half + i, docs] = chosen

    return pl.pallas_call(
        kernel,
        out_shape=jax.ShapeDtypeStruct((peers, docs + 1, SLICE, head_dim), jnp.bfloat16),
        in_specs=[vmem()] * 4,
        out_specs=vmem(),
        compiler_params=params(),
    )(doc_keys, doc_values, owner_pick, doc_pick)


def join_docs(slices):
    peers, docs, rows, head_dim = slices.shape
    half = peers // 2
    shape = jax.ShapeDtypeStruct((docs, half * rows, head_dim), jnp.bfloat16)

    def kernel(in_ref, key_ref, value_ref):
        for i in range(half):
            at = slice(i * rows, (i + 1) * rows)
            key_ref[:, at, :] = in_ref[i]
            value_ref[:, at, :] = in_ref[half + i]

    return pl.pallas_call(
        kernel,
        out_shape=(shape, shape),
        in_specs=[vmem()],
        out_specs=(vmem(), vmem()),
        compiler_params=params(),
    )(slices)


def split_heads(me, queries, out_grad, keys, values, peers):
    blocks, rows, features = queries.shape
    wide = features // peers
    narrow = keys.shape[2] // peers
    width = 2 * wide + 2 * narrow

    def kernel(me_ref, q_ref, g_ref, k_ref, v_ref, *outs):
        for s in range(peers):
            head = lax.rem(me_ref[0] + s, peers)
            big = pl.ds(pl.multiple_of(head * wide, wide), wide)
            small = pl.ds(pl.multiple_of(head * narrow, narrow), narrow)
            outs[s][:, :, 0:wide] = q_ref[:, :, big]
            outs[s][:, :, wide : 2 * wide] = g_ref[:, :, big]
            outs[s][:, :, 2 * wide : 2 * wide + narrow] = k_ref[:, :, small]
            outs[s][:, :, 2 * wide + narrow : width] = v_ref[:, :, small]

    shape = jax.ShapeDtypeStruct((blocks, rows, width), jnp.bfloat16)
    return pl.pallas_call(
        kernel,
        out_shape=(shape,) * peers,
        in_specs=[smem()] + [vmem()] * 4,
        out_specs=(vmem(),) * peers,
        compiler_params=params(),
    )(me, queries, out_grad, keys, values)


def join_heads(me, parts, wide, narrow):
    peers = len(parts)
    blocks, rows, width = parts[0].shape

    def kernel(me_ref, *refs):
        ins, (a_ref, q_ref, k_ref, v_ref) = refs[:peers], refs[peers:]
        for s in range(peers):
            head = lax.rem(me_ref[0] + s, peers)
            big = pl.ds(pl.multiple_of(head * wide, wide), wide)
            small = pl.ds(pl.multiple_of(head * narrow, narrow), narrow)
            a_ref[:, :, big] = ins[s][:, :, 0:wide]
            q_ref[:, :, big] = ins[s][:, :, wide : 2 * wide]
            k_ref[:, :, small] = ins[s][:, :, 2 * wide : 2 * wide + narrow]
            v_ref[:, :, small] = ins[s][:, :, 2 * wide + narrow : width]

    big_shape = jax.ShapeDtypeStruct((blocks, rows, peers * wide), jnp.bfloat16)
    small_shape = jax.ShapeDtypeStruct((blocks, rows, peers * narrow), jnp.bfloat16)
    return pl.pallas_call(
        kernel,
        out_shape=(big_shape, big_shape, small_shape, small_shape),
        in_specs=[smem()] + [vmem()] * peers,
        out_specs=(vmem(),) * 4,
        compiler_params=params(),
    )(me, *parts)


def gather_pairs(slices, blocks, fan, steps=4):
    peers, kept, rows, head_dim = slices.shape
    docs = kept - 1
    count = peers // steps
    table_shape = (peers, 8, head_dim)

    shift = docs.bit_length() - 1

    def kernel(in_ref, out_ref, table_ref, slot_ref, chosen_ref, sem):
        step = pl.program_id(0)
        flat_ref = in_ref.reshape(peers * kept, rows, head_dim)

        @pl.when(step == 0)
        def _():
            tile = in_ref[:, docs].astype(jnp.float32)
            table = tile[:, :8].astype(jnp.int32)
            table_ref[...] = table
            slot_ref[...] = table + lax.shift_right_logical(table, shift)
            copy = pltpu.make_async_copy(slot_ref, chosen_ref, sem)
            copy.start()
            copy.wait()

        def body(i, _):
            q = step * count + i
            for b in range(blocks):
                for f in range(fan):
                    out_ref[i, b * fan + f] = flat_ref[chosen_ref[q, b, f]]
            return 0

        lax.fori_loop(0, count, body, 0)

    return pl.pallas_call(
        kernel,
        out_shape=(
            jax.ShapeDtypeStruct((peers, blocks * fan, rows, head_dim), jnp.bfloat16),
            jax.ShapeDtypeStruct(table_shape, jnp.int32),
        ),
        grid=(steps,),
        in_specs=[pl.BlockSpec(slices.shape, lambda i: (0, 0, 0, 0))],
        out_specs=(
            pl.BlockSpec((count, blocks * fan, rows, head_dim), lambda i: (i, 0, 0, 0)),
            pl.BlockSpec(table_shape, lambda i: (0, 0, 0)),
        ),
        scratch_shapes=[
            pltpu.VMEM(table_shape, jnp.int32),
            pltpu.SMEM(table_shape, jnp.int32),
            pltpu.SemaphoreType.DMA,
        ],
        compiler_params=params(),
    )(slices)


def sum_pairs(table, pairs, docs, blocks, fan, steps=4):
    peers, _, rows, head_dim = pairs.shape
    count = peers // steps

    def kernel(chosen_ref, in_ref, out_ref, acc_ref):
        step = pl.program_id(0)

        @pl.when(step == 0)
        def _():
            acc_ref[...] = jnp.zeros_like(acc_ref)

        def body(i, _):
            q = step * count + i
            for b in range(blocks):
                at = [chosen_ref[q, b, f] for f in range(fan)]
                sums = [
                    acc_ref[at[f]] + in_ref[i, b * fan + f].astype(jnp.float32)
                    for f in range(fan)
                ]
                for f in range(fan):
                    acc_ref[at[f]] = sums[f]
            return 0

        lax.fori_loop(0, count, body, 0)

        @pl.when(step == steps - 1)
        def _():
            total = acc_ref[...].astype(jnp.bfloat16)
            out_ref[...] = total.reshape(out_ref.shape)

    return pl.pallas_call(
        kernel,
        out_shape=jax.ShapeDtypeStruct((peers, docs, rows, head_dim), jnp.bfloat16),
        grid=(steps,),
        in_specs=[
            smem(),
            pl.BlockSpec((count, blocks * fan, rows, head_dim), lambda i: (i, 0, 0, 0)),
        ],
        out_specs=pl.BlockSpec((peers, docs, rows, head_dim), lambda i: (0, 0, 0, 0)),
        scratch_shapes=[pltpu.VMEM((peers * docs, rows, head_dim), jnp.float32)],
        compiler_params=params(),
    )(table, pairs)


def attend_kernel(
    peers, rows, group, head_dim, me_ref, kv_ref, *refs
):
    ins, refs = refs[:peers], refs[peers:]
    dkv_ref, outs = refs[0], refs[1 : 1 + peers]
    k_all, v_all, k_t, v_t, q_n, q_t, g_n, g_t, s_t, p_t, ds_t = refs[1 + peers :]
    half, fan = kv_ref.shape[0] // 2, kv_ref.shape[1]
    doc_rows = half * fan * SLICE
    own = peers * rows
    keys_all = doc_rows + own
    wide = group * head_dim
    scaling = 1.0 / math.sqrt(head_dim)
    f32, bf16 = jnp.float32, jnp.bfloat16

    def dot(a, b):
        return jnp.dot(a, b, preferred_element_type=f32)

    k_all[:doc_rows] = kv_ref[:half].reshape(doc_rows, head_dim)
    v_all[:doc_rows] = kv_ref[half:].reshape(doc_rows, head_dim)
    for s in range(peers):
        at = slice(doc_rows + s * rows, doc_rows + (s + 1) * rows)
        k_all[at] = ins[s][0, :, 2 * wide : 2 * wide + head_dim]
        v_all[at] = ins[s][0, :, 2 * wide + head_dim : 2 * wide + 2 * head_dim]
        for g in range(group):
            to = slice(g * own + s * rows, g * own + (s + 1) * rows)
            q_n[to] = ins[s][0, :, g * head_dim : (g + 1) * head_dim]
            g_n[to] = ins[s][0, :, wide + g * head_dim : wide + (g + 1) * head_dim]
    k_t[...] = k_all[...].T
    v_t[:head_dim] = v_all[...].T
    v_t[head_dim:] = jnp.ones((v_t.shape[0] - head_dim, keys_all), bf16)
    q_t[...] = q_n[...].T
    g_t[...] = g_n[...].T

    def place(index):
        source = lax.rem(me_ref[0] + peers - index // rows, peers)
        return source * rows + lax.rem(index, rows)

    chunk = 2 * own
    key_place = place(lax.broadcasted_iota(jnp.int32, (own, chunk), 0))
    query_place = place(lax.rem(lax.broadcasted_iota(jnp.int32, (own, chunk), 1), own))
    hidden = key_place > query_place

    for c in range(group // 2):
        at = slice(c * chunk, (c + 1) * chunk)
        q_c = q_t[:, at]
        g_c = g_t[:, at]
        s_doc = dot(k_all[:doc_rows], q_c)
        s_t[:doc_rows] = s_doc
        s_own = jnp.where(hidden, -jnp.inf, dot(k_all[doc_rows:], q_c))
        s_t[doc_rows:] = s_own
        top = jnp.maximum(
            jnp.max(s_doc, axis=0, keepdims=True), jnp.max(s_own, axis=0, keepdims=True)
        )
        p = jnp.exp2((s_t[...] - top) * (scaling * LOG2E)).astype(bf16)
        p_t[:, at] = p
        o = dot(v_t[...], p)
        inverse = 1.0 / o[head_dim : head_dim + 1]
        attended = (o[:head_dim] * inverse).astype(bf16)
        row_dot = jnp.sum(
            g_c.astype(f32) * attended.astype(f32), axis=0, keepdims=True
        )
        g_n[at] = (g_c.astype(f32) * inverse).astype(bf16).T
        dp = dot(v_all[...], g_c)
        ds = (p.astype(f32) * ((dp - row_dot) * (inverse * scaling))).astype(bf16)
        ds_t[:, at] = ds
        dq = dot(k_t[...], ds).astype(bf16).T
        attended = attended.T
        for g in range(2):
            lanes = slice((2 * c + g) * head_dim, (2 * c + g + 1) * head_dim)
            shifted = slice(wide + lanes.start, wide + lanes.stop)
            for s in range(peers):
                r = slice(g * own + s * rows, g * own + (s + 1) * rows)
                outs[s][0, :, lanes] = attended[r]
                outs[s][0, :, shifted] = dq[r]

    dv = dot(p_t[...], g_n[...]).astype(bf16)
    dk = dot(ds_t[...], q_n[...]).astype(bf16)
    dkv_ref[:half] = dk[:doc_rows].reshape(half, fan, SLICE, head_dim)
    dkv_ref[half:] = dv[:doc_rows].reshape(half, fan, SLICE, head_dim)
    for s in range(peers):
        at = slice(doc_rows + s * rows, doc_rows + (s + 1) * rows)
        outs[s][0, :, 2 * wide : 2 * wide + head_dim] = dk[at]
        outs[s][0, :, 2 * wide + head_dim : 2 * wide + 2 * head_dim] = dv[at]


def attend(me, pairs, parts, group, head_dim, fan):
    peers = len(parts)
    blocks, rows, width = parts[0].shape
    relays = pairs.shape[0]
    own = peers * rows
    queries = group * own
    keys_all = relays // 2 * fan * SLICE + own
    bf16, f32 = jnp.bfloat16, jnp.float32
    part_spec = pl.BlockSpec((1, rows, width), lambda b: (b, 0, 0))
    pair_spec = pl.BlockSpec((relays, fan, SLICE, head_dim), lambda b: (0, b, 0, 0))
    part_shape = jax.ShapeDtypeStruct((blocks, rows, width), bf16)
    flops = 12 * blocks * queries * keys_all * head_dim
    return pl.pallas_call(
        functools.partial(attend_kernel, peers, rows, group, head_dim),
        out_shape=(jax.ShapeDtypeStruct(pairs.shape, bf16),) + (part_shape,) * peers,
        grid=(blocks,),
        in_specs=[smem(), pair_spec] + [part_spec] * peers,
        out_specs=(pair_spec,) + (part_spec,) * peers,
        scratch_shapes=[
            pltpu.VMEM((keys_all, head_dim), bf16),
            pltpu.VMEM((keys_all, head_dim), bf16),
            pltpu.VMEM((head_dim, keys_all), bf16),
            pltpu.VMEM((head_dim + 16, keys_all), bf16),
            pltpu.VMEM((queries, head_dim), bf16),
            pltpu.VMEM((head_dim, queries), bf16),
            pltpu.VMEM((queries, head_dim), bf16),
            pltpu.VMEM((head_dim, queries), bf16),
            pltpu.VMEM((keys_all, 2 * own), f32),
            pltpu.VMEM((keys_all, queries), bf16),
            pltpu.VMEM((keys_all, queries), bf16),
        ],
        compiler_params=params(),
        cost_estimate=pl.CostEstimate(
            flops=flops,
            bytes_accessed=2 * pairs.size * 2 + 4 * peers * parts[0].size,
            transcendentals=blocks * queries * keys_all,
        ),
    )(me, pairs, *parts)


def exchange(x):
    return lax.all_to_all(x, "docs", split_axis=0, concat_axis=0, tiled=True)


def send(x, distance, peers):
    return lax.ppermute(x, "heads", [(i, (i + distance) % peers) for i in range(peers)])


def shards(queries, keys, values, out_grad, doc_keys, doc_values, owner_pick, doc_pick):
    relays = lax.axis_size("docs")
    peers = lax.axis_size("heads")
    me = lax.axis_index("heads").astype(jnp.int32).reshape(1)
    blocks, fan = owner_pick.shape
    docs, _, head_dim = doc_keys.shape
    wide = queries.shape[2] // peers
    narrow = keys.shape[2] // peers
    group = wide // head_dim

    near, far = (1, 7, 2, 6), (3, 5, 4)
    parts = split_heads(me, queries, out_grad, keys, values, peers)
    got = {0: parts[0]}
    slices = exchange(split_docs(doc_keys, doc_values, owner_pick, doc_pick, relays))
    first = [send(parts[s], s, peers) for s in near]
    slices, *first = lax.optimization_barrier([slices] + first)
    got.update(zip(near, first))
    pairs, table = gather_pairs(slices, blocks, fan)
    pairs = exchange(pairs)
    got.update((s, send(parts[s], s, peers)) for s in far)

    parts = [got[s] for s in range(peers)]
    pair_grads, *parts = attend(me, pairs, parts, group, head_dim, fan)

    back = {0: parts[0]}
    pair_grads = exchange(pair_grads)
    near, far = (1, 7), (3, 5, 4, 2, 6)
    first = [send(parts[s], -s, peers) for s in far]
    pair_grads, *first = lax.optimization_barrier([pair_grads] + first)
    back.update(zip(far, first))
    doc_grads = exchange(sum_pairs(table, pair_grads, docs, blocks, fan))
    back.update((s, send(parts[s], -s, peers)) for s in near)
    doc_key_grad, doc_value_grad = join_docs(doc_grads)
    parts = [back[s] for s in range(peers)]
    attended, query_grad, key_grad, value_grad = join_heads(me, parts, wide, narrow)
    return (attended, query_grad, key_grad, value_grad, doc_key_grad, doc_value_grad)


def solution(mesh):
    tokens = P("docs", "heads", None)
    documents = P("docs", None, "heads")
    picks = P("docs", None)
    return jax.shard_map(
        shards,
        mesh=mesh,
        in_specs=(tokens,) * 4 + (documents,) * 2 + (picks,) * 2,
        out_specs=(tokens,) * 4 + (documents,) * 2,
        check_vma=False,
    )
```

time: 534 us -> 212 us (0.40)
  the two profiles are of different devices: /device:TPU:8 before, /device:TPU:1 now
where the time goes in v1:
time: 212 us; the launch traced here: 211 us
  waiting for transfers between devices  80.7 us (38%)
  starting transfers between devices  62 us (29%)
  Pallas kernels  59.7 us (28%)
  local copies, waits for them, and re-layouts  7.74 us (4%)
    ppermute x14, waiting for transfers between devices, send(): lax.ppermute(x, 'heads', [(i, (i + distance) % peers) for i in range(peer...  67.7 us
    pallas_call x1, Pallas kernels, attend(): pl.pallas_call(functools.partial(attend_kernel, peers, rows, group, head_...  36.6 us
    ppermute x14, starting transfers between devices, send(): lax.ppermute(x, 'heads', [(i, (i + distance) % peers) for i in range(peer...  32.2 us
    all_to_all x4, starting transfers between devices, exchange(): return lax.all_to_all(x, 'docs', split_axis=0, concat_axis=0, tiled=True)  29.8 us
    all_to_all x4, waiting for transfers between devices, exchange(): return lax.all_to_all(x, 'docs', split_axis=0, concat_axis=0, tiled=True)  13 us
    unnamed x32, local copies, waits for them, and re-layouts  7.74 us
    pallas_call x1, Pallas kernels, gather_pairs(): pl.pallas_call(kernel, out_shape=(jax.ShapeDtypeStruct((peers, blocks * f...  6.6 us
    pallas_call x1, Pallas kernels, sum_pairs(): pl.pallas_call(kernel, out_shape=jax.ShapeDtypeStruct((peers, docs, rows,...  6.33 us
  transfers between devices with their start and end apart: 18, of which 15 were waited for; matrix products, arithmetic and copies ran while one was open for 0% of the time, Pallas kernels for 3%

profile of v1, /device:TPU:1, one launch (start us, length us, event | category | flops | bytes accessed | tf_op | source)
XLA Modules:
  0.0 210.9 jit_solution(18029976410129959017)
XLA Ops:
  0.6 2.3 %shard_map.127 = bf16[32,9,16,128]{3,2,1,0:T(8,128)(2,1)} custom-call(bf16[8,256,128]{2,1,0:T(8,128)(2,1)} %key_ref.1, bf16[8,256,128]{2,1,0:T(8,128)(2,1)} %value_ref.1, s32[3,8]{1,0:T(4,128)} %owner_ref.1, s32[3,8]{1,0:T(4,128)} %pick_ref.1), custom_call_target="tpu_custom_call" | custom-call | tf_op jit(solution)/shard_map/pallas_call | solution.py:44
  3.0 8.6 %all-to-all-start = ((bf16[32,9,16,128]{3,2,1,0:T(8,128)(2,1)}), bf16[32,9,16,128]{3,2,1,0:T(8,128)(2,1)S(1)}, u32[]{:S(2)}, u32[]{:S(2)}) async-start(bf16[32,9,16,128]{3,2,1,0:T(8,128)(2,1)} %shard_map.127), calls=%async_computation | async-start | bytes 2359296 | tf_op jit(solution)/shard_map/all_to_all | solution.py:347
  11.6 2.7 %shard_map.128 = (bf16[3,16,2304]{2,1,0:T(8,128)(2,1)}, bf16[3,16,2304]{2,1,0:T(8,128)(2,1)}, bf16[3,16,2304]{2,1,0:T(8,128)(2,1)}, bf16[3,16,2304]{2,1,0:T(8,12...) custom-call(s32[1]{0:T(128)} %bitcast.me_ref, ...), custom_call_target="tpu_custom_call" | custom-call | tf_op jit(solution)/shard_map/pallas_call | solution.py:90
  14.3 1.6 collective-permute-start
  15.9 4.0 %collective-permute-start.1 = (bf16[3,16,2304]{2,1,0:T(8,128)(2,1)}, bf16[3,16,2304]{2,1,0:T(8,128)(2,1)S(1)}, u32[]{:S(2)}, u32[]{:S(2)}) collective-permute-start(bf16[3,16,2304]{2,1,0:T(8,128)(2,1)} %get-tuple-element.43), channel_id=1, source_target_pairs={{0,7},{1,0},{2,1},{3,2},{4,3},{5,4},{6,5},{7,6},{8,15},{9,8},{10,9... | collective-permute-start | bytes 663560 | tf_op jit(solution)/shard_map/ppermute | solution.py:351
  19.9 0.0 collective-permute-start.2
  19.9 3.6 %collective-permute-start.3 = (bf16[3,16,2304]{2,1,0:T(8,128)(2,1)}, bf16[3,16,2304]{2,1,0:T(8,128)(2,1)S(1)}, u32[]{:S(2)}, u32[]{:S(2)}) collective-permute-start(bf16[3,16,2304]{2,1,0:T(8,128)(2,1)} %get-tuple-element.45), channel_id=1, source_target_pairs={{0,6},{1,7},{2,0},{3,1},{4,2},{5,3},{6,4},{7,5},{8,14},{9,15},{10,... | collective-permute-start | bytes 663560 | tf_op jit(solution)/shard_map/ppermute | solution.py:351
  23.5 2.2 %collective-permute-done.refs_1_ = bf16[3,16,2304]{2,1,0:T(8,128)(2,1)S(1)} collective-permute-done((bf16[3,16,2304]{2,1,0:T(8,128)(2,1)}, bf16[3,16,2304]{2,1,0:T(8,128)(2,1)S(1)}, u32[]{:S(2)}, u32[]{:S(2)}) %collective-permute-start) | collective-permute-done | bytes 221216 | tf_op jit(solution)/shard_map/ppermute | solution.py:351
  25.7 0.7 collective-permute-done.1.refs_7_
  26.5 5.5 %collective-permute-done.2.refs_2_ = bf16[3,16,2304]{2,1,0:T(8,128)(2,1)S(1)} collective-permute-done((bf16[3,16,2304]{2,1,0:T(8,128)(2,1)}, bf16[3,16,2304]{2,1,0:T(8,128)(2,1)S(1)}, u32[]{:S(2)}, u32[]{:S(2)}) %collective-permute-start.2) | collective-permute-done | bytes 221216 | tf_op jit(solution)/shard_map/ppermute | solution.py:351
  31.9 2.4 %collective-permute-done.3.refs_6_ = bf16[3,16,2304]{2,1,0:T(8,128)(2,1)S(1)} collective-permute-done((bf16[3,16,2304]{2,1,0:T(8,128)(2,1)}, bf16[3,16,2304]{2,1,0:T(8,128)(2,1)S(1)}, u32[]{:S(2)}, u32[]{:S(2)}) %collective-permute-start.3) | collective-permute-done | bytes 221216 | tf_op jit(solution)/shard_map/ppermute | solution.py:351
  34.3 1.1 copy-done.1
  35.4 6.6 %shard_map.129 = (bf16[32,24,16,128]{3,2,1,0:T(8,128)(2,1)}, s32[32,8,128]{2,1,0:T(8,128)}) custom-call(bf16[32,9,16,128]{3,2,1,0:T(8,128)(2,1)} %copy-done.1), custom_call_target="tpu_custom_call" | custom-call | tf_op jit(solution)/shard_map/pallas_call | solution.py:156
  42.0 8.3 %all-to-all-start.1 = ((bf16[32,24,16,128]{3,2,1,0:T(8,128)(2,1)}), bf16[32,24,16,128]{3,2,1,0:T(8,128)(2,1)S(1)}, u32[]{:S(2)}, u32[]{:S(2)}) async-start(bf16[32,24,16,128]{3,2,1,0:T(8,128)(2,1)} %get-tuple-element.47), calls=%async_computation.1 | async-start | bytes 6291456 | tf_op jit(solution)/shard_map/all_to_all | solution.py:347
  50.3 1.5 collective-permute-start.4
  51.8 3.9 %collective-permute-start.5 = (bf16[3,16,2304]{2,1,0:T(8,128)(2,1)}, bf16[3,16,2304]{2,1,0:T(8,128)(2,1)S(1)}, u32[]{:S(2)}, u32[]{:S(2)}) collective-permute-start(bf16[3,16,2304]{2,1,0:T(8,128)(2,1)} %get-tuple-element.52), channel_id=1, source_target_pairs={{0,4},{1,5},{2,6},{3,7},{4,0},{5,1},{6,2},{7,3},{8,12},{9,13},{10,... | collective-permute-start | bytes 663560 | tf_op jit(solution)/shard_map/ppermute | solution.py:351
  55.7 3.6 %collective-permute-start.6 = (bf16[3,16,2304]{2,1,0:T(8,128)(2,1)}, bf16[3,16,2304]{2,1,0:T(8,128)(2,1)}, u32[]{:S(2)}, u32[]{:S(2)}) collective-permute-start(bf16[3,16,2304]{2,1,0:T(8,128)(2,1)} %get-tuple-element.53), channel_id=1, source_target_pairs={{0,5},{1,6},{2,7},{3,0},{4,1},{5,2},{6,3},{7,4},{8,13},{9,14},{10,... | collective-permute-start | bytes 663560 | tf_op jit(solution)/shard_map/ppermute | solution.py:351
  59.2 12.8 %collective-permute-done.4.refs_3_ = bf16[3,16,2304]{2,1,0:T(8,128)(2,1)S(1)} collective-permute-done((bf16[3,16,2304]{2,1,0:T(8,128)(2,1)}, bf16[3,16,2304]{2,1,0:T(8,128)(2,1)S(1)}, u32[]{:S(2)}, u32[]{:S(2)}) %collective-permute-start.4) | collective-permute-done | bytes 221216 | tf_op jit(solution)/shard_map/ppermute | solution.py:351
  72.1 0.4 collective-permute-done.5.refs_4_
  72.5 0.2 copy-done.14
  72.8 0.7 copy-done.15
  73.5 8.2 %collective-permute-done.6.refs_5_ = bf16[3,16,2304]{2,1,0:T(8,128)(2,1)} collective-permute-done((bf16[3,16,2304]{2,1,0:T(8,128)(2,1)}, bf16[3,16,2304]{2,1,0:T(8,128)(2,1)}, u32[]{:S(2)}, u32[]{:S(2)}) %collective-permute-start.6) | collective-permute-done | bytes 221216 | tf_op jit(solution)/shard_map/ppermute | solution.py:351
  81.7 8.4 %all-to-all-done.1.kv_ref = bf16[32,24,16,128]{3,2,1,0:T(8,128)(2,1)S(1)} async-done(((bf16[32,24,16,128]{3,2,1,0:T(8,128)(2,1)}), bf16[32,24,16,128]{3,2,1,0:T(8,128)(2,1)S(1)}, u32[]{:S(2)}, u32[]{:S(2)}) %all-to-all-start.1) | async-done | bytes 3145760 | tf_op jit(solution)/shard_map/all_to_all | solution.py:347
  90.1 1.7 copy-done.3
  91.7 36.6 %shard_map.130 = (bf16[32,24,16,128]{3,2,1,0:T(8,128)(2,1)}, bf16[3,16,2304]{2,1,0:T(8,128)(2,1)}, bf16[3,16,2304]{2,1,0:T(8,128)(2,1)}, bf16[3,16,2304]{2,1,0:T...) custom-call(s32[1]{0:T(128)} %bitcast.me_ref, ...), custom_call_target="tpu_custom_call" | custom-call | flops 10267656192 | bytes 9830400 | tf_op jit(solution)/shard_map/pallas_call | solution.py:318
  128.3 5.0 %all-to-all-start.2 = ((bf16[32,24,16,128]{3,2,1,0:T(8,128)(2,1)}), bf16[32,24,16,128]{3,2,1,0:T(8,128)(2,1)S(1)}, u32[]{:S(2)}, u32[]{:S(2)}) async-start(bf16[32,24,16,128]{3,2,1,0:T(8,128)(2,1)} %get-tuple-element.58), calls=%async_computation.2 | async-start | bytes 6291456 | tf_op jit(solution)/shard_map/all_to_all | solution.py:347
  133.3 4.5 %collective-permute-start.8 = (bf16[3,16,2304]{2,1,0:T(8,128)(2,1)}, bf16[3,16,2304]{2,1,0:T(8,128)(2,1)S(1)}, u32[]{:S(2)}, u32[]{:S(2)}) collective-permute-start(bf16[3,16,2304]{2,1,0:T(8,128)(2,1)} %get-tuple-element.59), channel_id=1, source_target_pairs={{0,5},{1,6},{2,7},{3,0},{4,1},{5,2},{6,3},{7,4},{8,13},{9,14},{10,... | collective-permute-start | bytes 663560 | tf_op jit(solution)/shard_map/ppermute | solution.py:351
  137.8 0.0 collective-permute-start.9
  137.8 3.2 %collective-permute-start.10 = (bf16[3,16,2304]{2,1,0:T(8,128)(2,1)}, bf16[3,16,2304]{2,1,0:T(8,128)(2,1)S(1)}, u32[]{:S(2)}, u32[]{:S(2)}) collective-permute-start(bf16[3,16,2304]{2,1,0:T(8,128)(2,1)} %get-tuple-element.61), channel_id=1, source_target_pairs={{0,4},{1,5},{2,6},{3,7},{4,0},{5,1},{6,2},{7,3},{8,12},{9,13},{10,... | collective-permute-start | bytes 663560 | tf_op jit(solution)/shard_map/ppermute | solution.py:351
  141.0 4.8 %collective-permute-start.11 = (bf16[3,16,2304]{2,1,0:T(8,128)(2,1)}, bf16[3,16,2304]{2,1,0:T(8,128)(2,1)S(1)}, u32[]{:S(2)}, u32[]{:S(2)}) collective-permute-start(bf16[3,16,2304]{2,1,0:T(8,128)(2,1)} %get-tuple-element.62), channel_id=1, source_target_pairs={{0,6},{1,7},{2,0},{3,1},{4,2},{5,3},{6,4},{7,5},{8,14},{9,15},{10,... | collective-permute-start | bytes 663560 | tf_op jit(solution)/shard_map/ppermute | solution.py:351
  145.9 0.0 collective-permute-start.12
  145.9 13.0 %collective-permute-done.8.refs_3_ = bf16[3,16,2304]{2,1,0:T(8,128)(2,1)S(1)} collective-permute-done((bf16[3,16,2304]{2,1,0:T(8,128)(2,1)}, bf16[3,16,2304]{2,1,0:T(8,128)(2,1)S(1)}, u32[]{:S(2)}, u32[]{:S(2)}) %collective-permute-start.8) | collective-permute-done | bytes 221216 | tf_op jit(solution)/shard_map/ppermute | solution.py:351
  158.9 2.8 %collective-permute-done.10.refs_4_ = bf16[3,16,2304]{2,1,0:T(8,128)(2,1)S(1)} collective-permute-done((bf16[3,16,2304]{2,1,0:T(8,128)(2,1)}, bf16[3,16,2304]{2,1,0:T(8,128)(2,1)S(1)}, u32[]{:S(2)}, u32[]{:S(2)}) %collective-permute-start.10) | collective-permute-done | bytes 221216 | tf_op jit(solution)/shard_map/ppermute | solution.py:351
  161.7 9.7 %collective-permute-done.11.refs_2_ = bf16[3,16,2304]{2,1,0:T(8,128)(2,1)S(1)} collective-permute-done((bf16[3,16,2304]{2,1,0:T(8,128)(2,1)}, bf16[3,16,2304]{2,1,0:T(8,128)(2,1)S(1)}, u32[]{:S(2)}, u32[]{:S(2)}) %collective-permute-start.11) | collective-permute-done | bytes 221216 | tf_op jit(solution)/shard_map/ppermute | solution.py:351
  171.4 0.7 copy-done.7
  172.0 2.7 %collective-permute-done.12.refs_6_ = bf16[3,16,2304]{2,1,0:T(8,128)(2,1)} collective-permute-done((bf16[3,16,2304]{2,1,0:T(8,128)(2,1)}, bf16[3,16,2304]{2,1,0:T(8,128)(2,1)}, u32[]{:S(2)}, u32[]{:S(2)}) %collective-permute-start.12) | collective-permute-done | bytes 221216 | tf_op jit(solution)/shard_map/ppermute | solution.py:351
  174.8 1.6 copy-done
  176.4 6.3 %shard_map.132 = bf16[32,8,16,128]{3,2,1,0:T(8,128)(2,1)} custom-call(s32[32,8,128]{2,1,0:T(8,128)} %get-tuple-element.74.chosen_ref, bf16[32,24,16,128]{3,2,1,0:T(8,128)(2,1)} %copy-done), custom_call_target="tpu_custom_call" | custom-call | tf_op jit(solution)/shard_map/pallas_call | solution.py:207
  182.8 7.9 %all-to-all-start.3 = ((bf16[32,8,16,128]{3,2,1,0:T(8,128)(2,1)}), bf16[32,8,16,128]{3,2,1,0:T(8,128)(2,1)S(1)}, u32[]{:S(2)}, u32[]{:S(2)}) async-start(bf16[32,8,16,128]{3,2,1,0:T(8,128)(2,1)} %shard_map.132), calls=%async_computation.3 | async-start | bytes 2097152 | tf_op jit(solution)/shard_map/all_to_all | solution.py:347
  190.7 0.9 collective-permute-start.7
  191.6 0.7 collective-permute-start.13
  192.3 5.5 %collective-permute-done.7.refs_1_ = bf16[3,16,2304]{2,1,0:T(8,128)(2,1)S(1)} collective-permute-done((bf16[3,16,2304]{2,1,0:T(8,128)(2,1)}, bf16[3,16,2304]{2,1,0:T(8,128)(2,1)S(1)}, u32[]{:S(2)}, u32[]{:S(2)}) %collective-permute-start.7) | collective-permute-done | bytes 221216 | tf_op jit(solution)/shard_map/ppermute | solution.py:351
  197.8 1.7 collective-permute-done.13.refs_7_
  199.5 0.7 copy-done.9
  200.2 2.9 %shard_map.131 = (bf16[3,16,8192]{2,1,0:T(8,128)(2,1)}, bf16[3,16,8192]{2,1,0:T(8,128)(2,1)}, bf16[3,16,1024]{2,1,0:T(8,128)(2,1)}, bf16[3,16,1024]{2,1,0:T(8,128)(2,1)}) custom-call(s32[1]{0:T(128)} %bitcast.me_ref, bf16[3,16,2304]{2,1,0:T(8,128)(2,1)} %get-tuple-element.56.refs_0_, bf16[3,16,2304]{2,1,0:T(8,128)(2,1)} %copy-done.8, ...), custom_call_target="tpu_custom_call" | custom-call | tf_op jit(solution)/shard_map/pallas_call | solution.py:116
  203.0 4.6 %all-to-all-done.3.in_ref = bf16[32,8,16,128]{3,2,1,0:T(8,128)(2,1)S(1)} async-done(((bf16[32,8,16,128]{3,2,1,0:T(8,128)(2,1)}), bf16[32,8,16,128]{3,2,1,0:T(8,128)(2,1)S(1)}, u32[]{:S(2)}, u32[]{:S(2)}) %all-to-all-start.3) | async-done | bytes 1048608 | tf_op jit(solution)/shard_map/all_to_all | solution.py:347
  207.6 1.0 copy-done.2
  208.6 2.3 %shard_map.133 = (bf16[8,256,128]{2,1,0:T(8,128)(2,1)}, bf16[8,256,128]{2,1,0:T(8,128)(2,1)}) custom-call(bf16[32,8,16,128]{3,2,1,0:T(8,128)(2,1)} %copy-done.2), custom_call_target="tpu_custom_call" | custom-call | tf_op jit(solution)/shard_map/pallas_call | solution.py:64
  (27 shorter events, 0.1 us)
Async XLA Ops:
  3.0 31.4 %all-to-all-start = ((bf16[32,9,16,128]{3,2,1,0:T(8,128)(2,1)}), bf16[32,9,16,128]{3,2,1,0:T(8,128)(2,1)S(1)}, u32[]{:S(2)}, u32[]{:S(2)}) async-start(bf16[32,9,16,128]{3,2,1,0:T(8,128)(2,1)} %shard_map.127), calls=%async_computation | async-start | bytes 2359296 | tf_op jit(solution)/shard_map/all_to_all | solution.py:347
  14.3 11.4 %collective-permute-start = (bf16[3,16,2304]{2,1,0:T(8,128)(2,1)}, bf16[3,16,2304]{2,1,0:T(8,128)(2,1)S(1)}, u32[]{:S(2)}, u32[]{:S(2)}) collective-permute-start(bf16[3,16,2304]{2,1,0:T(8,128)(2,1)} %get-tuple-element.42), channel_id=1, source_target_pairs={{0,1},{1,2},{2,3},{3,4},{4,5},{5,6},{6,7},{7,0},{8,9},{9,10},{10,1... | collective-permute-start | bytes 663560 | tf_op jit(solution)/shard_map/ppermute | solution.py:351
  15.9 10.5 %collective-permute-start.1 = (bf16[3,16,2304]{2,1,0:T(8,128)(2,1)}, bf16[3,16,2304]{2,1,0:T(8,128)(2,1)S(1)}, u32[]{:S(2)}, u32[]{:S(2)}) collective-permute-start(bf16[3,16,2304]{2,1,0:T(8,128)(2,1)} %get-tuple-element.43), channel_id=1, source_target_pairs={{0,7},{1,0},{2,1},{3,2},{4,3},{5,4},{6,5},{7,6},{8,15},{9,8},{10,9... | collective-permute-start | bytes 663560 | tf_op jit(solution)/shard_map/ppermute | solution.py:351
  19.9 12.0 %collective-permute-start.2 = (bf16[3,16,2304]{2,1,0:T(8,128)(2,1)}, bf16[3,16,2304]{2,1,0:T(8,128)(2,1)S(1)}, u32[]{:S(2)}, u32[]{:S(2)}) collective-permute-start(bf16[3,16,2304]{2,1,0:T(8,128)(2,1)} %get-tuple-element.44), channel_id=1, source_target_pairs={{0,2},{1,3},{2,4},{3,5},{4,6},{5,7},{6,0},{7,1},{8,10},{9,11},{10,... | collective-permute-start | bytes 663560 | tf_op jit(solution)/shard_map/ppermute | solution.py:351
  19.9 14.4 %collective-permute-start.3 = (bf16[3,16,2304]{2,1,0:T(8,128)(2,1)}, bf16[3,16,2304]{2,1,0:T(8,128)(2,1)S(1)}, u32[]{:S(2)}, u32[]{:S(2)}) collective-permute-start(bf16[3,16,2304]{2,1,0:T(8,128)(2,1)} %get-tuple-element.45), channel_id=1, source_target_pairs={{0,6},{1,7},{2,0},{3,1},{4,2},{5,3},{6,4},{7,5},{8,14},{9,15},{10,... | collective-permute-start | bytes 663560 | tf_op jit(solution)/shard_map/ppermute | solution.py:351
  25.7 64.3 %copy-start.10 = (bf16[3,16,2304]{2,1,0:T(8,128)(2,1)}, bf16[3,16,2304]{2,1,0:T(8,128)(2,1)S(1)}, u32[]{:S(2)}) copy-start(bf16[3,16,2304]{2,1,0:T(8,128)(2,1)S(1)} %collective-permute-done.refs_1_) | copy-start | bytes 663556
  26.5 15.5 %copy-start.11 = (bf16[3,16,2304]{2,1,0:T(8,128)(2,1)}, bf16[3,16,2304]{2,1,0:T(8,128)(2,1)S(1)}, u32[]{:S(2)}) copy-start(bf16[3,16,2304]{2,1,0:T(8,128)(2,1)S(1)} %collective-permute-done.1.refs_7_) | copy-start | bytes 663556
  31.9 10.1 %copy-start.12 = (bf16[3,16,2304]{2,1,0:T(8,128)(2,1)}, bf16[3,16,2304]{2,1,0:T(8,128)(2,1)S(1)}, u32[]{:S(2)}) copy-start(bf16[3,16,2304]{2,1,0:T(8,128)(2,1)S(1)} %collective-permute-done.2.refs_2_) | copy-start | bytes 663556
  34.3 7.7 %copy-start.13 = (bf16[3,16,2304]{2,1,0:T(8,128)(2,1)}, bf16[3,16,2304]{2,1,0:T(8,128)(2,1)S(1)}, u32[]{:S(2)}) copy-start(bf16[3,16,2304]{2,1,0:T(8,128)(2,1)S(1)} %collective-permute-done.3.refs_6_) | copy-start | bytes 663556
  34.3 1.1 copy-start.1
  42.0 48.0 %all-to-all-start.1 = ((bf16[32,24,16,128]{3,2,1,0:T(8,128)(2,1)}), bf16[32,24,16,128]{3,2,1,0:T(8,128)(2,1)S(1)}, u32[]{:S(2)}, u32[]{:S(2)}) async-start(bf16[32,24,16,128]{3,2,1,0:T(8,128)(2,1)} %get-tuple-element.47), calls=%async_computation.1 | async-start | bytes 6291456 | tf_op jit(solution)/shard_map/all_to_all | solution.py:347
  50.3 21.8 %collective-permute-start.4 = (bf16[3,16,2304]{2,1,0:T(8,128)(2,1)}, bf16[3,16,2304]{2,1,0:T(8,128)(2,1)S(1)}, u32[]{:S(2)}, u32[]{:S(2)}) collective-permute-start(bf16[3,16,2304]{2,1,0:T(8,128)(2,1)} %get-tuple-element.51), channel_id=1, source_target_pairs={{0,3},{1,4},{2,5},{3,6},{4,7},{5,0},{6,1},{7,2},{8,11},{9,12},{10,... | collective-permute-start | bytes 663560 | tf_op jit(solution)/shard_map/ppermute | solution.py:351
  51.8 20.7 %collective-permute-start.5 = (bf16[3,16,2304]{2,1,0:T(8,128)(2,1)}, bf16[3,16,2304]{2,1,0:T(8,128)(2,1)S(1)}, u32[]{:S(2)}, u32[]{:S(2)}) collective-permute-start(bf16[3,16,2304]{2,1,0:T(8,128)(2,1)} %get-tuple-element.52), channel_id=1, source_target_pairs={{0,4},{1,5},{2,6},{3,7},{4,0},{5,1},{6,2},{7,3},{8,12},{9,13},{10,... | collective-permute-start | bytes 663560 | tf_op jit(solution)/shard_map/ppermute | solution.py:351
  55.7 26.0 %collective-permute-start.6 = (bf16[3,16,2304]{2,1,0:T(8,128)(2,1)}, bf16[3,16,2304]{2,1,0:T(8,128)(2,1)}, u32[]{:S(2)}, u32[]{:S(2)}) collective-permute-start(bf16[3,16,2304]{2,1,0:T(8,128)(2,1)} %get-tuple-element.53), channel_id=1, source_target_pairs={{0,5},{1,6},{2,7},{3,0},{4,1},{5,2},{6,3},{7,4},{8,13},{9,14},{10,... | collective-permute-start | bytes 663560 | tf_op jit(solution)/shard_map/ppermute | solution.py:351
  72.1 0.7 copy-start.14
  72.7 0.7 copy-start.15
  90.1 1.7 copy-start.3
  128.3 46.5 %all-to-all-start.2 = ((bf16[32,24,16,128]{3,2,1,0:T(8,128)(2,1)}), bf16[32,24,16,128]{3,2,1,0:T(8,128)(2,1)S(1)}, u32[]{:S(2)}, u32[]{:S(2)}) async-start(bf16[32,24,16,128]{3,2,1,0:T(8,128)(2,1)} %get-tuple-element.58), calls=%async_computation.2 | async-start | bytes 6291456 | tf_op jit(solution)/shard_map/all_to_all | solution.py:347
  133.3 25.5 %collective-permute-start.8 = (bf16[3,16,2304]{2,1,0:T(8,128)(2,1)}, bf16[3,16,2304]{2,1,0:T(8,128)(2,1)S(1)}, u32[]{:S(2)}, u32[]{:S(2)}) collective-permute-start(bf16[3,16,2304]{2,1,0:T(8,128)(2,1)} %get-tuple-element.59), channel_id=1, source_target_pairs={{0,5},{1,6},{2,7},{3,0},{4,1},{5,2},{6,3},{7,4},{8,13},{9,14},{10,... | collective-permute-start | bytes 663560 | tf_op jit(solution)/shard_map/ppermute | solution.py:351
  137.8 21.1 %collective-permute-start.9 = (bf16[3,16,2304]{2,1,0:T(8,128)(2,1)}, bf16[3,16,2304]{2,1,0:T(8,128)(2,1)S(1)}, u32[]{:S(2)}, u32[]{:S(2)}) collective-permute-start(bf16[3,16,2304]{2,1,0:T(8,128)(2,1)} %get-tuple-element.60), channel_id=1, source_target_pairs={{0,3},{1,4},{2,5},{3,6},{4,7},{5,0},{6,1},{7,2},{8,11},{9,12},{10,... | collective-permute-start | bytes 663560 | tf_op jit(solution)/shard_map/ppermute | solution.py:351
  137.8 23.8 %collective-permute-start.10 = (bf16[3,16,2304]{2,1,0:T(8,128)(2,1)}, bf16[3,16,2304]{2,1,0:T(8,128)(2,1)S(1)}, u32[]{:S(2)}, u32[]{:S(2)}) collective-permute-start(bf16[3,16,2304]{2,1,0:T(8,128)(2,1)} %get-tuple-element.61), channel_id=1, source_target_pairs={{0,4},{1,5},{2,6},{3,7},{4,0},{5,1},{6,2},{7,3},{8,12},{9,13},{10,... | collective-permute-start | bytes 663560 | tf_op jit(solution)/shard_map/ppermute | solution.py:351
  141.0 30.3 %collective-permute-start.11 = (bf16[3,16,2304]{2,1,0:T(8,128)(2,1)}, bf16[3,16,2304]{2,1,0:T(8,128)(2,1)S(1)}, u32[]{:S(2)}, u32[]{:S(2)}) collective-permute-start(bf16[3,16,2304]{2,1,0:T(8,128)(2,1)} %get-tuple-element.62), channel_id=1, source_target_pairs={{0,6},{1,7},{2,0},{3,1},{4,2},{5,3},{6,4},{7,5},{8,14},{9,15},{10,... | collective-permute-start | bytes 663560 | tf_op jit(solution)/shard_map/ppermute | solution.py:351
  145.9 28.9 %collective-permute-start.12 = (bf16[3,16,2304]{2,1,0:T(8,128)(2,1)}, bf16[3,16,2304]{2,1,0:T(8,128)(2,1)}, u32[]{:S(2)}, u32[]{:S(2)}) collective-permute-start(bf16[3,16,2304]{2,1,0:T(8,128)(2,1)} %get-tuple-element.63), channel_id=1, source_target_pairs={{0,2},{1,3},{2,4},{3,5},{4,6},{5,7},{6,0},{7,1},{8,10},{9,11},{10,... | collective-permute-start | bytes 663560 | tf_op jit(solution)/shard_map/ppermute | solution.py:351
  158.9 40.6 %copy-start.4 = (bf16[3,16,2304]{2,1,0:T(8,128)(2,1)}, bf16[3,16,2304]{2,1,0:T(8,128)(2,1)S(1)}, u32[]{:S(2)}) copy-start(bf16[3,16,2304]{2,1,0:T(8,128)(2,1)S(1)} %collective-permute-done.8.refs_3_) | copy-start | bytes 663556
  158.9 12.5 %copy-start.5 = (bf16[3,16,2304]{2,1,0:T(8,128)(2,1)}, bf16[3,16,2304]{2,1,0:T(8,128)(2,1)S(1)}, u32[]{:S(2)}) copy-start(bf16[3,16,2304]{2,1,0:T(8,128)(2,1)S(1)} %collective-permute-done.9.refs_5_) | copy-start | bytes 663556
  161.7 9.7 %copy-start.6 = (bf16[3,16,2304]{2,1,0:T(8,128)(2,1)}, bf16[3,16,2304]{2,1,0:T(8,128)(2,1)S(1)}, u32[]{:S(2)}) copy-start(bf16[3,16,2304]{2,1,0:T(8,128)(2,1)S(1)} %collective-permute-done.10.refs_4_) | copy-start | bytes 663556
  171.4 0.7 copy-start.7
  174.8 1.6 copy-start
  182.8 24.9 %all-to-all-start.3 = ((bf16[32,8,16,128]{3,2,1,0:T(8,128)(2,1)}), bf16[32,8,16,128]{3,2,1,0:T(8,128)(2,1)S(1)}, u32[]{:S(2)}, u32[]{:S(2)}) async-start(bf16[32,8,16,128]{3,2,1,0:T(8,128)(2,1)} %shard_map.132), calls=%async_computation.3 | async-start | bytes 2097152 | tf_op jit(solution)/shard_map/all_to_all | solution.py:347
  190.7 7.1 %collective-permute-start.7 = (bf16[3,16,2304]{2,1,0:T(8,128)(2,1)}, bf16[3,16,2304]{2,1,0:T(8,128)(2,1)S(1)}, u32[]{:S(2)}, u32[]{:S(2)}) collective-permute-start(bf16[3,16,2304]{2,1,0:T(8,128)(2,1)} %get-tuple-element.57), channel_id=1, source_target_pairs={{0,7},{1,0},{2,1},{3,2},{4,3},{5,4},{6,5},{7,6},{8,15},{9,8},{10,9... | collective-permute-start | bytes 663560 | tf_op jit(solution)/shard_map/ppermute | solution.py:351
  191.6 7.9 %collective-permute-start.13 = (bf16[3,16,2304]{2,1,0:T(8,128)(2,1)}, bf16[3,16,2304]{2,1,0:T(8,128)(2,1)S(1)}, u32[]{:S(2)}, u32[]{:S(2)}) collective-permute-start(bf16[3,16,2304]{2,1,0:T(8,128)(2,1)} %get-tuple-element.69), channel_id=1, source_target_pairs={{0,1},{1,2},{2,3},{3,4},{4,5},{5,6},{6,7},{7,0},{8,9},{9,10},{10,1... | collective-permute-start | bytes 663560 | tf_op jit(solution)/shard_map/ppermute | solution.py:351
  197.8 1.7 copy-start.8
  199.5 0.7 copy-start.9
  207.6 1.0 copy-start.2

commit v2 on v1

--- a/solution.py
+++ b/solution.py
@@ -8,7 +8,7 @@
 from jax.experimental.pallas import tpu as pltpu
 from jax.sharding import PartitionSpec as P
 
-VMEM_LIMIT = 60 * 1024 * 1024
+VMEM_LIMIT = 63 * 1024 * 1024
 SLICE = 16
 LOG2E = 1.4426950408889634
 
@@ -32,8 +32,9 @@
 
     def kernel(key_ref, value_ref, owner_ref, pick_ref, out_ref):
         chosen = (owner_ref[...] * docs + pick_ref[...]).astype(jnp.float32)
-        chosen = jnp.pad(chosen, ((0, SLICE - blocks), (0, head_dim - fan)))
-        chosen = chosen.astype(jnp.bfloat16)
+        row = jnp.concatenate([chosen[b : b + 1] for b in range(blocks)], axis=1)
+        row = jnp.pad(row, ((0, 0), (0, head_dim - blocks * fan)))
+        chosen = jnp.broadcast_to(row, (SLICE, head_dim)).astype(jnp.bfloat16)
         for i in range(half):
             rows = slice(i * SLICE, (i + 1) * SLICE)
             out_ref[i, :docs] = key_ref[:, rows, :]
@@ -50,10 +51,12 @@
     )(doc_keys, doc_values, owner_pick, doc_pick)
 
 
-def join_docs(slices):
+def join_docs(slices, steps=2):
     peers, docs, rows, head_dim = slices.shape
     half = peers // 2
+    part = docs // steps
     shape = jax.ShapeDtypeStruct((docs, half * rows, head_dim), jnp.bfloat16)
+    doc_spec = pl.BlockSpec((part, half * rows, head_dim), lambda i: (i, 0, 0))
 
     def kernel(in_ref, key_ref, value_ref):
         for i in range(half):
@@ -64,8 +67,9 @@
     return pl.pallas_call(
         kernel,
         out_shape=(shape, shape),
-        in_specs=[vmem()],
-        out_specs=(vmem(), vmem()),
+        grid=(steps,),
+        in_specs=[pl.BlockSpec((peers, part, rows, head_dim), lambda i: (0, i, 0, 0))],
+        out_specs=(doc_spec, doc_spec),
         compiler_params=params(),
     )(slices)
 
@@ -122,51 +126,50 @@
     )(me, *parts)
 
 
-def gather_pairs(slices, blocks, fan, steps=4):
+def gather_pairs(slices, blocks, fan, steps=2):
     peers, kept, rows, head_dim = slices.shape
     docs = kept - 1
-    count = peers // steps
-    table_shape = (peers, 8, head_dim)
-
     shift = docs.bit_length() - 1
-
-    def kernel(in_ref, out_ref, table_ref, slot_ref, chosen_ref, sem):
+    part = peers // steps
+    pairs = blocks * fan
+    table_shape = (peers, head_dim)
+
+    def kernel(in_ref, out_ref, table_ref, chosen_ref, sem):
         step = pl.program_id(0)
         flat_ref = in_ref.reshape(peers * kept, rows, head_dim)
 
         @pl.when(step == 0)
         def _():
             tile = in_ref[:, docs].astype(jnp.float32)
-            table = tile[:, :8].astype(jnp.int32)
-            table_ref[...] = table
-            slot_ref[...] = table + lax.shift_right_logical(table, shift)
-            copy = pltpu.make_async_copy(slot_ref, chosen_ref, sem)
+            table = tile[:, 0].astype(jnp.int32)
+            table_ref[...] = table + lax.shift_right_logical(table, shift)
+            copy = pltpu.make_async_copy(table_ref, chosen_ref, sem)
             copy.start()
             copy.wait()
 
         def body(i, _):
-            q = step * count + i
-            for b in range(blocks):
+            q = step * part + i
+            for p in range(0, pairs, fan):
+                tiles = [flat_ref[chosen_ref[q, p + f]] for f in range(fan)]
                 for f in range(fan):
-                    out_ref[i, b * fan + f] = flat_ref[chosen_ref[q, b, f]]
+                    out_ref[i, p + f] = tiles[f]
             return 0
 
-        lax.fori_loop(0, count, body, 0)
+        lax.fori_loop(0, part, body, 0)
 
     return pl.pallas_call(
         kernel,
         out_shape=(
-            jax.ShapeDtypeStruct((peers, blocks * fan, rows, head_dim), jnp.bfloat16),
+            jax.ShapeDtypeStruct((peers, pairs, rows, head_dim), jnp.bfloat16),
             jax.ShapeDtypeStruct(table_shape, jnp.int32),
         ),
         grid=(steps,),
         in_specs=[pl.BlockSpec(slices.shape, lambda i: (0, 0, 0, 0))],
         out_specs=(
-            pl.BlockSpec((count, blocks * fan, rows, head_dim), lambda i: (i, 0, 0, 0)),
-            pl.BlockSpec(table_shape, lambda i: (0, 0, 0)),
+            pl.BlockSpec((part, pairs, rows, head_dim), lambda i: (i, 0, 0, 0)),
+            pl.BlockSpec(table_shape, lambda i: (0, 0)),
         ),
         scratch_shapes=[
-            pltpu.VMEM(table_shape, jnp.int32),
             pltpu.SMEM(table_shape, jnp.int32),
             pltpu.SemaphoreType.DMA,
         ],
@@ -174,9 +177,10 @@
     )(slices)
 
 
-def sum_pairs(table, pairs, docs, blocks, fan, steps=4):
-    peers, _, rows, head_dim = pairs.shape
-    count = peers // steps
+def sum_pairs(table, pairs, kept, fan, steps=2):
+    peers, count, rows, head_dim = pairs.shape
+    part = peers // steps
+    out_shape = (peers, kept - 1, rows, head_dim)
 
     def kernel(chosen_ref, in_ref, out_ref, acc_ref):
         step = pl.program_id(0)
@@ -186,34 +190,35 @@
             acc_ref[...] = jnp.zeros_like(acc_ref)
 
         def body(i, _):
-            q = step * count + i
-            for b in range(blocks):
-                at = [chosen_ref[q, b, f] for f in range(fan)]
+            q = step * part + i
+            for p in range(0, count, fan):
+                at = [chosen_ref[q, p + f] for f in range(fan)]
                 sums = [
-                    acc_ref[at[f]] + in_ref[i, b * fan + f].astype(jnp.float32)
+                    acc_ref[at[f]] + in_ref[i, p + f].astype(jnp.float32)
                     for f in range(fan)
                 ]
                 for f in range(fan):
                     acc_ref[at[f]] = sums[f]
             return 0
 
-        lax.fori_loop(0, count, body, 0)
+        lax.fori_loop(0, part, body, 0)
 
         @pl.when(step == steps - 1)
         def _():
-            total = acc_ref[...].astype(jnp.bfloat16)
-            out_ref[...] = total.reshape(out_ref.shape)
-
-    return pl.pallas_call(
-        kernel,
-        out_shape=jax.ShapeDtypeStruct((peers, docs, rows, head_dim), jnp.bfloat16),
+            for i in range(peers):
+                rounded = acc_ref[i * kept : i * kept + kept - 1]
+                out_ref[i] = rounded.astype(jnp.bfloat16)
+
+    return pl.pallas_call(
+        kernel,
+        out_shape=jax.ShapeDtypeStruct(out_shape, jnp.bfloat16),
         grid=(steps,),
         in_specs=[
             smem(),
-            pl.BlockSpec((count, blocks * fan, rows, head_dim), lambda i: (i, 0, 0, 0)),
+            pl.BlockSpec((part, count, rows, head_dim), lambda i: (i, 0, 0, 0)),
         ],
-        out_specs=pl.BlockSpec((peers, docs, rows, head_dim), lambda i: (0, 0, 0, 0)),
-        scratch_shapes=[pltpu.VMEM((peers * docs, rows, head_dim), jnp.float32)],
+        out_specs=pl.BlockSpec(out_shape, lambda i: (0, 0, 0, 0)),
+        scratch_shapes=[pltpu.VMEM((peers * kept, rows, head_dim), jnp.float32)],
         compiler_params=params(),
     )(table, pairs)
 
@@ -231,6 +236,7 @@
     wide = group * head_dim
     scaling = 1.0 / math.sqrt(head_dim)
     f32, bf16 = jnp.float32, jnp.bfloat16
+    queries = group * own
 
     def dot(a, b):
         return jnp.dot(a, b, preferred_element_type=f32)
@@ -259,39 +265,65 @@
     key_place = place(lax.broadcasted_iota(jnp.int32, (own, chunk), 0))
     query_place = place(lax.rem(lax.broadcasted_iota(jnp.int32, (own, chunk), 1), own))
     hidden = key_place > query_place
-
-    for c in range(group // 2):
+    tiles = [slice(t, min(t + 256, doc_rows)) for t in range(0, doc_rows, 256)]
+    tiles.append(slice(doc_rows, keys_all))
+
+    def rows_max(x):
+        return jnp.max(x.reshape(x.shape[0] // 8, 8, chunk), axis=0)
+
+    def score(c, buf):
+        q_c = q_t[:, c * chunk : (c + 1) * chunk]
+        top = None
+        for t in tiles:
+            x = dot(k_all[t], q_c)
+            if t.start == doc_rows:
+                x = jnp.where(hidden, -jnp.inf, x)
+            buf[t] = x
+            m = rows_max(x)
+            top = m if top is None else jnp.maximum(top, m)
+        return jnp.max(top, axis=0, keepdims=True)
+
+    def finish(c, o):
         at = slice(c * chunk, (c + 1) * chunk)
-        q_c = q_t[:, at]
-        g_c = g_t[:, at]
-        s_doc = dot(k_all[:doc_rows], q_c)
-        s_t[:doc_rows] = s_doc
-        s_own = jnp.where(hidden, -jnp.inf, dot(k_all[doc_rows:], q_c))
-        s_t[doc_rows:] = s_own
-        top = jnp.maximum(
-            jnp.max(s_doc, axis=0, keepdims=True), jnp.max(s_own, axis=0, keepdims=True)
-        )
-        p = jnp.exp2((s_t[...] - top) * (scaling * LOG2E)).astype(bf16)
-        p_t[:, at] = p
-        o = dot(v_t[...], p)
+        g_c = g_t[:, at].astype(f32)
         inverse = 1.0 / o[head_dim : head_dim + 1]
         attended = (o[:head_dim] * inverse).astype(bf16)
-        row_dot = jnp.sum(
-            g_c.astype(f32) * attended.astype(f32), axis=0, keepdims=True
-        )
-        g_n[at] = (g_c.astype(f32) * inverse).astype(bf16).T
-        dp = dot(v_all[...], g_c)
-        ds = (p.astype(f32) * ((dp - row_dot) * (inverse * scaling))).astype(bf16)
-        ds_t[:, at] = ds
-        dq = dot(k_t[...], ds).astype(bf16).T
-        attended = attended.T
-        for g in range(2):
-            lanes = slice((2 * c + g) * head_dim, (2 * c + g + 1) * head_dim)
-            shifted = slice(wide + lanes.start, wide + lanes.stop)
+        row_dot = jnp.sum(g_c * attended.astype(f32), axis=0, keepdims=True)
+        g_n[at] = (g_c * inverse).astype(bf16).T
+        return attended, row_dot, inverse * scaling
+
+    def put(c, x, base):
+        x = x.T
+        for g in range(chunk // own):
+            lanes = slice(base + (c * (chunk // own) + g) * head_dim, base + (c * (chunk // own) + g + 1) * head_dim)
             for s in range(peers):
-                r = slice(g * own + s * rows, g * own + (s + 1) * rows)
-                outs[s][0, :, lanes] = attended[r]
-                outs[s][0, :, shifted] = dq[r]
+                outs[s][0, :, lanes] = x[g * own + s * rows : g * own + (s + 1) * rows]
+
+    tops = [score(0, s_t.at[0])]
+    count = queries // chunk
+    for c in range(count):
+        at = slice(c * chunk, (c + 1) * chunk)
+        cur, nxt = s_t.at[c % 2], s_t.at[(c + 1) % 2]
+        m = None
+        q_c = q_t[:, (c + 1) * chunk : (c + 2) * chunk] if c + 1 < count else None
+        for t in tiles:
+            p_t[t, at] = jnp.exp2((cur[t] - tops[c]) * (scaling * LOG2E)).astype(bf16)
+            if q_c is not None:
+                x = dot(k_all[t], q_c)
+                if t.start == doc_rows:
+                    x = jnp.where(hidden, -jnp.inf, x)
+                nxt[t] = x
+                y = rows_max(x)
+                m = y if m is None else jnp.maximum(m, y)
+        if m is not None:
+            tops.append(jnp.max(m, axis=0, keepdims=True))
+        attended, row_dot, factor = finish(c, dot(v_t[...], p_t[:, at]))
+        g_c = g_t[:, at]
+        for t in tiles:
+            dp = dot(v_all[t], g_c)
+            ds_t[t, at] = (p_t[t, at].astype(f32) * ((dp - row_dot) * factor)).astype(bf16)
+        put(c, attended, 0)
+        put(c, dot(k_t[...], ds_t[:, at]).astype(bf16), wide)
 
     dv = dot(p_t[...], g_n[...]).astype(bf16)
     dk = dot(ds_t[...], q_n[...]).astype(bf16)
@@ -305,15 +337,16 @@
 
 def attend(me, pairs, parts, group, head_dim, fan):
     peers = len(parts)
-    blocks, rows, width = parts[0].shape
+    _, rows, width = parts[0].shape
     relays = pairs.shape[0]
+    blocks = pairs.shape[1] // fan
     own = peers * rows
     queries = group * own
     keys_all = relays // 2 * fan * SLICE + own
     bf16, f32 = jnp.bfloat16, jnp.float32
     part_spec = pl.BlockSpec((1, rows, width), lambda b: (b, 0, 0))
     pair_spec = pl.BlockSpec((relays, fan, SLICE, head_dim), lambda b: (0, b, 0, 0))
-    part_shape = jax.ShapeDtypeStruct((blocks, rows, width), bf16)
+    part_shape = jax.ShapeDtypeStruct(parts[0].shape, bf16)
     flops = 12 * blocks * queries * keys_all * head_dim
     return pl.pallas_call(
         functools.partial(attend_kernel, peers, rows, group, head_dim),
@@ -330,7 +363,7 @@
             pltpu.VMEM((head_dim, queries), bf16),
             pltpu.VMEM((queries, head_dim), bf16),
             pltpu.VMEM((head_dim, queries), bf16),
-            pltpu.VMEM((keys_all, 2 * own), f32),
+            pltpu.VMEM((2, keys_all, 2 * own), f32),
             pltpu.VMEM((keys_all, queries), bf16),
             pltpu.VMEM((keys_all, queries), bf16),
         ],
@@ -361,28 +394,26 @@
     narrow = keys.shape[2] // peers
     group = wide // head_dim
 
-    near, far = (1, 7, 2, 6), (3, 5, 4)
+    def beside(array, distances, sign, into):
+        sent = [send(parts[s], sign * s, peers) for s in distances]
+        array, *sent = lax.optimization_barrier([array] + sent)
+        into.update(zip(distances, sent))
+        return array
+
     parts = split_heads(me, queries, out_grad, keys, values, peers)
     got = {0: parts[0]}
     slices = exchange(split_docs(doc_keys, doc_values, owner_pick, doc_pick, relays))
-    first = [send(parts[s], s, peers) for s in near]
-    slices, *first = lax.optimization_barrier([slices] + first)
-    got.update(zip(near, first))
+    slices = beside(slices, (1, 7), 1, got)
     pairs, table = gather_pairs(slices, blocks, fan)
-    pairs = exchange(pairs)
-    got.update((s, send(parts[s], s, peers)) for s in far)
+    pairs = beside(exchange(pairs), (2, 6, 3, 5, 4), 1, got)
 
     parts = [got[s] for s in range(peers)]
-    pair_grads, *parts = attend(me, pairs, parts, group, head_dim, fan)
+    grads, *parts = attend(me, pairs, parts, group, head_dim, fan)
 
     back = {0: parts[0]}
-    pair_grads = exchange(pair_grads)
-    near, far = (1, 7), (3, 5, 4, 2, 6)
-    first = [send(parts[s], -s, peers) for s in far]
-    pair_grads, *first = lax.optimization_barrier([pair_grads] + first)
-    back.update(zip(far, first))
-    doc_grads = exchange(sum_pairs(table, pair_grads, docs, blocks, fan))
-    back.update((s, send(parts[s], -s, peers)) for s in near)
+    grads = beside(exchange(grads), (2, 6, 3, 5, 4), -1, back)
+    doc_grads = exchange(sum_pairs(table, grads, docs + 1, fan))
+    back.update((s, send(parts[s], -s, peers)) for s in (1, 7))
     doc_key_grad, doc_value_grad = join_docs(doc_grads)
     parts = [back[s] for s in range(peers)]
     attended, query_grad, key_grad, value_grad = join_heads(me, parts, wide, narrow)

time: 212 us -> 187 us (0.88)
  the two profiles are of different devices: /device:TPU:1 before, /device:TPU:65 now
where the time goes in v2:
time: 187 us; the launch traced here: 186 us
  waiting for transfers between devices  82.1 us (44%)
  starting transfers between devices  56.9 us (30%)
  Pallas kernels  45.1 us (24%)
    ppermute x14, waiting for transfers between devices, send(): lax.ppermute(x, 'heads', [(i, (i + distance) % peers) for i in range(peer...  70.1 us
    all_to_all x4, starting transfers between devices, exchange(): return lax.all_to_all(x, 'docs', split_axis=0, concat_axis=0, tiled=True)  29.2 us
    ppermute x14, starting transfers between devices, send(): lax.ppermute(x, 'heads', [(i, (i + distance) % peers) for i in range(peer...  27.7 us
    pallas_call x1, Pallas kernels, attend(): pl.pallas_call(functools.partial(attend_kernel, peers, rows, group, head_...  26.9 us
    all_to_all x4, waiting for transfers between devices, exchange(): return lax.all_to_all(x, 'docs', split_axis=0, concat_axis=0, tiled=True)  11.9 us
    pallas_call x1, Pallas kernels, gather_pairs(): pl.pallas_call(kernel, out_shape=(jax.ShapeDtypeStruct((peers, pairs, row...  4.27 us
    pallas_call x1, Pallas kernels, sum_pairs(): pl.pallas_call(kernel, out_shape=jax.ShapeDtypeStruct(out_shape, jnp.bflo...  3.89 us
  transfers between devices with their start and end apart: 18, of which 13 were waited for; matrix products, arithmetic and copies ran while one was open for 0% of the time, Pallas kernels for 3%

profile of v2, /device:TPU:65, one launch (start us, length us, event | category | flops | bytes accessed | tf_op | source)
XLA Modules:
  0.0 186.4 jit_solution(3880685084983978866)
XLA Ops:
  0.6 2.3 %shard_map.127 = bf16[32,9,16,128]{3,2,1,0:T(8,128)(2,1)} custom-call(bf16[8,256,128]{2,1,0:T(8,128)(2,1)} %key_ref.1, bf16[8,256,128]{2,1,0:T(8,128)(2,1)} %value_ref.1, s32[3,8]{1,0:T(4,128)} %owner_ref.1, s32[3,8]{1,0:T(4,128)} %pick_ref.1), custom_call_target="tpu_custom_call" | custom-call | tf_op jit(solution)/shard_map/pallas_call | solution.py:45
  3.0 7.8 %all-to-all-start = ((bf16[32,9,16,128]{3,2,1,0:T(8,128)(2,1)}), bf16[32,9,16,128]{3,2,1,0:T(8,128)(2,1)}, u32[]{:S(2)}, u32[]{:S(2)}) async-start(bf16[32,9,16,128]{3,2,1,0:T(8,128)(2,1)} %shard_map.127), calls=%async_computation | async-start | bytes 2359296 | tf_op jit(solution)/shard_map/all_to_all | solution.py:380
  10.8 2.7 %shard_map.128 = (bf16[3,16,2304]{2,1,0:T(8,128)(2,1)}, bf16[3,16,2304]{2,1,0:T(8,128)(2,1)}, bf16[3,16,2304]{2,1,0:T(8,128)(2,1)}, bf16[3,16,2304]{2,1,0:T(8,12...) custom-call(s32[1]{0:T(128)} %bitcast.me_ref, ...), custom_call_target="tpu_custom_call" | custom-call | tf_op jit(solution)/shard_map/pallas_call | solution.py:94
  13.5 1.6 collective-permute-start
  15.2 0.0 collective-permute-start.1
  15.2 5.4 %collective-permute-done.refs_1_ = bf16[3,16,2304]{2,1,0:T(8,128)(2,1)S(1)} collective-permute-done((bf16[3,16,2304]{2,1,0:T(8,128)(2,1)}, bf16[3,16,2304]{2,1,0:T(8,128)(2,1)S(1)}, u32[]{:S(2)}, u32[]{:S(2)}) %collective-permute-start) | collective-permute-done | bytes 221216 | tf_op jit(solution)/shard_map/ppermute | solution.py:384
  20.6 3.0 %collective-permute-done.1.refs_7_ = bf16[3,16,2304]{2,1,0:T(8,128)(2,1)S(1)} collective-permute-done((bf16[3,16,2304]{2,1,0:T(8,128)(2,1)}, bf16[3,16,2304]{2,1,0:T(8,128)(2,1)S(1)}, u32[]{:S(2)}, u32[]{:S(2)}) %collective-permute-start.1) | collective-permute-done | bytes 221216 | tf_op jit(solution)/shard_map/ppermute | solution.py:384
  23.6 5.6 %all-to-all-done.in_ref = bf16[32,9,16,128]{3,2,1,0:T(8,128)(2,1)} async-done(((bf16[32,9,16,128]{3,2,1,0:T(8,128)(2,1)}), bf16[32,9,16,128]{3,2,1,0:T(8,128)(2,1)}, u32[]{:S(2)}, u32[]{:S(2)}) %all-to-all-start) | async-done | bytes 1179680 | tf_op jit(solution)/shard_map/all_to_all | solution.py:380
  29.2 4.3 %shard_map.129 = (bf16[32,24,16,128]{3,2,1,0:T(8,128)(2,1)}, s32[32,128]{1,0:T(8,128)}) custom-call(bf16[32,9,16,128]{3,2,1,0:T(8,128)(2,1)} %all-to-all-done.in_ref), custom_call_target="tpu_custom_call" | custom-call | tf_op jit(solution)/shard_map/pallas_call | solution.py:160
  33.5 0.0 copy-start.12
  33.5 0.0 copy-start.10
  33.6 4.8 %all-to-all-start.1 = ((bf16[32,24,16,128]{3,2,1,0:T(8,128)(2,1)}), bf16[32,24,16,128]{3,2,1,0:T(8,128)(2,1)}, u32[]{:S(2)}, u32[]{:S(2)}) async-start(bf16[32,24,16,128]{3,2,1,0:T(8,128)(2,1)} %get-tuple-element.49), calls=%async_computation.1 | async-start | bytes 6291456 | tf_op jit(solution)/shard_map/all_to_all | solution.py:380
  38.4 4.3 %collective-permute-start.2 = (bf16[3,16,2304]{2,1,0:T(8,128)(2,1)S(1)}, bf16[3,16,2304]{2,1,0:T(8,128)(2,1)S(1)}, u32[]{:S(2)}, u32[]{:S(2)}) collective-permute-start(bf16[3,16,2304]{2,1,0:T(8,128)(2,1)S(1)} %copy-done.12), channel_id=1, source_target_pairs={{0,2},{1,3},{2,4},{3,5},{4,6},{5,7},{6,0},{7,1},{8,10},{9,11},{10,... | collective-permute-start | bytes 663560 | tf_op jit(solution)/shard_map/ppermute | solution.py:384
  42.6 0.0 collective-permute-start.3
  42.7 4.0 %collective-permute-start.4 = (bf16[3,16,2304]{2,1,0:T(8,128)(2,1)S(1)}, bf16[3,16,2304]{2,1,0:T(8,128)(2,1)S(1)}, u32[]{:S(2)}, u32[]{:S(2)}) collective-permute-start(bf16[3,16,2304]{2,1,0:T(8,128)(2,1)S(1)} %copy-done.10), channel_id=1, source_target_pairs={{0,3},{1,4},{2,5},{3,6},{4,7},{5,0},{6,1},{7,2},{8,11},{9,12},{10,... | collective-permute-start | bytes 663560 | tf_op jit(solution)/shard_map/ppermute | solution.py:384
  46.7 0.5 collective-permute-start.5
  47.2 3.2 %collective-permute-start.6 = (bf16[3,16,2304]{2,1,0:T(8,128)(2,1)S(1)}, bf16[3,16,2304]{2,1,0:T(8,128)(2,1)S(1)}, u32[]{:S(2)}, u32[]{:S(2)}) collective-permute-start(bf16[3,16,2304]{2,1,0:T(8,128)(2,1)S(1)} %copy-done.8), channel_id=1, source_target_pairs={{0,4},{1,5},{2,6},{3,7},{4,0},{5,1},{6,2},{7,3},{8,12},{9,13},{10,... | collective-permute-start | bytes 663560 | tf_op jit(solution)/shard_map/ppermute | solution.py:384
  50.4 8.8 %collective-permute-done.2.refs_2_ = bf16[3,16,2304]{2,1,0:T(8,128)(2,1)S(1)} collective-permute-done((bf16[3,16,2304]{2,1,0:T(8,128)(2,1)S(1)}, bf16[3,16,2304]{2,1,0:T(8,128)(2,1)S(1)}, u32[]{:S(2)}, u32[]{:S(2)}) %collective-permute-start.2) | collective-permute-done | bytes 221216 | tf_op jit(solution)/shard_map/ppermute | solution.py:384
  59.2 0.0 collective-permute-done.3.refs_6_
  59.2 10.2 %collective-permute-done.4.refs_3_ = bf16[3,16,2304]{2,1,0:T(8,128)(2,1)S(1)} collective-permute-done((bf16[3,16,2304]{2,1,0:T(8,128)(2,1)S(1)}, bf16[3,16,2304]{2,1,0:T(8,128)(2,1)S(1)}, u32[]{:S(2)}, u32[]{:S(2)}) %collective-permute-start.4) | collective-permute-done | bytes 221216 | tf_op jit(solution)/shard_map/ppermute | solution.py:384
  69.4 0.0 collective-permute-done.5.refs_5_
  69.4 8.1 %collective-permute-done.6.refs_4_ = bf16[3,16,2304]{2,1,0:T(8,128)(2,1)S(1)} collective-permute-done((bf16[3,16,2304]{2,1,0:T(8,128)(2,1)S(1)}, bf16[3,16,2304]{2,1,0:T(8,128)(2,1)S(1)}, u32[]{:S(2)}, u32[]{:S(2)}) %collective-permute-start.6) | collective-permute-done | bytes 221216 | tf_op jit(solution)/shard_map/ppermute | solution.py:384
  77.5 0.7 copy-done.21
  78.2 0.1 all-to-all-done.1.kv_ref
  78.3 26.9 %shard_map.130 = (bf16[32,24,16,128]{3,2,1,0:T(8,128)(2,1)}, bf16[3,16,2304]{2,1,0:T(8,128)(2,1)}, bf16[3,16,2304]{2,1,0:T(8,128)(2,1)}, bf16[3,16,2304]{2,1,0:T...) custom-call(s32[1]{0:T(128)} %bitcast.me_ref, ...), custom_call_target="tpu_custom_call" | custom-call | flops 10267656192 | bytes 9830400 | tf_op jit(solution)/shard_map/pallas_call | solution.py:351
  105.3 8.2 %all-to-all-start.2 = ((bf16[32,24,16,128]{3,2,1,0:T(8,128)(2,1)}), bf16[32,24,16,128]{3,2,1,0:T(8,128)(2,1)}, u32[]{:S(2)}, u32[]{:S(2)}) async-start(bf16[32,24,16,128]{3,2,1,0:T(8,128)(2,1)} %get-tuple-element.66), calls=%async_computation.2 | async-start | bytes 6291456 | tf_op jit(solution)/shard_map/all_to_all | solution.py:380
  113.5 0.1 collective-permute-start.8
  113.6 3.6 %collective-permute-start.9 = (bf16[3,16,2304]{2,1,0:T(8,128)(2,1)S(1)}, bf16[3,16,2304]{2,1,0:T(8,128)(2,1)S(1)}, u32[]{:S(2)}, u32[]{:S(2)}) collective-permute-start(bf16[3,16,2304]{2,1,0:T(8,128)(2,1)S(1)} %copy-done.20), channel_id=1, source_target_pairs={{0,2},{1,3},{2,4},{3,5},{4,6},{5,7},{6,0},{7,1},{8,10},{9,11},{10,... | collective-permute-start | bytes 663560 | tf_op jit(solution)/shard_map/ppermute | solution.py:384
  117.1 3.7 %collective-permute-start.10 = (bf16[3,16,2304]{2,1,0:T(8,128)(2,1)S(1)}, bf16[3,16,2304]{2,1,0:T(8,128)(2,1)S(1)}, u32[]{:S(2)}, u32[]{:S(2)}) collective-permute-start(bf16[3,16,2304]{2,1,0:T(8,128)(2,1)S(1)} %copy-done.18), channel_id=1, source_target_pairs={{0,5},{1,6},{2,7},{3,0},{4,1},{5,2},{6,3},{7,4},{8,13},{9,14},{10,... | collective-permute-start | bytes 663560 | tf_op jit(solution)/shard_map/ppermute | solution.py:384
  120.8 0.8 collective-permute-start.11
  121.6 4.4 %collective-permute-start.12 = (bf16[3,16,2304]{2,1,0:T(8,128)(2,1)S(1)}, bf16[3,16,2304]{2,1,0:T(8,128)(2,1)}, u32[]{:S(2)}, u32[]{:S(2)}) collective-permute-start(bf16[3,16,2304]{2,1,0:T(8,128)(2,1)S(1)} %copy-done.14), channel_id=1, source_target_pairs={{0,4},{1,5},{2,6},{3,7},{4,0},{5,1},{6,2},{7,3},{8,12},{9,13},{10,... | collective-permute-start | bytes 663560 | tf_op jit(solution)/shard_map/ppermute | solution.py:384
  126.0 0.0 collective-permute-done.8.refs_2_
  126.0 0.0 collective-permute-done.9.refs_6_
  126.0 15.8 %collective-permute-done.10.refs_3_ = bf16[3,16,2304]{2,1,0:T(8,128)(2,1)S(1)} collective-permute-done((bf16[3,16,2304]{2,1,0:T(8,128)(2,1)S(1)}, bf16[3,16,2304]{2,1,0:T(8,128)(2,1)S(1)}, u32[]{:S(2)}, u32[]{:S(2)}) %collective-permute-start.10) | collective-permute-done | bytes 221216 | tf_op jit(solution)/shard_map/ppermute | solution.py:384
  141.8 0.9 collective-permute-done.11.refs_5_
  142.8 12.3 %collective-permute-done.12.refs_4_ = bf16[3,16,2304]{2,1,0:T(8,128)(2,1)} collective-permute-done((bf16[3,16,2304]{2,1,0:T(8,128)(2,1)S(1)}, bf16[3,16,2304]{2,1,0:T(8,128)(2,1)}, u32[]{:S(2)}, u32[]{:S(2)}) %collective-permute-start.12) | collective-permute-done | bytes 221216 | tf_op jit(solution)/shard_map/ppermute | solution.py:384
  155.0 0.0 all-to-all-done.2.in_ref
  155.0 3.9 %shard_map.132 = bf16[32,8,16,128]{3,2,1,0:T(8,128)(2,1)} custom-call(s32[32,128]{1,0:T(8,128)} %get-tuple-element.82.chosen_ref, bf16[32,24,16,128]{3,2,1,0:T(8,128)(2,1)} %all-to-all-done.2.in_ref), custom_call_target="tpu_custom_call" | custom-call | tf_op jit(solution)/shard_map/pallas_call | solution.py:212
  158.9 8.5 %all-to-all-start.3 = ((bf16[32,8,16,128]{3,2,1,0:T(8,128)(2,1)}), bf16[32,8,16,128]{3,2,1,0:T(8,128)(2,1)}, u32[]{:S(2)}, u32[]{:S(2)}) async-start(bf16[32,8,16,128]{3,2,1,0:T(8,128)(2,1)} %shard_map.132), calls=%async_computation.3 | async-start | bytes 2097152 | tf_op jit(solution)/shard_map/all_to_all | solution.py:380
  167.4 0.1 collective-permute-start.7
  167.5 1.5 collective-permute-start.13
  169.0 5.6 %collective-permute-done.7.refs_1_ = bf16[3,16,2304]{2,1,0:T(8,128)(2,1)S(1)} collective-permute-done((bf16[3,16,2304]{2,1,0:T(8,128)(2,1)}, bf16[3,16,2304]{2,1,0:T(8,128)(2,1)S(1)}, u32[]{:S(2)}, u32[]{:S(2)}) %collective-permute-start.7) | collective-permute-done | bytes 221216 | tf_op jit(solution)/shard_map/ppermute | solution.py:384
  174.5 0.1 collective-permute-done.13.refs_7_
  174.6 0.6 copy-done.4
  175.2 0.1 copy-done.5
  175.3 2.9 %shard_map.131 = (bf16[3,16,8192]{2,1,0:T(8,128)(2,1)}, bf16[3,16,8192]{2,1,0:T(8,128)(2,1)}, bf16[3,16,1024]{2,1,0:T(8,128)(2,1)}, bf16[3,16,1024]{2,1,0:T(8,128)(2,1)}) custom-call(s32[1]{0:T(128)} %bitcast.me_ref, bf16[3,16,2304]{2,1,0:T(8,128)(2,1)} %get-tuple-element.64.refs_0_, bf16[3,16,2304]{2,1,0:T(8,128)(2,1)} %copy-done.4, ...), custom_call_target="tpu_custom_call" | custom-call | tf_op jit(solution)/shard_map/pallas_call | solution.py:120
  178.2 6.2 %all-to-all-done.3.in_ref = bf16[32,8,16,128]{3,2,1,0:T(8,128)(2,1)} async-done(((bf16[32,8,16,128]{3,2,1,0:T(8,128)(2,1)}), bf16[32,8,16,128]{3,2,1,0:T(8,128)(2,1)}, u32[]{:S(2)}, u32[]{:S(2)}) %all-to-all-start.3) | async-done | bytes 1048608 | tf_op jit(solution)/shard_map/all_to_all | solution.py:380
  184.4 2.0 %shard_map.133 = (bf16[8,256,128]{2,1,0:T(8,128)(2,1)}, bf16[8,256,128]{2,1,0:T(8,128)(2,1)}) custom-call(bf16[32,8,16,128]{3,2,1,0:T(8,128)(2,1)} %all-to-all-done.3.in_ref), custom_call_target="tpu_custom_call" | custom-call | tf_op jit(solution)/shard_map/pallas_call | solution.py:67
  (41 shorter events, 0.1 us)
Async XLA Ops:
  3.0 26.2 %all-to-all-start = ((bf16[32,9,16,128]{3,2,1,0:T(8,128)(2,1)}), bf16[32,9,16,128]{3,2,1,0:T(8,128)(2,1)}, u32[]{:S(2)}, u32[]{:S(2)}) async-start(bf16[32,9,16,128]{3,2,1,0:T(8,128)(2,1)} %shard_map.127), calls=%async_computation | async-start | bytes 2359296 | tf_op jit(solution)/shard_map/all_to_all | solution.py:380
  13.5 7.0 %collective-permute-start = (bf16[3,16,2304]{2,1,0:T(8,128)(2,1)}, bf16[3,16,2304]{2,1,0:T(8,128)(2,1)S(1)}, u32[]{:S(2)}, u32[]{:S(2)}) collective-permute-start(bf16[3,16,2304]{2,1,0:T(8,128)(2,1)} %get-tuple-element.46), channel_id=1, source_target_pairs={{0,1},{1,2},{2,3},{3,4},{4,5},{5,6},{6,7},{7,0},{8,9},{9,10},{10,1... | collective-permute-start | bytes 663560 | tf_op jit(solution)/shard_map/ppermute | solution.py:384
  15.2 8.4 %collective-permute-start.1 = (bf16[3,16,2304]{2,1,0:T(8,128)(2,1)}, bf16[3,16,2304]{2,1,0:T(8,128)(2,1)S(1)}, u32[]{:S(2)}, u32[]{:S(2)}) collective-permute-start(bf16[3,16,2304]{2,1,0:T(8,128)(2,1)} %get-tuple-element.47), channel_id=1, source_target_pairs={{0,7},{1,0},{2,1},{3,2},{4,3},{5,4},{6,5},{7,6},{8,15},{9,8},{10,9... | collective-permute-start | bytes 663560 | tf_op jit(solution)/shard_map/ppermute | solution.py:384
  20.6 13.0 %copy-start.6 = (bf16[3,16,2304]{2,1,0:T(8,128)(2,1)}, bf16[3,16,2304]{2,1,0:T(8,128)(2,1)S(1)}, u32[]{:S(2)}) copy-start(bf16[3,16,2304]{2,1,0:T(8,128)(2,1)S(1)} %collective-permute-done.refs_1_) | copy-start | bytes 663556
  23.6 9.9 %copy-start.7 = (bf16[3,16,2304]{2,1,0:T(8,128)(2,1)}, bf16[3,16,2304]{2,1,0:T(8,128)(2,1)S(1)}, u32[]{:S(2)}) copy-start(bf16[3,16,2304]{2,1,0:T(8,128)(2,1)S(1)} %collective-permute-done.1.refs_7_) | copy-start | bytes 663556
  33.5 4.9 %copy-start.12 = (bf16[3,16,2304]{2,1,0:T(8,128)(2,1)S(1)}, bf16[3,16,2304]{2,1,0:T(8,128)(2,1)}, u32[]{:S(2)}) copy-start(bf16[3,16,2304]{2,1,0:T(8,128)(2,1)} %get-tuple-element.50) | copy-start | bytes 663556
  33.5 9.2 %copy-start.11 = (bf16[3,16,2304]{2,1,0:T(8,128)(2,1)S(1)}, bf16[3,16,2304]{2,1,0:T(8,128)(2,1)}, u32[]{:S(2)}) copy-start(bf16[3,16,2304]{2,1,0:T(8,128)(2,1)} %get-tuple-element.51) | copy-start | bytes 663556
  33.5 9.2 %copy-start.10 = (bf16[3,16,2304]{2,1,0:T(8,128)(2,1)S(1)}, bf16[3,16,2304]{2,1,0:T(8,128)(2,1)}, u32[]{:S(2)}) copy-start(bf16[3,16,2304]{2,1,0:T(8,128)(2,1)} %get-tuple-element.52) | copy-start | bytes 663556
  33.5 13.2 %copy-start.9 = (bf16[3,16,2304]{2,1,0:T(8,128)(2,1)S(1)}, bf16[3,16,2304]{2,1,0:T(8,128)(2,1)}, u32[]{:S(2)}) copy-start(bf16[3,16,2304]{2,1,0:T(8,128)(2,1)} %get-tuple-element.53) | copy-start | bytes 663556
  33.5 13.7 %copy-start.8 = (bf16[3,16,2304]{2,1,0:T(8,128)(2,1)S(1)}, bf16[3,16,2304]{2,1,0:T(8,128)(2,1)}, u32[]{:S(2)}) copy-start(bf16[3,16,2304]{2,1,0:T(8,128)(2,1)} %get-tuple-element.54) | copy-start | bytes 663556
  33.6 44.7 %all-to-all-start.1 = ((bf16[32,24,16,128]{3,2,1,0:T(8,128)(2,1)}), bf16[32,24,16,128]{3,2,1,0:T(8,128)(2,1)}, u32[]{:S(2)}, u32[]{:S(2)}) async-start(bf16[32,24,16,128]{3,2,1,0:T(8,128)(2,1)} %get-tuple-element.49), calls=%async_computation.1 | async-start | bytes 6291456 | tf_op jit(solution)/shard_map/all_to_all | solution.py:380
  38.4 20.9 %collective-permute-start.2 = (bf16[3,16,2304]{2,1,0:T(8,128)(2,1)S(1)}, bf16[3,16,2304]{2,1,0:T(8,128)(2,1)S(1)}, u32[]{:S(2)}, u32[]{:S(2)}) collective-permute-start(bf16[3,16,2304]{2,1,0:T(8,128)(2,1)S(1)} %copy-done.12), channel_id=1, source_target_pairs={{0,2},{1,3},{2,4},{3,5},{4,6},{5,7},{6,0},{7,1},{8,10},{9,11},{10,... | collective-permute-start | bytes 663560 | tf_op jit(solution)/shard_map/ppermute | solution.py:384
  42.6 16.6 %collective-permute-start.3 = (bf16[3,16,2304]{2,1,0:T(8,128)(2,1)S(1)}, bf16[3,16,2304]{2,1,0:T(8,128)(2,1)S(1)}, u32[]{:S(2)}, u32[]{:S(2)}) collective-permute-start(bf16[3,16,2304]{2,1,0:T(8,128)(2,1)S(1)} %copy-done.11), channel_id=1, source_target_pairs={{0,6},{1,7},{2,0},{3,1},{4,2},{5,3},{6,4},{7,5},{8,14},{9,15},{10,... | collective-permute-start | bytes 663560 | tf_op jit(solution)/shard_map/ppermute | solution.py:384
  42.7 26.8 %collective-permute-start.4 = (bf16[3,16,2304]{2,1,0:T(8,128)(2,1)S(1)}, bf16[3,16,2304]{2,1,0:T(8,128)(2,1)S(1)}, u32[]{:S(2)}, u32[]{:S(2)}) collective-permute-start(bf16[3,16,2304]{2,1,0:T(8,128)(2,1)S(1)} %copy-done.10), channel_id=1, source_target_pairs={{0,3},{1,4},{2,5},{3,6},{4,7},{5,0},{6,1},{7,2},{8,11},{9,12},{10,... | collective-permute-start | bytes 663560 | tf_op jit(solution)/shard_map/ppermute | solution.py:384
  46.7 22.7 %collective-permute-start.5 = (bf16[3,16,2304]{2,1,0:T(8,128)(2,1)S(1)}, bf16[3,16,2304]{2,1,0:T(8,128)(2,1)S(1)}, u32[]{:S(2)}, u32[]{:S(2)}) collective-permute-start(bf16[3,16,2304]{2,1,0:T(8,128)(2,1)S(1)} %copy-done.9), channel_id=1, source_target_pairs={{0,5},{1,6},{2,7},{3,0},{4,1},{5,2},{6,3},{7,4},{8,13},{9,14},{10,... | collective-permute-start | bytes 663560 | tf_op jit(solution)/shard_map/ppermute | solution.py:384
  47.2 30.3 %collective-permute-start.6 = (bf16[3,16,2304]{2,1,0:T(8,128)(2,1)S(1)}, bf16[3,16,2304]{2,1,0:T(8,128)(2,1)S(1)}, u32[]{:S(2)}, u32[]{:S(2)}) collective-permute-start(bf16[3,16,2304]{2,1,0:T(8,128)(2,1)S(1)} %copy-done.8), channel_id=1, source_target_pairs={{0,4},{1,5},{2,6},{3,7},{4,0},{5,1},{6,2},{7,3},{8,12},{9,13},{10,... | collective-permute-start | bytes 663560 | tf_op jit(solution)/shard_map/ppermute | solution.py:384
  59.2 19.1 %copy-start.13 = (bf16[3,16,2304]{2,1,0:T(8,128)(2,1)}, bf16[3,16,2304]{2,1,0:T(8,128)(2,1)S(1)}, u32[]{:S(2)}) copy-start(bf16[3,16,2304]{2,1,0:T(8,128)(2,1)S(1)} %collective-permute-done.2.refs_2_) | copy-start | bytes 663556
  59.2 19.1 %copy-start.15 = (bf16[3,16,2304]{2,1,0:T(8,128)(2,1)}, bf16[3,16,2304]{2,1,0:T(8,128)(2,1)S(1)}, u32[]{:S(2)}) copy-start(bf16[3,16,2304]{2,1,0:T(8,128)(2,1)S(1)} %collective-permute-done.3.refs_6_) | copy-start | bytes 663556
  69.4 8.9 %copy-start.17 = (bf16[3,16,2304]{2,1,0:T(8,128)(2,1)}, bf16[3,16,2304]{2,1,0:T(8,128)(2,1)S(1)}, u32[]{:S(2)}) copy-start(bf16[3,16,2304]{2,1,0:T(8,128)(2,1)S(1)} %collective-permute-done.4.refs_3_) | copy-start | bytes 663556
  69.4 8.9 %copy-start.19 = (bf16[3,16,2304]{2,1,0:T(8,128)(2,1)}, bf16[3,16,2304]{2,1,0:T(8,128)(2,1)S(1)}, u32[]{:S(2)}) copy-start(bf16[3,16,2304]{2,1,0:T(8,128)(2,1)S(1)} %collective-permute-done.5.refs_5_) | copy-start | bytes 663556
  77.5 0.7 copy-start.21
  105.3 8.2 %copy-start.22 = (bf16[3,16,2304]{2,1,0:T(8,128)(2,1)S(1)}, bf16[3,16,2304]{2,1,0:T(8,128)(2,1)}, u32[]{:S(2)}) copy-start(bf16[3,16,2304]{2,1,0:T(8,128)(2,1)} %get-tuple-element.67) | copy-start | bytes 663556
  105.3 8.3 %copy-start.20 = (bf16[3,16,2304]{2,1,0:T(8,128)(2,1)S(1)}, bf16[3,16,2304]{2,1,0:T(8,128)(2,1)}, u32[]{:S(2)}) copy-start(bf16[3,16,2304]{2,1,0:T(8,128)(2,1)} %get-tuple-element.68) | copy-start | bytes 663556
  105.3 11.9 %copy-start.18 = (bf16[3,16,2304]{2,1,0:T(8,128)(2,1)S(1)}, bf16[3,16,2304]{2,1,0:T(8,128)(2,1)}, u32[]{:S(2)}) copy-start(bf16[3,16,2304]{2,1,0:T(8,128)(2,1)} %get-tuple-element.69) | copy-start | bytes 663556
  105.3 15.5 %copy-start.16 = (bf16[3,16,2304]{2,1,0:T(8,128)(2,1)S(1)}, bf16[3,16,2304]{2,1,0:T(8,128)(2,1)}, u32[]{:S(2)}) copy-start(bf16[3,16,2304]{2,1,0:T(8,128)(2,1)} %get-tuple-element.70) | copy-start | bytes 663556
  105.3 16.3 %copy-start.14 = (bf16[3,16,2304]{2,1,0:T(8,128)(2,1)S(1)}, bf16[3,16,2304]{2,1,0:T(8,128)(2,1)}, u32[]{:S(2)}) copy-start(bf16[3,16,2304]{2,1,0:T(8,128)(2,1)} %get-tuple-element.71) | copy-start | bytes 663556
  105.3 49.7 %all-to-all-start.2 = ((bf16[32,24,16,128]{3,2,1,0:T(8,128)(2,1)}), bf16[32,24,16,128]{3,2,1,0:T(8,128)(2,1)}, u32[]{:S(2)}, u32[]{:S(2)}) async-start(bf16[32,24,16,128]{3,2,1,0:T(8,128)(2,1)} %get-tuple-element.66), calls=%async_computation.2 | async-start | bytes 6291456 | tf_op jit(solution)/shard_map/all_to_all | solution.py:380
  113.5 12.5 %collective-permute-start.8 = (bf16[3,16,2304]{2,1,0:T(8,128)(2,1)S(1)}, bf16[3,16,2304]{2,1,0:T(8,128)(2,1)S(1)}, u32[]{:S(2)}, u32[]{:S(2)}) collective-permute-start(bf16[3,16,2304]{2,1,0:T(8,128)(2,1)S(1)} %copy-done.22), channel_id=1, source_target_pairs={{0,6},{1,7},{2,0},{3,1},{4,2},{5,3},{6,4},{7,5},{8,14},{9,15},{10,... | collective-permute-start | bytes 663560 | tf_op jit(solution)/shard_map/ppermute | solution.py:384
  113.6 12.4 %collective-permute-start.9 = (bf16[3,16,2304]{2,1,0:T(8,128)(2,1)S(1)}, bf16[3,16,2304]{2,1,0:T(8,128)(2,1)S(1)}, u32[]{:S(2)}, u32[]{:S(2)}) collective-permute-start(bf16[3,16,2304]{2,1,0:T(8,128)(2,1)S(1)} %copy-done.20), channel_id=1, source_target_pairs={{0,2},{1,3},{2,4},{3,5},{4,6},{5,7},{6,0},{7,1},{8,10},{9,11},{10,... | collective-permute-start | bytes 663560 | tf_op jit(solution)/shard_map/ppermute | solution.py:384
  117.1 24.7 %collective-permute-start.10 = (bf16[3,16,2304]{2,1,0:T(8,128)(2,1)S(1)}, bf16[3,16,2304]{2,1,0:T(8,128)(2,1)S(1)}, u32[]{:S(2)}, u32[]{:S(2)}) collective-permute-start(bf16[3,16,2304]{2,1,0:T(8,128)(2,1)S(1)} %copy-done.18), channel_id=1, source_target_pairs={{0,5},{1,6},{2,7},{3,0},{4,1},{5,2},{6,3},{7,4},{8,13},{9,14},{10,... | collective-permute-start | bytes 663560 | tf_op jit(solution)/shard_map/ppermute | solution.py:384
  120.8 21.9 %collective-permute-start.11 = (bf16[3,16,2304]{2,1,0:T(8,128)(2,1)S(1)}, bf16[3,16,2304]{2,1,0:T(8,128)(2,1)S(1)}, u32[]{:S(2)}, u32[]{:S(2)}) collective-permute-start(bf16[3,16,2304]{2,1,0:T(8,128)(2,1)S(1)} %copy-done.16), channel_id=1, source_target_pairs={{0,3},{1,4},{2,5},{3,6},{4,7},{5,0},{6,1},{7,2},{8,11},{9,12},{10,... | collective-permute-start | bytes 663560 | tf_op jit(solution)/shard_map/ppermute | solution.py:384
  121.6 33.4 %collective-permute-start.12 = (bf16[3,16,2304]{2,1,0:T(8,128)(2,1)S(1)}, bf16[3,16,2304]{2,1,0:T(8,128)(2,1)}, u32[]{:S(2)}, u32[]{:S(2)}) collective-permute-start(bf16[3,16,2304]{2,1,0:T(8,128)(2,1)S(1)} %copy-done.14), channel_id=1, source_target_pairs={{0,4},{1,5},{2,6},{3,7},{4,0},{5,1},{6,2},{7,3},{8,12},{9,13},{10,... | collective-permute-start | bytes 663560 | tf_op jit(solution)/shard_map/ppermute | solution.py:384
  126.0 32.9 %copy-start = (bf16[3,16,2304]{2,1,0:T(8,128)(2,1)}, bf16[3,16,2304]{2,1,0:T(8,128)(2,1)S(1)}, u32[]{:S(2)}) copy-start(bf16[3,16,2304]{2,1,0:T(8,128)(2,1)S(1)} %collective-permute-done.8.refs_2_) | copy-start | bytes 663556
  126.0 32.9 %copy-start.1 = (bf16[3,16,2304]{2,1,0:T(8,128)(2,1)}, bf16[3,16,2304]{2,1,0:T(8,128)(2,1)S(1)}, u32[]{:S(2)}) copy-start(bf16[3,16,2304]{2,1,0:T(8,128)(2,1)S(1)} %collective-permute-done.9.refs_6_) | copy-start | bytes 663556
  141.8 17.1 %copy-start.2 = (bf16[3,16,2304]{2,1,0:T(8,128)(2,1)}, bf16[3,16,2304]{2,1,0:T(8,128)(2,1)S(1)}, u32[]{:S(2)}) copy-start(bf16[3,16,2304]{2,1,0:T(8,128)(2,1)S(1)} %collective-permute-done.10.refs_3_) | copy-start | bytes 663556
  142.8 16.2 %copy-start.3 = (bf16[3,16,2304]{2,1,0:T(8,128)(2,1)}, bf16[3,16,2304]{2,1,0:T(8,128)(2,1)S(1)}, u32[]{:S(2)}) copy-start(bf16[3,16,2304]{2,1,0:T(8,128)(2,1)S(1)} %collective-permute-done.11.refs_5_) | copy-start | bytes 663556
  158.9 25.5 %all-to-all-start.3 = ((bf16[32,8,16,128]{3,2,1,0:T(8,128)(2,1)}), bf16[32,8,16,128]{3,2,1,0:T(8,128)(2,1)}, u32[]{:S(2)}, u32[]{:S(2)}) async-start(bf16[32,8,16,128]{3,2,1,0:T(8,128)(2,1)} %shard_map.132), calls=%async_computation.3 | async-start | bytes 2097152 | tf_op jit(solution)/shard_map/all_to_all | solution.py:380
  167.4 7.1 %collective-permute-start.7 = (bf16[3,16,2304]{2,1,0:T(8,128)(2,1)}, bf16[3,16,2304]{2,1,0:T(8,128)(2,1)S(1)}, u32[]{:S(2)}, u32[]{:S(2)}) collective-permute-start(bf16[3,16,2304]{2,1,0:T(8,128)(2,1)} %get-tuple-element.65), channel_id=1, source_target_pairs={{0,7},{1,0},{2,1},{3,2},{4,3},{5,4},{6,5},{7,6},{8,15},{9,8},{10,9... | collective-permute-start | bytes 663560 | tf_op jit(solution)/shard_map/ppermute | solution.py:384
  167.5 7.1 %collective-permute-start.13 = (bf16[3,16,2304]{2,1,0:T(8,128)(2,1)}, bf16[3,16,2304]{2,1,0:T(8,128)(2,1)S(1)}, u32[]{:S(2)}, u32[]{:S(2)}) collective-permute-start(bf16[3,16,2304]{2,1,0:T(8,128)(2,1)} %get-tuple-element.77), channel_id=1, source_target_pairs={{0,1},{1,2},{2,3},{3,4},{4,5},{5,6},{6,7},{7,0},{8,9},{9,10},{10,1... | collective-permute-start | bytes 663560 | tf_op jit(solution)/shard_map/ppermute | solution.py:384
  174.5 0.7 copy-start.4
  174.6 0.7 copy-start.5

commit v3 on v2

--- a/solution.py
+++ b/solution.py
@@ -8,7 +8,7 @@
 from jax.experimental.pallas import tpu as pltpu
 from jax.sharding import PartitionSpec as P
 
-VMEM_LIMIT = 63 * 1024 * 1024
+VMEM = 64 * 1024 * 1024
 SLICE = 16
 LOG2E = 1.4426950408889634
 
@@ -21,8 +21,8 @@
     return pl.BlockSpec(memory_space=pltpu.SMEM)
 
 
-def params(**kw):
-    return pltpu.CompilerParams(vmem_limit_bytes=VMEM_LIMIT, **kw)
+def params(room):
+    return pltpu.CompilerParams(vmem_limit_bytes=VMEM - room)
 
 
 def split_docs(doc_keys, doc_values, owner_pick, doc_pick, peers):
@@ -47,7 +47,7 @@
         out_shape=jax.ShapeDtypeStruct((peers, docs + 1, SLICE, head_dim), jnp.bfloat16),
         in_specs=[vmem()] * 4,
         out_specs=vmem(),
-        compiler_params=params(),
+        compiler_params=params(131072),
     )(doc_keys, doc_values, owner_pick, doc_pick)
 
 
@@ -70,7 +70,7 @@
         grid=(steps,),
         in_specs=[pl.BlockSpec((peers, part, rows, head_dim), lambda i: (0, i, 0, 0))],
         out_specs=(doc_spec, doc_spec),
-        compiler_params=params(),
+        compiler_params=params(33554432),
     )(slices)
 
 
@@ -96,7 +96,7 @@
         out_shape=(shape,) * peers,
         in_specs=[smem()] + [vmem()] * 4,
         out_specs=(vmem(),) * peers,
-        compiler_params=params(),
+        compiler_params=params(1500000),
     )(me, queries, out_grad, keys, values)
 
 
@@ -122,7 +122,7 @@
         out_shape=(big_shape, big_shape, small_shape, small_shape),
         in_specs=[smem()] + [vmem()] * peers,
         out_specs=(vmem(),) * 4,
-        compiler_params=params(),
+        compiler_params=params(1500000),
     )(me, *parts)
 
 
@@ -173,7 +173,7 @@
             pltpu.SMEM(table_shape, jnp.int32),
             pltpu.SemaphoreType.DMA,
         ],
-        compiler_params=params(),
+        compiler_params=params(33554432),
     )(slices)
 
 
@@ -219,7 +219,7 @@
         ],
         out_specs=pl.BlockSpec(out_shape, lambda i: (0, 0, 0, 0)),
         scratch_shapes=[pltpu.VMEM((peers * kept, rows, head_dim), jnp.float32)],
-        compiler_params=params(),
+        compiler_params=params(33554432),
     )(table, pairs)
 
 
@@ -367,7 +367,7 @@
             pltpu.VMEM((keys_all, queries), bf16),
             pltpu.VMEM((keys_all, queries), bf16),
         ],
-        compiler_params=params(),
+        compiler_params=params(131072),
         cost_estimate=pl.CostEstimate(
             flops=flops,
             bytes_accessed=2 * pairs.size * 2 + 4 * peers * parts[0].size,

time: 187 us -> 184 us (0.984)
  Pallas kernels: 45.1 us -> 40 us
  local copies, waits for them, and re-layouts: 1.46 us -> 6.06 us
    unnamed x46 -> x34, local copies, waits for them, and re-layouts: 1.46 us -> 6.06 us
    pallas_call x1, Pallas kernels: 4.27 us -> 1.83 us  [gather_pairs(): pl.pallas_call(kernel, out_shape=(jax.ShapeDtypeStruct((peers, pairs, row...]
    ppermute x14, waiting for transfers between devices: 70.1 us -> 68 us  [send(): lax.ppermute(x, 'heads', [(i, (i + distance) % peers) for i in range(peer...]
where the time goes in v3:
time: 184 us; the launch traced here: 183 us
  waiting for transfers between devices  80.3 us (44%)
  starting transfers between devices  56 us (30%)
  Pallas kernels  40 us (22%)
  local copies, waits for them, and re-layouts  6.06 us (3%)
    ppermute x14, waiting for transfers between devices, send(): lax.ppermute(x, 'heads', [(i, (i + distance) % peers) for i in range(peer...  68 us
    all_to_all x4, starting transfers between devices, exchange(): return lax.all_to_all(x, 'docs', split_axis=0, concat_axis=0, tiled=True)  28.3 us
    ppermute x14, starting transfers between devices, send(): lax.ppermute(x, 'heads', [(i, (i + distance) % peers) for i in range(peer...  27.7 us
    pallas_call x1, Pallas kernels, attend(): pl.pallas_call(functools.partial(attend_kernel, peers, rows, group, head_...  26.9 us
    all_to_all x4, waiting for transfers between devices, exchange(): return lax.all_to_all(x, 'docs', split_axis=0, concat_axis=0, tiled=True)  12.4 us
    unnamed x34, local copies, waits for them, and re-layouts  6.06 us
  transfers between devices with their start and end apart: 18, of which 13 were waited for; matrix products, arithmetic and copies ran while one was open for 0% of the time, Pallas kernels for 3%

profile of v3, /device:TPU:65, one launch (start us, length us, event | category | flops | bytes accessed | tf_op | source)
XLA Modules:
  0.0 183.1 jit_solution(2829586336056498766)
XLA Ops:
  0.6 2.3 %shard_map.127 = bf16[32,9,16,128]{3,2,1,0:T(8,128)(2,1)} custom-call(bf16[8,256,128]{2,1,0:T(8,128)(2,1)} %key_ref.1, bf16[8,256,128]{2,1,0:T(8,128)(2,1)} %value_ref.1, s32[3,8]{1,0:T(4,128)} %owner_ref.1, s32[3,8]{1,0:T(4,128)} %pick_ref.1), custom_call_target="tpu_custom_call" | custom-call | tf_op jit(solution)/shard_map/pallas_call | solution.py:45
  3.0 7.8 %all-to-all-start = ((bf16[32,9,16,128]{3,2,1,0:T(8,128)(2,1)}), bf16[32,9,16,128]{3,2,1,0:T(8,128)(2,1)S(1)}, u32[]{:S(2)}, u32[]{:S(2)}) async-start(bf16[32,9,16,128]{3,2,1,0:T(8,128)(2,1)} %shard_map.127), calls=%async_computation | async-start | bytes 2359296 | tf_op jit(solution)/shard_map/all_to_all | solution.py:380
  10.7 2.7 %shard_map.128 = (bf16[3,16,2304]{2,1,0:T(8,128)(2,1)}, bf16[3,16,2304]{2,1,0:T(8,128)(2,1)}, bf16[3,16,2304]{2,1,0:T(8,128)(2,1)}, bf16[3,16,2304]{2,1,0:T(8,12...) custom-call(s32[1]{0:T(128)} %bitcast.me_ref, ...), custom_call_target="tpu_custom_call" | custom-call | tf_op jit(solution)/shard_map/pallas_call | solution.py:94
  13.5 1.6 collective-permute-start
  15.1 0.0 collective-permute-start.1
  15.1 5.5 %collective-permute-done.refs_1_ = bf16[3,16,2304]{2,1,0:T(8,128)(2,1)S(1)} collective-permute-done((bf16[3,16,2304]{2,1,0:T(8,128)(2,1)}, bf16[3,16,2304]{2,1,0:T(8,128)(2,1)S(1)}, u32[]{:S(2)}, u32[]{:S(2)}) %collective-permute-start) | collective-permute-done | bytes 221216 | tf_op jit(solution)/shard_map/ppermute | solution.py:384
  20.6 0.7 copy-done.7
  21.3 2.3 %collective-permute-done.1.refs_7_ = bf16[3,16,2304]{2,1,0:T(8,128)(2,1)} collective-permute-done((bf16[3,16,2304]{2,1,0:T(8,128)(2,1)}, bf16[3,16,2304]{2,1,0:T(8,128)(2,1)}, u32[]{:S(2)}, u32[]{:S(2)}) %collective-permute-start.1) | collective-permute-done | bytes 221216 | tf_op jit(solution)/shard_map/ppermute | solution.py:384
  23.6 5.5 %all-to-all-done.in_ref = bf16[32,9,16,128]{3,2,1,0:T(8,128)(2,1)S(1)} async-done(((bf16[32,9,16,128]{3,2,1,0:T(8,128)(2,1)}), bf16[32,9,16,128]{3,2,1,0:T(8,128)(2,1)S(1)}, u32[]{:S(2)}, u32[]{:S(2)}) %all-to-all-start) | async-done | bytes 1179680 | tf_op jit(solution)/shard_map/all_to_all | solution.py:380
  29.1 1.8 shard_map.129
  30.9 1.7 copy-done.1
  32.6 4.8 %all-to-all-start.1 = ((bf16[32,24,16,128]{3,2,1,0:T(8,128)(2,1)}), bf16[32,24,16,128]{3,2,1,0:T(8,128)(2,1)}, u32[]{:S(2)}, u32[]{:S(2)}) async-start(bf16[32,24,16,128]{3,2,1,0:T(8,128)(2,1)} %copy-done.1), calls=%async_computation.1 | async-start | bytes 6291456 | tf_op jit(solution)/shard_map/all_to_all | solution.py:380
  37.4 4.3 %collective-permute-start.2 = (bf16[3,16,2304]{2,1,0:T(8,128)(2,1)S(1)}, bf16[3,16,2304]{2,1,0:T(8,128)(2,1)S(1)}, u32[]{:S(2)}, u32[]{:S(2)}) collective-permute-start(bf16[3,16,2304]{2,1,0:T(8,128)(2,1)S(1)} %copy-done.12), channel_id=1, source_target_pairs={{0,2},{1,3},{2,4},{3,5},{4,6},{5,7},{6,0},{7,1},{8,10},{9,11},{10,... | collective-permute-start | bytes 663560 | tf_op jit(solution)/shard_map/ppermute | solution.py:384
  41.7 0.0 collective-permute-start.3
  41.7 4.0 %collective-permute-start.4 = (bf16[3,16,2304]{2,1,0:T(8,128)(2,1)S(1)}, bf16[3,16,2304]{2,1,0:T(8,128)(2,1)S(1)}, u32[]{:S(2)}, u32[]{:S(2)}) collective-permute-start(bf16[3,16,2304]{2,1,0:T(8,128)(2,1)S(1)} %copy-done.10), channel_id=1, source_target_pairs={{0,3},{1,4},{2,5},{3,6},{4,7},{5,0},{6,1},{7,2},{8,11},{9,12},{10,... | collective-permute-start | bytes 663560 | tf_op jit(solution)/shard_map/ppermute | solution.py:384
  45.8 0.5 collective-permute-start.5
  46.3 3.2 %collective-permute-start.6 = (bf16[3,16,2304]{2,1,0:T(8,128)(2,1)S(1)}, bf16[3,16,2304]{2,1,0:T(8,128)(2,1)}, u32[]{:S(2)}, u32[]{:S(2)}) collective-permute-start(bf16[3,16,2304]{2,1,0:T(8,128)(2,1)S(1)} %copy-done.8), channel_id=1, source_target_pairs={{0,4},{1,5},{2,6},{3,7},{4,0},{5,1},{6,2},{7,3},{8,12},{9,13},{10,... | collective-permute-start | bytes 663560 | tf_op jit(solution)/shard_map/ppermute | solution.py:384
  49.5 8.8 %collective-permute-done.2.refs_2_ = bf16[3,16,2304]{2,1,0:T(8,128)(2,1)S(1)} collective-permute-done((bf16[3,16,2304]{2,1,0:T(8,128)(2,1)S(1)}, bf16[3,16,2304]{2,1,0:T(8,128)(2,1)S(1)}, u32[]{:S(2)}, u32[]{:S(2)}) %collective-permute-start.2) | collective-permute-done | bytes 221216 | tf_op jit(solution)/shard_map/ppermute | solution.py:384
  58.3 0.0 collective-permute-done.3.refs_6_
  58.3 10.2 %collective-permute-done.4.refs_3_ = bf16[3,16,2304]{2,1,0:T(8,128)(2,1)S(1)} collective-permute-done((bf16[3,16,2304]{2,1,0:T(8,128)(2,1)S(1)}, bf16[3,16,2304]{2,1,0:T(8,128)(2,1)S(1)}, u32[]{:S(2)}, u32[]{:S(2)}) %collective-permute-start.4) | collective-permute-done | bytes 221216 | tf_op jit(solution)/shard_map/ppermute | solution.py:384
  68.5 0.7 copy-done.15
  69.2 0.7 copy-done.16
  69.9 6.8 %collective-permute-done.6.refs_4_ = bf16[3,16,2304]{2,1,0:T(8,128)(2,1)} collective-permute-done((bf16[3,16,2304]{2,1,0:T(8,128)(2,1)S(1)}, bf16[3,16,2304]{2,1,0:T(8,128)(2,1)}, u32[]{:S(2)}, u32[]{:S(2)}) %collective-permute-start.6) | collective-permute-done | bytes 221216 | tf_op jit(solution)/shard_map/ppermute | solution.py:384
  76.7 0.7 all-to-all-done.1.kv_ref
  77.4 26.9 %shard_map.130 = (bf16[32,24,16,128]{3,2,1,0:T(8,128)(2,1)}, bf16[3,16,2304]{2,1,0:T(8,128)(2,1)}, bf16[3,16,2304]{2,1,0:T(8,128)(2,1)}, bf16[3,16,2304]{2,1,0:T...) custom-call(s32[1]{0:T(128)} %bitcast.me_ref, ...), custom_call_target="tpu_custom_call" | custom-call | flops 10267656192 | bytes 9830400 | tf_op jit(solution)/shard_map/pallas_call | solution.py:351
  104.3 7.4 %all-to-all-start.2 = ((bf16[32,24,16,128]{3,2,1,0:T(8,128)(2,1)}), bf16[32,24,16,128]{3,2,1,0:T(8,128)(2,1)S(1)}, u32[]{:S(2)}, u32[]{:S(2)}) async-start(bf16[32,24,16,128]{3,2,1,0:T(8,128)(2,1)} %get-tuple-element.66), calls=%async_computation.2 | async-start | bytes 6291456 | tf_op jit(solution)/shard_map/all_to_all | solution.py:380
  111.7 0.1 collective-permute-start.8
  111.8 3.6 %collective-permute-start.9 = (bf16[3,16,2304]{2,1,0:T(8,128)(2,1)}, bf16[3,16,2304]{2,1,0:T(8,128)(2,1)S(1)}, u32[]{:S(2)}, u32[]{:S(2)}) collective-permute-start(bf16[3,16,2304]{2,1,0:T(8,128)(2,1)} %get-tuple-element.68), channel_id=1, source_target_pairs={{0,2},{1,3},{2,4},{3,5},{4,6},{5,7},{6,0},{7,1},{8,10},{9,11},{10,... | collective-permute-start | bytes 663560 | tf_op jit(solution)/shard_map/ppermute | solution.py:384
  115.3 4.2 %collective-permute-start.10 = (bf16[3,16,2304]{2,1,0:T(8,128)(2,1)}, bf16[3,16,2304]{2,1,0:T(8,128)(2,1)S(1)}, u32[]{:S(2)}, u32[]{:S(2)}) collective-permute-start(bf16[3,16,2304]{2,1,0:T(8,128)(2,1)} %get-tuple-element.69), channel_id=1, source_target_pairs={{0,5},{1,6},{2,7},{3,0},{4,1},{5,2},{6,3},{7,4},{8,13},{9,14},{10,... | collective-permute-start | bytes 663560 | tf_op jit(solution)/shard_map/ppermute | solution.py:384
  119.6 0.3 collective-permute-start.11
  119.8 4.4 %collective-permute-start.12 = (bf16[3,16,2304]{2,1,0:T(8,128)(2,1)}, bf16[3,16,2304]{2,1,0:T(8,128)(2,1)}, u32[]{:S(2)}, u32[]{:S(2)}) collective-permute-start(bf16[3,16,2304]{2,1,0:T(8,128)(2,1)} %get-tuple-element.71), channel_id=1, source_target_pairs={{0,4},{1,5},{2,6},{3,7},{4,0},{5,1},{6,2},{7,3},{8,12},{9,13},{10,... | collective-permute-start | bytes 663560 | tf_op jit(solution)/shard_map/ppermute | solution.py:384
  124.2 0.0 collective-permute-done.8.refs_2_
  124.2 15.9 %collective-permute-done.10.refs_3_ = bf16[3,16,2304]{2,1,0:T(8,128)(2,1)S(1)} collective-permute-done((bf16[3,16,2304]{2,1,0:T(8,128)(2,1)}, bf16[3,16,2304]{2,1,0:T(8,128)(2,1)S(1)}, u32[]{:S(2)}, u32[]{:S(2)}) %collective-permute-start.10) | collective-permute-done | bytes 221216 | tf_op jit(solution)/shard_map/ppermute | solution.py:384
  140.1 2.4 %collective-permute-done.11.refs_5_ = bf16[3,16,2304]{2,1,0:T(8,128)(2,1)S(1)} collective-permute-done((bf16[3,16,2304]{2,1,0:T(8,128)(2,1)}, bf16[3,16,2304]{2,1,0:T(8,128)(2,1)S(1)}, u32[]{:S(2)}, u32[]{:S(2)}) %collective-permute-start.11) | collective-permute-done | bytes 221216 | tf_op jit(solution)/shard_map/ppermute | solution.py:384
  142.5 0.7 copy-done.5
  143.2 10.3 %collective-permute-done.12.refs_4_ = bf16[3,16,2304]{2,1,0:T(8,128)(2,1)} collective-permute-done((bf16[3,16,2304]{2,1,0:T(8,128)(2,1)}, bf16[3,16,2304]{2,1,0:T(8,128)(2,1)}, u32[]{:S(2)}, u32[]{:S(2)}) %collective-permute-start.12) | collective-permute-done | bytes 221216 | tf_op jit(solution)/shard_map/ppermute | solution.py:384
  153.5 0.0 all-to-all-done.2.in_ref
  153.5 2.3 %shard_map.132 = bf16[32,8,16,128]{3,2,1,0:T(8,128)(2,1)S(1)} custom-call(s32[32,128]{1,0:T(8,128)S(1)} %get-tuple-element.82.chosen_ref, bf16[32,24,16,128]{3,2,1,0:T(8,128)(2,1)S(1)} %all-to-all-done.2.in_ref), custom_call_target="tpu_custom_call" | custom-call | tf_op jit(solution)/shard_map/pallas_call | solution.py:212
  155.8 1.0 copy-done
  156.7 8.3 %all-to-all-start.3 = ((bf16[32,8,16,128]{3,2,1,0:T(8,128)(2,1)}), bf16[32,8,16,128]{3,2,1,0:T(8,128)(2,1)S(1)}, u32[]{:S(2)}, u32[]{:S(2)}) async-start(bf16[32,8,16,128]{3,2,1,0:T(8,128)(2,1)} %copy-done), calls=%async_computation.3 | async-start | bytes 2097152 | tf_op jit(solution)/shard_map/all_to_all | solution.py:380
  165.1 0.1 collective-permute-start.7
  165.2 1.5 collective-permute-start.13
  166.6 5.6 %collective-permute-done.7.refs_1_ = bf16[3,16,2304]{2,1,0:T(8,128)(2,1)S(1)} collective-permute-done((bf16[3,16,2304]{2,1,0:T(8,128)(2,1)}, bf16[3,16,2304]{2,1,0:T(8,128)(2,1)S(1)}, u32[]{:S(2)}, u32[]{:S(2)}) %collective-permute-start.7) | collective-permute-done | bytes 221216 | tf_op jit(solution)/shard_map/ppermute | solution.py:384
  172.3 0.1 collective-permute-done.13.refs_7_
  172.4 0.6 copy-done.6
  173.0 2.9 %shard_map.131 = (bf16[3,16,8192]{2,1,0:T(8,128)(2,1)}, bf16[3,16,8192]{2,1,0:T(8,128)(2,1)}, bf16[3,16,1024]{2,1,0:T(8,128)(2,1)}, bf16[3,16,1024]{2,1,0:T(8,128)(2,1)}) custom-call(s32[1]{0:T(128)} %bitcast.me_ref, bf16[3,16,2304]{2,1,0:T(8,128)(2,1)} %get-tuple-element.64.refs_0_, bf16[3,16,2304]{2,1,0:T(8,128)(2,1)} %copy-done.6, ...), custom_call_target="tpu_custom_call" | custom-call | tf_op jit(solution)/shard_map/pallas_call | solution.py:120
  175.8 6.2 %all-to-all-done.3.in_ref = bf16[32,8,16,128]{3,2,1,0:T(8,128)(2,1)S(1)} async-done(((bf16[32,8,16,128]{3,2,1,0:T(8,128)(2,1)}), bf16[32,8,16,128]{3,2,1,0:T(8,128)(2,1)S(1)}, u32[]{:S(2)}, u32[]{:S(2)}) %all-to-all-start.3) | async-done | bytes 1048608 | tf_op jit(solution)/shard_map/all_to_all | solution.py:380
  182.0 1.1 shard_map.133
  (29 shorter events, 0.1 us)
Async XLA Ops:
  3.0 26.1 %all-to-all-start = ((bf16[32,9,16,128]{3,2,1,0:T(8,128)(2,1)}), bf16[32,9,16,128]{3,2,1,0:T(8,128)(2,1)S(1)}, u32[]{:S(2)}, u32[]{:S(2)}) async-start(bf16[32,9,16,128]{3,2,1,0:T(8,128)(2,1)} %shard_map.127), calls=%async_computation | async-start | bytes 2359296 | tf_op jit(solution)/shard_map/all_to_all | solution.py:380
  13.5 7.1 %collective-permute-start = (bf16[3,16,2304]{2,1,0:T(8,128)(2,1)}, bf16[3,16,2304]{2,1,0:T(8,128)(2,1)S(1)}, u32[]{:S(2)}, u32[]{:S(2)}) collective-permute-start(bf16[3,16,2304]{2,1,0:T(8,128)(2,1)} %get-tuple-element.46), channel_id=1, source_target_pairs={{0,1},{1,2},{2,3},{3,4},{4,5},{5,6},{6,7},{7,0},{8,9},{9,10},{10,1... | collective-permute-start | bytes 663560 | tf_op jit(solution)/shard_map/ppermute | solution.py:384
  15.1 8.5 %collective-permute-start.1 = (bf16[3,16,2304]{2,1,0:T(8,128)(2,1)}, bf16[3,16,2304]{2,1,0:T(8,128)(2,1)}, u32[]{:S(2)}, u32[]{:S(2)}) collective-permute-start(bf16[3,16,2304]{2,1,0:T(8,128)(2,1)} %get-tuple-element.47), channel_id=1, source_target_pairs={{0,7},{1,0},{2,1},{3,2},{4,3},{5,4},{6,5},{7,6},{8,15},{9,8},{10,9... | collective-permute-start | bytes 663560 | tf_op jit(solution)/shard_map/ppermute | solution.py:384
  20.6 0.7 copy-start.7
  30.9 1.7 copy-start.1
  32.6 4.8 %copy-start.12 = (bf16[3,16,2304]{2,1,0:T(8,128)(2,1)S(1)}, bf16[3,16,2304]{2,1,0:T(8,128)(2,1)}, u32[]{:S(2)}) copy-start(bf16[3,16,2304]{2,1,0:T(8,128)(2,1)} %get-tuple-element.50) | copy-start | bytes 663556
  32.6 9.1 %copy-start.11 = (bf16[3,16,2304]{2,1,0:T(8,128)(2,1)S(1)}, bf16[3,16,2304]{2,1,0:T(8,128)(2,1)}, u32[]{:S(2)}) copy-start(bf16[3,16,2304]{2,1,0:T(8,128)(2,1)} %get-tuple-element.51) | copy-start | bytes 663556
  32.6 9.1 %copy-start.10 = (bf16[3,16,2304]{2,1,0:T(8,128)(2,1)S(1)}, bf16[3,16,2304]{2,1,0:T(8,128)(2,1)}, u32[]{:S(2)}) copy-start(bf16[3,16,2304]{2,1,0:T(8,128)(2,1)} %get-tuple-element.52) | copy-start | bytes 663556
  32.6 13.1 %copy-start.9 = (bf16[3,16,2304]{2,1,0:T(8,128)(2,1)S(1)}, bf16[3,16,2304]{2,1,0:T(8,128)(2,1)}, u32[]{:S(2)}) copy-start(bf16[3,16,2304]{2,1,0:T(8,128)(2,1)} %get-tuple-element.53) | copy-start | bytes 663556
  32.6 13.7 %copy-start.8 = (bf16[3,16,2304]{2,1,0:T(8,128)(2,1)S(1)}, bf16[3,16,2304]{2,1,0:T(8,128)(2,1)}, u32[]{:S(2)}) copy-start(bf16[3,16,2304]{2,1,0:T(8,128)(2,1)} %get-tuple-element.54) | copy-start | bytes 663556
  32.6 44.7 %all-to-all-start.1 = ((bf16[32,24,16,128]{3,2,1,0:T(8,128)(2,1)}), bf16[32,24,16,128]{3,2,1,0:T(8,128)(2,1)}, u32[]{:S(2)}, u32[]{:S(2)}) async-start(bf16[32,24,16,128]{3,2,1,0:T(8,128)(2,1)} %copy-done.1), calls=%async_computation.1 | async-start | bytes 6291456 | tf_op jit(solution)/shard_map/all_to_all | solution.py:380
  37.4 20.9 %collective-permute-start.2 = (bf16[3,16,2304]{2,1,0:T(8,128)(2,1)S(1)}, bf16[3,16,2304]{2,1,0:T(8,128)(2,1)S(1)}, u32[]{:S(2)}, u32[]{:S(2)}) collective-permute-start(bf16[3,16,2304]{2,1,0:T(8,128)(2,1)S(1)} %copy-done.12), channel_id=1, source_target_pairs={{0,2},{1,3},{2,4},{3,5},{4,6},{5,7},{6,0},{7,1},{8,10},{9,11},{10,... | collective-permute-start | bytes 663560 | tf_op jit(solution)/shard_map/ppermute | solution.py:384
  41.7 16.6 %collective-permute-start.3 = (bf16[3,16,2304]{2,1,0:T(8,128)(2,1)S(1)}, bf16[3,16,2304]{2,1,0:T(8,128)(2,1)S(1)}, u32[]{:S(2)}, u32[]{:S(2)}) collective-permute-start(bf16[3,16,2304]{2,1,0:T(8,128)(2,1)S(1)} %copy-done.11), channel_id=1, source_target_pairs={{0,6},{1,7},{2,0},{3,1},{4,2},{5,3},{6,4},{7,5},{8,14},{9,15},{10,... | collective-permute-start | bytes 663560 | tf_op jit(solution)/shard_map/ppermute | solution.py:384
  41.7 26.8 %collective-permute-start.4 = (bf16[3,16,2304]{2,1,0:T(8,128)(2,1)S(1)}, bf16[3,16,2304]{2,1,0:T(8,128)(2,1)S(1)}, u32[]{:S(2)}, u32[]{:S(2)}) collective-permute-start(bf16[3,16,2304]{2,1,0:T(8,128)(2,1)S(1)} %copy-done.10), channel_id=1, source_target_pairs={{0,3},{1,4},{2,5},{3,6},{4,7},{5,0},{6,1},{7,2},{8,11},{9,12},{10,... | collective-permute-start | bytes 663560 | tf_op jit(solution)/shard_map/ppermute | solution.py:384
  45.8 22.7 %collective-permute-start.5 = (bf16[3,16,2304]{2,1,0:T(8,128)(2,1)S(1)}, bf16[3,16,2304]{2,1,0:T(8,128)(2,1)S(1)}, u32[]{:S(2)}, u32[]{:S(2)}) collective-permute-start(bf16[3,16,2304]{2,1,0:T(8,128)(2,1)S(1)} %copy-done.9), channel_id=1, source_target_pairs={{0,5},{1,6},{2,7},{3,0},{4,1},{5,2},{6,3},{7,4},{8,13},{9,14},{10,... | collective-permute-start | bytes 663560 | tf_op jit(solution)/shard_map/ppermute | solution.py:384
  46.3 30.4 %collective-permute-start.6 = (bf16[3,16,2304]{2,1,0:T(8,128)(2,1)S(1)}, bf16[3,16,2304]{2,1,0:T(8,128)(2,1)}, u32[]{:S(2)}, u32[]{:S(2)}) collective-permute-start(bf16[3,16,2304]{2,1,0:T(8,128)(2,1)S(1)} %copy-done.8), channel_id=1, source_target_pairs={{0,4},{1,5},{2,6},{3,7},{4,0},{5,1},{6,2},{7,3},{8,12},{9,13},{10,... | collective-permute-start | bytes 663560 | tf_op jit(solution)/shard_map/ppermute | solution.py:384
  58.3 10.2 %copy-start.13 = (bf16[3,16,2304]{2,1,0:T(8,128)(2,1)}, bf16[3,16,2304]{2,1,0:T(8,128)(2,1)S(1)}, u32[]{:S(2)}) copy-start(bf16[3,16,2304]{2,1,0:T(8,128)(2,1)S(1)} %collective-permute-done.2.refs_2_) | copy-start | bytes 663556
  58.3 10.2 %copy-start.14 = (bf16[3,16,2304]{2,1,0:T(8,128)(2,1)}, bf16[3,16,2304]{2,1,0:T(8,128)(2,1)S(1)}, u32[]{:S(2)}) copy-start(bf16[3,16,2304]{2,1,0:T(8,128)(2,1)S(1)} %collective-permute-done.3.refs_6_) | copy-start | bytes 663556
  68.5 0.7 copy-start.15
  69.2 0.7 copy-start.16
  104.3 49.2 %all-to-all-start.2 = ((bf16[32,24,16,128]{3,2,1,0:T(8,128)(2,1)}), bf16[32,24,16,128]{3,2,1,0:T(8,128)(2,1)S(1)}, u32[]{:S(2)}, u32[]{:S(2)}) async-start(bf16[32,24,16,128]{3,2,1,0:T(8,128)(2,1)} %get-tuple-element.66), calls=%async_computation.2 | async-start | bytes 6291456 | tf_op jit(solution)/shard_map/all_to_all | solution.py:380
  111.7 12.5 %collective-permute-start.8 = (bf16[3,16,2304]{2,1,0:T(8,128)(2,1)}, bf16[3,16,2304]{2,1,0:T(8,128)(2,1)S(1)}, u32[]{:S(2)}, u32[]{:S(2)}) collective-permute-start(bf16[3,16,2304]{2,1,0:T(8,128)(2,1)} %get-tuple-element.67), channel_id=1, source_target_pairs={{0,6},{1,7},{2,0},{3,1},{4,2},{5,3},{6,4},{7,5},{8,14},{9,15},{10,... | collective-permute-start | bytes 663560 | tf_op jit(solution)/shard_map/ppermute | solution.py:384
  111.8 12.4 %collective-permute-start.9 = (bf16[3,16,2304]{2,1,0:T(8,128)(2,1)}, bf16[3,16,2304]{2,1,0:T(8,128)(2,1)S(1)}, u32[]{:S(2)}, u32[]{:S(2)}) collective-permute-start(bf16[3,16,2304]{2,1,0:T(8,128)(2,1)} %get-tuple-element.68), channel_id=1, source_target_pairs={{0,2},{1,3},{2,4},{3,5},{4,6},{5,7},{6,0},{7,1},{8,10},{9,11},{10,... | collective-permute-start | bytes 663560 | tf_op jit(solution)/shard_map/ppermute | solution.py:384
  115.3 24.8 %collective-permute-start.10 = (bf16[3,16,2304]{2,1,0:T(8,128)(2,1)}, bf16[3,16,2304]{2,1,0:T(8,128)(2,1)S(1)}, u32[]{:S(2)}, u32[]{:S(2)}) collective-permute-start(bf16[3,16,2304]{2,1,0:T(8,128)(2,1)} %get-tuple-element.69), channel_id=1, source_target_pairs={{0,5},{1,6},{2,7},{3,0},{4,1},{5,2},{6,3},{7,4},{8,13},{9,14},{10,... | collective-permute-start | bytes 663560 | tf_op jit(solution)/shard_map/ppermute | solution.py:384
  119.6 23.0 %collective-permute-start.11 = (bf16[3,16,2304]{2,1,0:T(8,128)(2,1)}, bf16[3,16,2304]{2,1,0:T(8,128)(2,1)S(1)}, u32[]{:S(2)}, u32[]{:S(2)}) collective-permute-start(bf16[3,16,2304]{2,1,0:T(8,128)(2,1)} %get-tuple-element.70), channel_id=1, source_target_pairs={{0,3},{1,4},{2,5},{3,6},{4,7},{5,0},{6,1},{7,2},{8,11},{9,12},{10,... | collective-permute-start | bytes 663560 | tf_op jit(solution)/shard_map/ppermute | solution.py:384
  119.8 33.7 %collective-permute-start.12 = (bf16[3,16,2304]{2,1,0:T(8,128)(2,1)}, bf16[3,16,2304]{2,1,0:T(8,128)(2,1)}, u32[]{:S(2)}, u32[]{:S(2)}) collective-permute-start(bf16[3,16,2304]{2,1,0:T(8,128)(2,1)} %get-tuple-element.71), channel_id=1, source_target_pairs={{0,4},{1,5},{2,6},{3,7},{4,0},{5,1},{6,2},{7,3},{8,12},{9,13},{10,... | collective-permute-start | bytes 663560 | tf_op jit(solution)/shard_map/ppermute | solution.py:384
  124.2 32.6 %copy-start.2 = (bf16[3,16,2304]{2,1,0:T(8,128)(2,1)}, bf16[3,16,2304]{2,1,0:T(8,128)(2,1)S(1)}, u32[]{:S(2)}) copy-start(bf16[3,16,2304]{2,1,0:T(8,128)(2,1)S(1)} %collective-permute-done.8.refs_2_) | copy-start | bytes 663556
  124.2 18.3 %copy-start.3 = (bf16[3,16,2304]{2,1,0:T(8,128)(2,1)}, bf16[3,16,2304]{2,1,0:T(8,128)(2,1)S(1)}, u32[]{:S(2)}) copy-start(bf16[3,16,2304]{2,1,0:T(8,128)(2,1)S(1)} %collective-permute-done.9.refs_6_) | copy-start | bytes 663556
  140.1 2.4 %copy-start.4 = (bf16[3,16,2304]{2,1,0:T(8,128)(2,1)}, bf16[3,16,2304]{2,1,0:T(8,128)(2,1)S(1)}, u32[]{:S(2)}) copy-start(bf16[3,16,2304]{2,1,0:T(8,128)(2,1)S(1)} %collective-permute-done.10.refs_3_) | copy-start | bytes 663556
  142.5 0.7 copy-start.5
  155.8 1.0 copy-start
  156.7 25.3 %all-to-all-start.3 = ((bf16[32,8,16,128]{3,2,1,0:T(8,128)(2,1)}), bf16[32,8,16,128]{3,2,1,0:T(8,128)(2,1)S(1)}, u32[]{:S(2)}, u32[]{:S(2)}) async-start(bf16[32,8,16,128]{3,2,1,0:T(8,128)(2,1)} %copy-done), calls=%async_computation.3 | async-start | bytes 2097152 | tf_op jit(solution)/shard_map/all_to_all | solution.py:380
  165.1 7.2 %collective-permute-start.7 = (bf16[3,16,2304]{2,1,0:T(8,128)(2,1)}, bf16[3,16,2304]{2,1,0:T(8,128)(2,1)S(1)}, u32[]{:S(2)}, u32[]{:S(2)}) collective-permute-start(bf16[3,16,2304]{2,1,0:T(8,128)(2,1)} %get-tuple-element.65), channel_id=1, source_target_pairs={{0,7},{1,0},{2,1},{3,2},{4,3},{5,4},{6,5},{7,6},{8,15},{9,8},{10,9... | collective-permute-start | bytes 663560 | tf_op jit(solution)/shard_map/ppermute | solution.py:384
  165.2 7.2 %collective-permute-start.13 = (bf16[3,16,2304]{2,1,0:T(8,128)(2,1)}, bf16[3,16,2304]{2,1,0:T(8,128)(2,1)}, u32[]{:S(2)}, u32[]{:S(2)}) collective-permute-start(bf16[3,16,2304]{2,1,0:T(8,128)(2,1)} %get-tuple-element.77), channel_id=1, source_target_pairs={{0,1},{1,2},{2,3},{3,4},{4,5},{5,6},{6,7},{7,0},{8,9},{9,10},{10,1... | collective-permute-start | bytes 663560 | tf_op jit(solution)/shard_map/ppermute | solution.py:384
  172.3 0.7 copy-start.6

commit v4 on v3

--- a/solution.py
+++ b/solution.py
@@ -173,7 +173,7 @@
             pltpu.SMEM(table_shape, jnp.int32),
             pltpu.SemaphoreType.DMA,
         ],
-        compiler_params=params(33554432),
+        compiler_params=params(4000000),
     )(slices)
 
 
@@ -219,7 +219,7 @@
         ],
         out_specs=pl.BlockSpec(out_shape, lambda i: (0, 0, 0, 0)),
         scratch_shapes=[pltpu.VMEM((peers * kept, rows, head_dim), jnp.float32)],
-        compiler_params=params(33554432),
+        compiler_params=params(4000000),
     )(table, pairs)
 
 

time: 184 us -> 188 us (1.022)
  Pallas kernels: 40 us -> 44.2 us
    pallas_call x1, Pallas kernels: 1.83 us -> 4.31 us  [gather_pairs(): pl.pallas_call(kernel, out_shape=(jax.ShapeDtypeStruct((peers, pairs, row...]
    unnamed x34 -> x32, local copies, waits for them, and re-layouts: 6.06 us -> 5.49 us
where the time goes in v4:
time: 188 us; the launch traced here: 187 us
  waiting for transfers between devices  80.9 us (43%)
  starting transfers between devices  56 us (30%)
  Pallas kernels  44.2 us (24%)
  local copies, waits for them, and re-layouts  5.49 us (3%)
    ppermute x14, waiting for transfers between devices, send(): lax.ppermute(x, 'heads', [(i, (i + distance) % peers) for i in range(peer...  67.9 us
    all_to_all x4, starting transfers between devices, exchange(): return lax.all_to_all(x, 'docs', split_axis=0, concat_axis=0, tiled=True)  28.3 us
    ppermute x14, starting transfers between devices, send(): lax.ppermute(x, 'heads', [(i, (i + distance) % peers) for i in range(peer...  27.7 us
    pallas_call x1, Pallas kernels, attend(): pl.pallas_call(functools.partial(attend_kernel, peers, rows, group, head_...  27 us
    all_to_all x4, waiting for transfers between devices, exchange(): return lax.all_to_all(x, 'docs', split_axis=0, concat_axis=0, tiled=True)  12.9 us
    unnamed x32, local copies, waits for them, and re-layouts  5.49 us
    pallas_call x1, Pallas kernels, gather_pairs(): pl.pallas_call(kernel, out_shape=(jax.ShapeDtypeStruct((peers, pairs, row...  4.31 us
    pallas_call x1, Pallas kernels, sum_pairs(): pl.pallas_call(kernel, out_shape=jax.ShapeDtypeStruct(out_shape, jnp.bflo...  3.89 us
  transfers between devices with their start and end apart: 18, of which 13 were waited for; matrix products, arithmetic and copies ran while one was open for 0% of the time, Pallas kernels for 3%

profile of v4, /device:TPU:65, one launch (start us, length us, event | category | flops | bytes accessed | tf_op | source)
XLA Modules:
  0.0 187.3 jit_solution(1923035893585771477)
XLA Ops:
  0.6 2.3 %shard_map.127 = bf16[32,9,16,128]{3,2,1,0:T(8,128)(2,1)} custom-call(bf16[8,256,128]{2,1,0:T(8,128)(2,1)} %key_ref.1, bf16[8,256,128]{2,1,0:T(8,128)(2,1)} %value_ref.1, s32[3,8]{1,0:T(4,128)} %owner_ref.1, s32[3,8]{1,0:T(4,128)} %pick_ref.1), custom_call_target="tpu_custom_call" | custom-call | tf_op jit(solution)/shard_map/pallas_call | solution.py:45
  3.0 7.8 %all-to-all-start = ((bf16[32,9,16,128]{3,2,1,0:T(8,128)(2,1)}), bf16[32,9,16,128]{3,2,1,0:T(8,128)(2,1)S(1)}, u32[]{:S(2)}, u32[]{:S(2)}) async-start(bf16[32,9,16,128]{3,2,1,0:T(8,128)(2,1)} %shard_map.127), calls=%async_computation | async-start | bytes 2359296 | tf_op jit(solution)/shard_map/all_to_all | solution.py:380
  10.7 2.7 %shard_map.128 = (bf16[3,16,2304]{2,1,0:T(8,128)(2,1)}, bf16[3,16,2304]{2,1,0:T(8,128)(2,1)}, bf16[3,16,2304]{2,1,0:T(8,128)(2,1)}, bf16[3,16,2304]{2,1,0:T(8,12...) custom-call(s32[1]{0:T(128)} %bitcast.me_ref, ...), custom_call_target="tpu_custom_call" | custom-call | tf_op jit(solution)/shard_map/pallas_call | solution.py:94
  13.5 1.6 collective-permute-start
  15.1 0.0 collective-permute-start.1
  15.1 5.5 %collective-permute-done.refs_1_ = bf16[3,16,2304]{2,1,0:T(8,128)(2,1)S(1)} collective-permute-done((bf16[3,16,2304]{2,1,0:T(8,128)(2,1)}, bf16[3,16,2304]{2,1,0:T(8,128)(2,1)S(1)}, u32[]{:S(2)}, u32[]{:S(2)}) %collective-permute-start) | collective-permute-done | bytes 221216 | tf_op jit(solution)/shard_map/ppermute | solution.py:384
  20.6 0.7 copy-done.6
  21.3 2.3 %collective-permute-done.1.refs_7_ = bf16[3,16,2304]{2,1,0:T(8,128)(2,1)} collective-permute-done((bf16[3,16,2304]{2,1,0:T(8,128)(2,1)}, bf16[3,16,2304]{2,1,0:T(8,128)(2,1)}, u32[]{:S(2)}, u32[]{:S(2)}) %collective-permute-start.1) | collective-permute-done | bytes 221216 | tf_op jit(solution)/shard_map/ppermute | solution.py:384
  23.6 5.5 %all-to-all-done.in_ref = bf16[32,9,16,128]{3,2,1,0:T(8,128)(2,1)S(1)} async-done(((bf16[32,9,16,128]{3,2,1,0:T(8,128)(2,1)}), bf16[32,9,16,128]{3,2,1,0:T(8,128)(2,1)S(1)}, u32[]{:S(2)}, u32[]{:S(2)}) %all-to-all-start) | async-done | bytes 1179680 | tf_op jit(solution)/shard_map/all_to_all | solution.py:380
  29.1 1.0 copy-done.1
  30.1 4.3 %shard_map.129 = (bf16[32,24,16,128]{3,2,1,0:T(8,128)(2,1)}, s32[32,128]{1,0:T(8,128)}) custom-call(bf16[32,9,16,128]{3,2,1,0:T(8,128)(2,1)} %copy-done.1), custom_call_target="tpu_custom_call" | custom-call | tf_op jit(solution)/shard_map/pallas_call | solution.py:160
  34.5 0.0 copy-start.11
  34.5 0.0 copy-start.9
  34.5 4.8 %all-to-all-start.1 = ((bf16[32,24,16,128]{3,2,1,0:T(8,128)(2,1)}), bf16[32,24,16,128]{3,2,1,0:T(8,128)(2,1)}, u32[]{:S(2)}, u32[]{:S(2)}) async-start(bf16[32,24,16,128]{3,2,1,0:T(8,128)(2,1)} %get-tuple-element.49), calls=%async_computation.1 | async-start | bytes 6291456 | tf_op jit(solution)/shard_map/all_to_all | solution.py:380
  39.3 4.3 %collective-permute-start.2 = (bf16[3,16,2304]{2,1,0:T(8,128)(2,1)S(1)}, bf16[3,16,2304]{2,1,0:T(8,128)(2,1)S(1)}, u32[]{:S(2)}, u32[]{:S(2)}) collective-permute-start(bf16[3,16,2304]{2,1,0:T(8,128)(2,1)S(1)} %copy-done.11), channel_id=1, source_target_pairs={{0,2},{1,3},{2,4},{3,5},{4,6},{5,7},{6,0},{7,1},{8,10},{9,11},{10,... | collective-permute-start | bytes 663560 | tf_op jit(solution)/shard_map/ppermute | solution.py:384
  43.6 4.0 %collective-permute-start.4 = (bf16[3,16,2304]{2,1,0:T(8,128)(2,1)S(1)}, bf16[3,16,2304]{2,1,0:T(8,128)(2,1)S(1)}, u32[]{:S(2)}, u32[]{:S(2)}) collective-permute-start(bf16[3,16,2304]{2,1,0:T(8,128)(2,1)S(1)} %copy-done.9), channel_id=1, source_target_pairs={{0,3},{1,4},{2,5},{3,6},{4,7},{5,0},{6,1},{7,2},{8,11},{9,12},{10,... | collective-permute-start | bytes 663560 | tf_op jit(solution)/shard_map/ppermute | solution.py:384
  47.7 0.5 collective-permute-start.5
  48.2 3.2 %collective-permute-start.6 = (bf16[3,16,2304]{2,1,0:T(8,128)(2,1)S(1)}, bf16[3,16,2304]{2,1,0:T(8,128)(2,1)}, u32[]{:S(2)}, u32[]{:S(2)}) collective-permute-start(bf16[3,16,2304]{2,1,0:T(8,128)(2,1)S(1)} %copy-done.7), channel_id=1, source_target_pairs={{0,4},{1,5},{2,6},{3,7},{4,0},{5,1},{6,2},{7,3},{8,12},{9,13},{10,... | collective-permute-start | bytes 663560 | tf_op jit(solution)/shard_map/ppermute | solution.py:384
  51.4 8.8 %collective-permute-done.2.refs_2_ = bf16[3,16,2304]{2,1,0:T(8,128)(2,1)S(1)} collective-permute-done((bf16[3,16,2304]{2,1,0:T(8,128)(2,1)S(1)}, bf16[3,16,2304]{2,1,0:T(8,128)(2,1)S(1)}, u32[]{:S(2)}, u32[]{:S(2)}) %collective-permute-start.2) | collective-permute-done | bytes 221216 | tf_op jit(solution)/shard_map/ppermute | solution.py:384
  60.2 0.0 collective-permute-done.3.refs_6_
  60.2 10.2 %collective-permute-done.4.refs_3_ = bf16[3,16,2304]{2,1,0:T(8,128)(2,1)S(1)} collective-permute-done((bf16[3,16,2304]{2,1,0:T(8,128)(2,1)S(1)}, bf16[3,16,2304]{2,1,0:T(8,128)(2,1)S(1)}, u32[]{:S(2)}, u32[]{:S(2)}) %collective-permute-start.4) | collective-permute-done | bytes 221216 | tf_op jit(solution)/shard_map/ppermute | solution.py:384
  70.4 0.0 collective-permute-done.5.refs_5_
  70.4 0.7 copy-done.14
  71.1 0.7 copy-done.15
  71.8 6.8 %collective-permute-done.6.refs_4_ = bf16[3,16,2304]{2,1,0:T(8,128)(2,1)} collective-permute-done((bf16[3,16,2304]{2,1,0:T(8,128)(2,1)S(1)}, bf16[3,16,2304]{2,1,0:T(8,128)(2,1)}, u32[]{:S(2)}, u32[]{:S(2)}) %collective-permute-start.6) | collective-permute-done | bytes 221216 | tf_op jit(solution)/shard_map/ppermute | solution.py:384
  78.6 0.7 all-to-all-done.1.kv_ref
  79.3 27.0 %shard_map.130 = (bf16[32,24,16,128]{3,2,1,0:T(8,128)(2,1)}, bf16[3,16,2304]{2,1,0:T(8,128)(2,1)}, bf16[3,16,2304]{2,1,0:T(8,128)(2,1)}, bf16[3,16,2304]{2,1,0:T...) custom-call(s32[1]{0:T(128)} %bitcast.me_ref, ...), custom_call_target="tpu_custom_call" | custom-call | flops 10267656192 | bytes 9830400 | tf_op jit(solution)/shard_map/pallas_call | solution.py:351
  106.2 7.4 %all-to-all-start.2 = ((bf16[32,24,16,128]{3,2,1,0:T(8,128)(2,1)}), bf16[32,24,16,128]{3,2,1,0:T(8,128)(2,1)S(1)}, u32[]{:S(2)}, u32[]{:S(2)}) async-start(bf16[32,24,16,128]{3,2,1,0:T(8,128)(2,1)} %get-tuple-element.66), calls=%async_computation.2 | async-start | bytes 6291456 | tf_op jit(solution)/shard_map/all_to_all | solution.py:380
  113.6 0.1 collective-permute-start.8
  113.7 3.6 %collective-permute-start.9 = (bf16[3,16,2304]{2,1,0:T(8,128)(2,1)}, bf16[3,16,2304]{2,1,0:T(8,128)(2,1)S(1)}, u32[]{:S(2)}, u32[]{:S(2)}) collective-permute-start(bf16[3,16,2304]{2,1,0:T(8,128)(2,1)} %get-tuple-element.68), channel_id=1, source_target_pairs={{0,2},{1,3},{2,4},{3,5},{4,6},{5,7},{6,0},{7,1},{8,10},{9,11},{10,... | collective-permute-start | bytes 663560 | tf_op jit(solution)/shard_map/ppermute | solution.py:384
  117.3 4.2 %collective-permute-start.10 = (bf16[3,16,2304]{2,1,0:T(8,128)(2,1)}, bf16[3,16,2304]{2,1,0:T(8,128)(2,1)S(1)}, u32[]{:S(2)}, u32[]{:S(2)}) collective-permute-start(bf16[3,16,2304]{2,1,0:T(8,128)(2,1)} %get-tuple-element.69), channel_id=1, source_target_pairs={{0,5},{1,6},{2,7},{3,0},{4,1},{5,2},{6,3},{7,4},{8,13},{9,14},{10,... | collective-permute-start | bytes 663560 | tf_op jit(solution)/shard_map/ppermute | solution.py:384
  121.5 0.3 collective-permute-start.11
  121.7 4.4 %collective-permute-start.12 = (bf16[3,16,2304]{2,1,0:T(8,128)(2,1)}, bf16[3,16,2304]{2,1,0:T(8,128)(2,1)}, u32[]{:S(2)}, u32[]{:S(2)}) collective-permute-start(bf16[3,16,2304]{2,1,0:T(8,128)(2,1)} %get-tuple-element.71), channel_id=1, source_target_pairs={{0,4},{1,5},{2,6},{3,7},{4,0},{5,1},{6,2},{7,3},{8,12},{9,13},{10,... | collective-permute-start | bytes 663560 | tf_op jit(solution)/shard_map/ppermute | solution.py:384
  126.1 0.0 collective-permute-done.9.refs_6_
  126.1 16.0 %collective-permute-done.10.refs_3_ = bf16[3,16,2304]{2,1,0:T(8,128)(2,1)S(1)} collective-permute-done((bf16[3,16,2304]{2,1,0:T(8,128)(2,1)}, bf16[3,16,2304]{2,1,0:T(8,128)(2,1)S(1)}, u32[]{:S(2)}, u32[]{:S(2)}) %collective-permute-start.10) | collective-permute-done | bytes 221216 | tf_op jit(solution)/shard_map/ppermute | solution.py:384
  142.1 2.3 %collective-permute-done.11.refs_5_ = bf16[3,16,2304]{2,1,0:T(8,128)(2,1)S(1)} collective-permute-done((bf16[3,16,2304]{2,1,0:T(8,128)(2,1)}, bf16[3,16,2304]{2,1,0:T(8,128)(2,1)S(1)}, u32[]{:S(2)}, u32[]{:S(2)}) %collective-permute-start.11) | collective-permute-done | bytes 221216 | tf_op jit(solution)/shard_map/ppermute | solution.py:384
  144.4 0.7 copy-done.5
  145.1 10.3 %collective-permute-done.12.refs_4_ = bf16[3,16,2304]{2,1,0:T(8,128)(2,1)} collective-permute-done((bf16[3,16,2304]{2,1,0:T(8,128)(2,1)}, bf16[3,16,2304]{2,1,0:T(8,128)(2,1)}, u32[]{:S(2)}, u32[]{:S(2)}) %collective-permute-start.12) | collective-permute-done | bytes 221216 | tf_op jit(solution)/shard_map/ppermute | solution.py:384
  155.4 1.6 copy-done
  157.1 3.9 %shard_map.132 = bf16[32,8,16,128]{3,2,1,0:T(8,128)(2,1)} custom-call(s32[32,128]{1,0:T(8,128)} %get-tuple-element.82.chosen_ref, bf16[32,24,16,128]{3,2,1,0:T(8,128)(2,1)} %copy-done), custom_call_target="tpu_custom_call" | custom-call | tf_op jit(solution)/shard_map/pallas_call | solution.py:212
  161.0 8.3 %all-to-all-start.3 = ((bf16[32,8,16,128]{3,2,1,0:T(8,128)(2,1)}), bf16[32,8,16,128]{3,2,1,0:T(8,128)(2,1)S(1)}, u32[]{:S(2)}, u32[]{:S(2)}) async-start(bf16[32,8,16,128]{3,2,1,0:T(8,128)(2,1)} %shard_map.132), calls=%async_computation.3 | async-start | bytes 2097152 | tf_op jit(solution)/shard_map/all_to_all | solution.py:380
  169.3 0.1 collective-permute-start.7
  169.4 1.5 collective-permute-start.13
  170.9 5.6 %collective-permute-done.7.refs_1_ = bf16[3,16,2304]{2,1,0:T(8,128)(2,1)} collective-permute-done((bf16[3,16,2304]{2,1,0:T(8,128)(2,1)}, bf16[3,16,2304]{2,1,0:T(8,128)(2,1)}, u32[]{:S(2)}, u32[]{:S(2)}) %collective-permute-start.7) | collective-permute-done | bytes 221216 | tf_op jit(solution)/shard_map/ppermute | solution.py:384
  176.5 0.1 collective-permute-done.13.refs_7_
  176.6 2.9 %shard_map.131 = (bf16[3,16,8192]{2,1,0:T(8,128)(2,1)}, bf16[3,16,8192]{2,1,0:T(8,128)(2,1)}, bf16[3,16,1024]{2,1,0:T(8,128)(2,1)}, bf16[3,16,1024]{2,1,0:T(8,128)(2,1)}) custom-call(s32[1]{0:T(128)} %bitcast.me_ref, bf16[3,16,2304]{2,1,0:T(8,128)(2,1)} %get-tuple-element.64.refs_0_, bf16[3,16,2304]{2,1,0:T(8,128)(2,1)} %collective-permute-done.7.refs_1_, ...), custom_call_target="tpu_custom_call" | custom-call | tf_op jit(solution)/shard_map/pallas_call | solution.py:120
  179.5 6.8 %all-to-all-done.3.in_ref = bf16[32,8,16,128]{3,2,1,0:T(8,128)(2,1)S(1)} async-done(((bf16[32,8,16,128]{3,2,1,0:T(8,128)(2,1)}), bf16[32,8,16,128]{3,2,1,0:T(8,128)(2,1)S(1)}, u32[]{:S(2)}, u32[]{:S(2)}) %all-to-all-start.3) | async-done | bytes 1048608 | tf_op jit(solution)/shard_map/all_to_all | solution.py:380
  186.2 1.1 shard_map.133
  (27 shorter events, 0.1 us)
Async XLA Ops:
  3.0 26.1 %all-to-all-start = ((bf16[32,9,16,128]{3,2,1,0:T(8,128)(2,1)}), bf16[32,9,16,128]{3,2,1,0:T(8,128)(2,1)S(1)}, u32[]{:S(2)}, u32[]{:S(2)}) async-start(bf16[32,9,16,128]{3,2,1,0:T(8,128)(2,1)} %shard_map.127), calls=%async_computation | async-start | bytes 2359296 | tf_op jit(solution)/shard_map/all_to_all | solution.py:380
  13.5 7.1 %collective-permute-start = (bf16[3,16,2304]{2,1,0:T(8,128)(2,1)}, bf16[3,16,2304]{2,1,0:T(8,128)(2,1)S(1)}, u32[]{:S(2)}, u32[]{:S(2)}) collective-permute-start(bf16[3,16,2304]{2,1,0:T(8,128)(2,1)} %get-tuple-element.46), channel_id=1, source_target_pairs={{0,1},{1,2},{2,3},{3,4},{4,5},{5,6},{6,7},{7,0},{8,9},{9,10},{10,1... | collective-permute-start | bytes 663560 | tf_op jit(solution)/shard_map/ppermute | solution.py:384
  15.1 8.5 %collective-permute-start.1 = (bf16[3,16,2304]{2,1,0:T(8,128)(2,1)}, bf16[3,16,2304]{2,1,0:T(8,128)(2,1)}, u32[]{:S(2)}, u32[]{:S(2)}) collective-permute-start(bf16[3,16,2304]{2,1,0:T(8,128)(2,1)} %get-tuple-element.47), channel_id=1, source_target_pairs={{0,7},{1,0},{2,1},{3,2},{4,3},{5,4},{6,5},{7,6},{8,15},{9,8},{10,9... | collective-permute-start | bytes 663560 | tf_op jit(solution)/shard_map/ppermute | solution.py:384
  20.6 0.7 copy-start.6
  29.1 1.0 copy-start.1
  34.5 4.9 %copy-start.11 = (bf16[3,16,2304]{2,1,0:T(8,128)(2,1)S(1)}, bf16[3,16,2304]{2,1,0:T(8,128)(2,1)}, u32[]{:S(2)}) copy-start(bf16[3,16,2304]{2,1,0:T(8,128)(2,1)} %get-tuple-element.50) | copy-start | bytes 663556
  34.5 9.2 %copy-start.10 = (bf16[3,16,2304]{2,1,0:T(8,128)(2,1)S(1)}, bf16[3,16,2304]{2,1,0:T(8,128)(2,1)}, u32[]{:S(2)}) copy-start(bf16[3,16,2304]{2,1,0:T(8,128)(2,1)} %get-tuple-element.51) | copy-start | bytes 663556
  34.5 9.1 %copy-start.9 = (bf16[3,16,2304]{2,1,0:T(8,128)(2,1)S(1)}, bf16[3,16,2304]{2,1,0:T(8,128)(2,1)}, u32[]{:S(2)}) copy-start(bf16[3,16,2304]{2,1,0:T(8,128)(2,1)} %get-tuple-element.52) | copy-start | bytes 663556
  34.5 13.2 %copy-start.8 = (bf16[3,16,2304]{2,1,0:T(8,128)(2,1)S(1)}, bf16[3,16,2304]{2,1,0:T(8,128)(2,1)}, u32[]{:S(2)}) copy-start(bf16[3,16,2304]{2,1,0:T(8,128)(2,1)} %get-tuple-element.53) | copy-start | bytes 663556
  34.5 13.7 %copy-start.7 = (bf16[3,16,2304]{2,1,0:T(8,128)(2,1)S(1)}, bf16[3,16,2304]{2,1,0:T(8,128)(2,1)}, u32[]{:S(2)}) copy-start(bf16[3,16,2304]{2,1,0:T(8,128)(2,1)} %get-tuple-element.54) | copy-start | bytes 663556
  34.5 44.8 %all-to-all-start.1 = ((bf16[32,24,16,128]{3,2,1,0:T(8,128)(2,1)}), bf16[32,24,16,128]{3,2,1,0:T(8,128)(2,1)}, u32[]{:S(2)}, u32[]{:S(2)}) async-start(bf16[32,24,16,128]{3,2,1,0:T(8,128)(2,1)} %get-tuple-element.49), calls=%async_computation.1 | async-start | bytes 6291456 | tf_op jit(solution)/shard_map/all_to_all | solution.py:380
  39.3 20.9 %collective-permute-start.2 = (bf16[3,16,2304]{2,1,0:T(8,128)(2,1)S(1)}, bf16[3,16,2304]{2,1,0:T(8,128)(2,1)S(1)}, u32[]{:S(2)}, u32[]{:S(2)}) collective-permute-start(bf16[3,16,2304]{2,1,0:T(8,128)(2,1)S(1)} %copy-done.11), channel_id=1, source_target_pairs={{0,2},{1,3},{2,4},{3,5},{4,6},{5,7},{6,0},{7,1},{8,10},{9,11},{10,... | collective-permute-start | bytes 663560 | tf_op jit(solution)/shard_map/ppermute | solution.py:384
  43.6 16.6 %collective-permute-start.3 = (bf16[3,16,2304]{2,1,0:T(8,128)(2,1)S(1)}, bf16[3,16,2304]{2,1,0:T(8,128)(2,1)S(1)}, u32[]{:S(2)}, u32[]{:S(2)}) collective-permute-start(bf16[3,16,2304]{2,1,0:T(8,128)(2,1)S(1)} %copy-done.10), channel_id=1, source_target_pairs={{0,6},{1,7},{2,0},{3,1},{4,2},{5,3},{6,4},{7,5},{8,14},{9,15},{10,... | collective-permute-start | bytes 663560 | tf_op jit(solution)/shard_map/ppermute | solution.py:384
  43.6 26.8 %collective-permute-start.4 = (bf16[3,16,2304]{2,1,0:T(8,128)(2,1)S(1)}, bf16[3,16,2304]{2,1,0:T(8,128)(2,1)S(1)}, u32[]{:S(2)}, u32[]{:S(2)}) collective-permute-start(bf16[3,16,2304]{2,1,0:T(8,128)(2,1)S(1)} %copy-done.9), channel_id=1, source_target_pairs={{0,3},{1,4},{2,5},{3,6},{4,7},{5,0},{6,1},{7,2},{8,11},{9,12},{10,... | collective-permute-start | bytes 663560 | tf_op jit(solution)/shard_map/ppermute | solution.py:384
  47.7 22.7 %collective-permute-start.5 = (bf16[3,16,2304]{2,1,0:T(8,128)(2,1)S(1)}, bf16[3,16,2304]{2,1,0:T(8,128)(2,1)S(1)}, u32[]{:S(2)}, u32[]{:S(2)}) collective-permute-start(bf16[3,16,2304]{2,1,0:T(8,128)(2,1)S(1)} %copy-done.8), channel_id=1, source_target_pairs={{0,5},{1,6},{2,7},{3,0},{4,1},{5,2},{6,3},{7,4},{8,13},{9,14},{10,... | collective-permute-start | bytes 663560 | tf_op jit(solution)/shard_map/ppermute | solution.py:384
  48.2 30.4 %collective-permute-start.6 = (bf16[3,16,2304]{2,1,0:T(8,128)(2,1)S(1)}, bf16[3,16,2304]{2,1,0:T(8,128)(2,1)}, u32[]{:S(2)}, u32[]{:S(2)}) collective-permute-start(bf16[3,16,2304]{2,1,0:T(8,128)(2,1)S(1)} %copy-done.7), channel_id=1, source_target_pairs={{0,4},{1,5},{2,6},{3,7},{4,0},{5,1},{6,2},{7,3},{8,12},{9,13},{10,... | collective-permute-start | bytes 663560 | tf_op jit(solution)/shard_map/ppermute | solution.py:384
  60.2 10.2 %copy-start.12 = (bf16[3,16,2304]{2,1,0:T(8,128)(2,1)}, bf16[3,16,2304]{2,1,0:T(8,128)(2,1)S(1)}, u32[]{:S(2)}) copy-start(bf16[3,16,2304]{2,1,0:T(8,128)(2,1)S(1)} %collective-permute-done.2.refs_2_) | copy-start | bytes 663556
  60.2 10.2 %copy-start.13 = (bf16[3,16,2304]{2,1,0:T(8,128)(2,1)}, bf16[3,16,2304]{2,1,0:T(8,128)(2,1)S(1)}, u32[]{:S(2)}) copy-start(bf16[3,16,2304]{2,1,0:T(8,128)(2,1)S(1)} %collective-permute-done.3.refs_6_) | copy-start | bytes 663556
  70.4 0.7 copy-start.14
  71.1 0.7 copy-start.15
  106.2 49.2 %all-to-all-start.2 = ((bf16[32,24,16,128]{3,2,1,0:T(8,128)(2,1)}), bf16[32,24,16,128]{3,2,1,0:T(8,128)(2,1)S(1)}, u32[]{:S(2)}, u32[]{:S(2)}) async-start(bf16[32,24,16,128]{3,2,1,0:T(8,128)(2,1)} %get-tuple-element.66), calls=%async_computation.2 | async-start | bytes 6291456 | tf_op jit(solution)/shard_map/all_to_all | solution.py:380
  113.6 12.5 %collective-permute-start.8 = (bf16[3,16,2304]{2,1,0:T(8,128)(2,1)}, bf16[3,16,2304]{2,1,0:T(8,128)(2,1)S(1)}, u32[]{:S(2)}, u32[]{:S(2)}) collective-permute-start(bf16[3,16,2304]{2,1,0:T(8,128)(2,1)} %get-tuple-element.67), channel_id=1, source_target_pairs={{0,6},{1,7},{2,0},{3,1},{4,2},{5,3},{6,4},{7,5},{8,14},{9,15},{10,... | collective-permute-start | bytes 663560 | tf_op jit(solution)/shard_map/ppermute | solution.py:384
  113.7 12.4 %collective-permute-start.9 = (bf16[3,16,2304]{2,1,0:T(8,128)(2,1)}, bf16[3,16,2304]{2,1,0:T(8,128)(2,1)S(1)}, u32[]{:S(2)}, u32[]{:S(2)}) collective-permute-start(bf16[3,16,2304]{2,1,0:T(8,128)(2,1)} %get-tuple-element.68), channel_id=1, source_target_pairs={{0,2},{1,3},{2,4},{3,5},{4,6},{5,7},{6,0},{7,1},{8,10},{9,11},{10,... | collective-permute-start | bytes 663560 | tf_op jit(solution)/shard_map/ppermute | solution.py:384
  117.3 24.8 %collective-permute-start.10 = (bf16[3,16,2304]{2,1,0:T(8,128)(2,1)}, bf16[3,16,2304]{2,1,0:T(8,128)(2,1)S(1)}, u32[]{:S(2)}, u32[]{:S(2)}) collective-permute-start(bf16[3,16,2304]{2,1,0:T(8,128)(2,1)} %get-tuple-element.69), channel_id=1, source_target_pairs={{0,5},{1,6},{2,7},{3,0},{4,1},{5,2},{6,3},{7,4},{8,13},{9,14},{10,... | collective-permute-start | bytes 663560 | tf_op jit(solution)/shard_map/ppermute | solution.py:384
  121.5 22.9 %collective-permute-start.11 = (bf16[3,16,2304]{2,1,0:T(8,128)(2,1)}, bf16[3,16,2304]{2,1,0:T(8,128)(2,1)S(1)}, u32[]{:S(2)}, u32[]{:S(2)}) collective-permute-start(bf16[3,16,2304]{2,1,0:T(8,128)(2,1)} %get-tuple-element.70), channel_id=1, source_target_pairs={{0,3},{1,4},{2,5},{3,6},{4,7},{5,0},{6,1},{7,2},{8,11},{9,12},{10,... | collective-permute-start | bytes 663560 | tf_op jit(solution)/shard_map/ppermute | solution.py:384
  121.7 33.7 %collective-permute-start.12 = (bf16[3,16,2304]{2,1,0:T(8,128)(2,1)}, bf16[3,16,2304]{2,1,0:T(8,128)(2,1)}, u32[]{:S(2)}, u32[]{:S(2)}) collective-permute-start(bf16[3,16,2304]{2,1,0:T(8,128)(2,1)} %get-tuple-element.71), channel_id=1, source_target_pairs={{0,4},{1,5},{2,6},{3,7},{4,0},{5,1},{6,2},{7,3},{8,12},{9,13},{10,... | collective-permute-start | bytes 663560 | tf_op jit(solution)/shard_map/ppermute | solution.py:384
  126.1 50.5 %copy-start.2 = (bf16[3,16,2304]{2,1,0:T(8,128)(2,1)}, bf16[3,16,2304]{2,1,0:T(8,128)(2,1)S(1)}, u32[]{:S(2)}) copy-start(bf16[3,16,2304]{2,1,0:T(8,128)(2,1)S(1)} %collective-permute-done.8.refs_2_) | copy-start | bytes 663556
  126.1 18.3 %copy-start.3 = (bf16[3,16,2304]{2,1,0:T(8,128)(2,1)}, bf16[3,16,2304]{2,1,0:T(8,128)(2,1)S(1)}, u32[]{:S(2)}) copy-start(bf16[3,16,2304]{2,1,0:T(8,128)(2,1)S(1)} %collective-permute-done.9.refs_6_) | copy-start | bytes 663556
  142.1 2.3 %copy-start.4 = (bf16[3,16,2304]{2,1,0:T(8,128)(2,1)}, bf16[3,16,2304]{2,1,0:T(8,128)(2,1)S(1)}, u32[]{:S(2)}) copy-start(bf16[3,16,2304]{2,1,0:T(8,128)(2,1)S(1)} %collective-permute-done.10.refs_3_) | copy-start | bytes 663556
  144.4 0.7 copy-start.5
  155.4 1.6 copy-start
  161.0 25.3 %all-to-all-start.3 = ((bf16[32,8,16,128]{3,2,1,0:T(8,128)(2,1)}), bf16[32,8,16,128]{3,2,1,0:T(8,128)(2,1)S(1)}, u32[]{:S(2)}, u32[]{:S(2)}) async-start(bf16[32,8,16,128]{3,2,1,0:T(8,128)(2,1)} %shard_map.132), calls=%async_computation.3 | async-start | bytes 2097152 | tf_op jit(solution)/shard_map/all_to_all | solution.py:380
  169.3 7.2 %collective-permute-start.7 = (bf16[3,16,2304]{2,1,0:T(8,128)(2,1)}, bf16[3,16,2304]{2,1,0:T(8,128)(2,1)}, u32[]{:S(2)}, u32[]{:S(2)}) collective-permute-start(bf16[3,16,2304]{2,1,0:T(8,128)(2,1)} %get-tuple-element.65), channel_id=1, source_target_pairs={{0,7},{1,0},{2,1},{3,2},{4,3},{5,4},{6,5},{7,6},{8,15},{9,8},{10,9... | collective-permute-start | bytes 663560 | tf_op jit(solution)/shard_map/ppermute | solution.py:384
  169.4 7.2 %collective-permute-start.13 = (bf16[3,16,2304]{2,1,0:T(8,128)(2,1)}, bf16[3,16,2304]{2,1,0:T(8,128)(2,1)}, u32[]{:S(2)}, u32[]{:S(2)}) collective-permute-start(bf16[3,16,2304]{2,1,0:T(8,128)(2,1)} %get-tuple-element.77), channel_id=1, source_target_pairs={{0,1},{1,2},{2,3},{3,4},{4,5},{5,6},{6,7},{7,0},{8,9},{9,10},{10,1... | collective-permute-start | bytes 663560 | tf_op jit(solution)/shard_map/ppermute | solution.py:384
